TPU v7x, 128 devices: a whole 4x4x4 slice. The times are simulated.
128 devices in a mesh: cells: 128 (over z, y, x, core).
Axes of the slice: x: 4, y: 4, z: 4, core: 2. Of those that a mesh axis runs over, the one named last changes fastest.
Arguments:
- positions: float32 [3, 1048576], P(None, 'cells'), may hold values from 0 to 1
- velocities: float32 [3, 1048576], P(None, 'cells'), may hold values from -6 to 6
- masses: float32 [1048576], P('cells'), may hold values from 0.5 to 2
- smoothing: float32 [1048576], P('cells'), may hold values from 0.5 to 1
- energies: float32 [1048576], P('cells'), may hold values from 0.5 to 2
- cell_counts: int32 [4096], P('cells'), may hold values from 128 to 256, as said below
- pair_list: int32 [4, 16384], P(None, 'cells'), may hold values from 0 to 31, as said below
- export_list: int32 [128, 26, 8], P('cells'), may hold values from -1 to 31, as said below
- mesh_owner: int32 [1048576, 1], P('cells'), may hold values from 0 to 127; in each aligned block of 8192 rows (0 to 8191, 8192 to 16383, ...) at most 128 rows name the same one
- mesh_cell: int32 [1048576], P('cells'), may hold values from 0 to 131071
Outputs:
- density: float32 [1048576], P('cells')
- acceleration: float32 [3, 1048576], P(None, 'cells')
- heating: float32 [1048576], P('cells')
- potential: float32 [256, 256, 256], P('cells')
Inputs may be any that keep to these rules, and one draw needn't show every extreme that they name: `cell_counts`: slots at and beyond a cell's count are padding; every device has at least one cell with all 256 slots live. `pair_list`: row 0 is the owner cell's index on the listing device, row 1 a neighbour index of 0 to 25, row 2 a slot of 0 to 7, row 3 a neighbour direction of 0 to 26 other than 13. Every device lists exactly 128 cross pairs, each (neighbour index, slot) at most once, at most 8 with one neighbour index and exactly 8 with one of them. `export_list`: entry [f, j, t] is the cell of device f that the device whose pair with neighbour index j and slot t names device f reads, or -1 where no pair names that slot. `mesh_owner`: at most 128 particles of one device have their mesh cell in one device's planes.
All inputs are finite; a program needn't handle non-finite values.
Results may differ from a plain program's by a relative error of at most 0.0003.
Values sent between devices are 32-bit elements; how exact they have to be, the bound alone decides.
No kernel may reach another device: no remote copies, remote signals or barrier semaphores. Data moves between devices by JAX's collectives and lax.ppermute only.
A program may use at most 64 MiB of HBM per device.

v0:
```python
import math

import jax
import jax.numpy as jnp
from jax import lax
from jax.sharding import PartitionSpec as P

M = 256


spline_norm = 8.0 / math.pi
pair_block = 16
highest = lax.Precision.HIGHEST


def shifted(value, axis, steps):
    count = lax.axis_size(axis)
    pairs = [(source, (source + steps) % count) for source in range(count)]
    return lax.ppermute(value, axis, pairs)


def spline_value(scaled_dist):
    inner_part = (
        1.0 - 6.0 * scaled_dist * scaled_dist + 6.0 * scaled_dist * scaled_dist * scaled_dist
    )
    outer_part = 2.0 * (1.0 - scaled_dist) ** 3
    return jnp.where(scaled_dist <= 0.5, inner_part, jnp.where(scaled_dist <= 1.0, outer_part, 0.0))


def spline_slope(scaled_dist):
    inner_part = -12.0 + 18.0 * scaled_dist
    outer_part = -6.0 * (1.0 - scaled_dist) ** 2 / jnp.maximum(scaled_dist, 0.5)
    return jnp.where(scaled_dist <= 0.5, inner_part, jnp.where(scaled_dist <= 1.0, outer_part, 0.0))


def offsets(direction):
    return jnp.stack(
        [direction // 9 - 1, direction // 3 % 3 - 1, direction % 3 - 1], axis=1
    ).astype(jnp.float32)


def density_terms(own_pos, own_reach, far_pos, far_weight):
    separation = own_pos[:, :, :, None] - far_pos[:, :, None, :]
    distance = jnp.sqrt(jnp.sum(separation * separation, axis=1))
    scaled_dist = distance / own_reach[:, :, None]
    scale_own = spline_norm / own_reach**3
    return scale_own * jnp.sum(spline_value(scaled_dist) * far_weight[:, None, :], axis=2)


def force_terms(
    own_pos, own_vel, own_reach, own_factor, far_pos, far_vel, far_reach, far_factor, far_weight
):
    separation = own_pos[:, :, :, None] - far_pos[:, :, None, :]
    distance = jnp.sqrt(jnp.sum(separation * separation, axis=1))
    own_slope = (
        spline_norm * spline_slope(distance / own_reach[:, :, None]) / own_reach[:, :, None] ** 5
    )
    far_slope = (
        spline_norm * spline_slope(distance / far_reach[:, None, :]) / far_reach[:, None, :] ** 5
    )
    coefficient = far_weight[:, None, :] * (
        own_factor[:, :, None] * own_slope + far_factor[:, None, :] * far_slope
    )
    push = -jnp.sum(coefficient[:, None] * separation, axis=3)
    relative = own_vel[:, :, :, None] - far_vel[:, :, None, :]
    closing = jnp.sum(relative * separation, axis=1)
    warming = own_factor * jnp.sum(far_weight[:, None, :] * own_slope * closing, axis=2)
    return jnp.concatenate([push, warming[:, None, :]], axis=1)


def blockwise(kernel_fn, arrays):
    amount = arrays[0].shape[0]
    block_size = math.gcd(pair_block, amount)
    shaped = tuple(
        (item.reshape((amount // block_size, block_size) + item.shape[1:]) for item in arrays)
    )
    results = lax.map(lambda block_args: kernel_fn(*block_args), shaped)
    return results.reshape((amount,) + results.shape[2:])


def along_middle(field, table):
    return jnp.einsum("ayz,yk->akz", field, table, precision=highest)


def along_first(field, table):
    return jnp.einsum("xyz,xk->kyz", field, table, precision=highest)


def per_device(
    positions,
    velocities,
    masses,
    smoothing,
    energies,
    cell_counts,
    pair_list,
    export_list,
    mesh_owner,
    mesh_cell,
):
    ncells = cell_counts.shape[0]
    per_cell = positions.shape[1] // ncells
    devices = lax.axis_size("cells")
    slots_iota = jnp.arange(per_cell, dtype=jnp.int32)
    live_mask = (slots_iota[None, :] < cell_counts[:, None]).astype(jnp.float32)
    own_pos = jnp.moveaxis(positions.reshape(3, ncells, per_cell), 1, 0)
    own_vel = jnp.moveaxis(velocities.reshape(3, ncells, per_cell), 1, 0)
    weight = masses.reshape(ncells, per_cell) * live_mask / per_cell
    own_reach = smoothing.reshape(ncells, per_cell)
    own_heat = energies.reshape(ncells, per_cell)
    exports = export_list[0]
    neighbours = exports.shape[0]
    half_peers = neighbours // 2
    wanted = jnp.maximum(exports, 0)
    present = (exports >= 0).astype(jnp.float32)

    def outbound(cell_data):
        picked = jnp.take(cell_data, wanted, axis=0)
        return picked * present.reshape(present.shape + (1,) * (picked.ndim - 2))

    def from_neighbours(cell_data, sender):
        leaving = outbound(cell_data)
        pieces = []
        for neighbour in range(neighbours):
            step_along = (
                neighbour - half_peers if neighbour < half_peers else neighbour - half_peers + 1
            )
            pieces.append(sender(leaving[neighbour], -step_along))
        return jnp.stack(pieces)

    owner_cell = pair_list[0]
    source = pair_list[1]
    slot_index = pair_list[2]
    shifts = offsets(pair_list[3])
    owner_onehot = (jnp.arange(ncells, dtype=jnp.int32)[:, None] == owner_cell[None, :]).astype(
        jnp.float32
    )

    def collect(term_rows):
        flat_rows = term_rows.reshape(term_rows.shape[0], -1)
        summed = jnp.dot(
            owner_onehot, flat_rows, precision=highest, preferred_element_type=jnp.float32
        )
        return summed.reshape((ncells,) + term_rows.shape[1:])

    def arriving(received):
        return received[source, slot_index]

    def send_first(piece, by):
        return shifted(piece, "cells", by)

    def send_second(piece, by):
        return shifted(piece, "cells", by)

    first_send = jnp.concatenate([own_pos, weight[:, None]], axis=1)
    far_first = arriving(from_neighbours(first_send, send_first))
    far_pos = far_first[:, 0:3] + shifts[:, :, None]
    far_weight = far_first[:, 3]
    self_density = blockwise(density_terms, (own_pos, own_reach, own_pos, weight))
    cross_density = blockwise(
        density_terms, (own_pos[owner_cell], own_reach[owner_cell], far_pos, far_weight)
    )
    raw_density = self_density + collect(cross_density)
    density = jnp.where(live_mask > 0, raw_density, 1.0)
    factor = 2.0 / 3.0 * own_heat / density
    second_send = jnp.concatenate(
        [
            own_pos,
            own_vel,
            weight[:, None],
            own_reach[:, None],
            density[:, None],
            own_heat[:, None],
        ],
        axis=1,
    )
    far_second = arriving(from_neighbours(second_send, send_second))
    far_pos = far_second[:, 0:3] + shifts[:, :, None]
    far_vel = far_second[:, 3:6]
    far_weight = far_second[:, 6]
    far_reach = far_second[:, 7]
    far_density = far_second[:, 8]
    far_heat = far_second[:, 9]
    far_factor = 2.0 / 3.0 * far_heat / far_density
    self_force = blockwise(
        force_terms,
        (own_pos, own_vel, own_reach, factor, own_pos, own_vel, own_reach, factor, weight),
    )
    cross_force = blockwise(
        force_terms,
        (
            own_pos[owner_cell],
            own_vel[owner_cell],
            own_reach[owner_cell],
            factor[owner_cell],
            far_pos,
            far_vel,
            far_reach,
            far_factor,
            far_weight,
        ),
    )
    summed_force = (self_force + collect(cross_force)) * live_mask[:, None, :]
    acceleration = jnp.moveaxis(summed_force[:, 0:3], 0, 1).reshape(3, -1)
    heating = summed_force[:, 3].reshape(-1)
    slab_depth = M // devices
    slab_cells = slab_depth * M * M
    capacity = 2 * ncells * per_cell // devices
    target = mesh_owner[:, 0]
    chosen = (target[:, None] == jnp.arange(devices, dtype=jnp.int32)[None, :]).astype(jnp.int32)
    slot_rank = jnp.sum((jnp.cumsum(chosen, axis=0) - 1) * chosen, axis=1)
    deposit = masses * live_mask.reshape(-1)
    outgoing = jnp.zeros((2, devices, capacity), jnp.float32)
    outgoing = outgoing.at[0, target, slot_rank].set(deposit)
    outgoing = outgoing.at[1, target, slot_rank].set(mesh_cell.astype(jnp.float32))
    incoming = lax.all_to_all(outgoing, "cells", split_axis=1, concat_axis=1, tiled=True)
    mass_grid = jax.ops.segment_sum(
        incoming[0].reshape(-1), incoming[1].reshape(-1).astype(jnp.int32), num_segments=slab_cells
    )
    mass_grid = mass_grid.reshape(slab_depth, M, M)
    wave_index = jnp.arange(M, dtype=jnp.int32)
    phase_index = wave_index[:, None] * wave_index[None, :] % M
    angle_table = 2.0 * math.pi / M * phase_index.astype(jnp.float32)
    cosine = jnp.cos(angle_table)
    sine_table = jnp.sin(angle_table)
    signed = jnp.where(wave_index < M // 2, wave_index, wave_index - M).astype(jnp.float32)
    local_rows = lax.axis_index("cells") * slab_depth + jnp.arange(slab_depth, dtype=jnp.int32)
    signed_rows = jnp.where(local_rows < M // 2, local_rows, local_rows - M).astype(jnp.float32)
    wave_step = 2.0 * math.pi / M
    real_part = jnp.matmul(mass_grid, cosine, precision=highest)
    imag_part = -jnp.matmul(mass_grid, sine_table, precision=highest)
    real_next = along_middle(real_part, cosine) + along_middle(imag_part, sine_table)
    imag_next = along_middle(imag_part, cosine) - along_middle(real_part, sine_table)
    turned = lax.all_to_all(
        jnp.stack([real_next, imag_next]), "cells", split_axis=2, concat_axis=1, tiled=True
    )
    real_part = turned[0]
    imag_part = turned[1]
    real_part, imag_part = (
        along_first(real_part, cosine) + along_first(imag_part, sine_table),
        along_first(imag_part, cosine) - along_first(real_part, sine_table),
    )
    wave_square = (
        wave_step
        * wave_step
        * (
            signed[:, None, None] ** 2
            + signed_rows[None, :, None] ** 2
            + signed[None, None, :] ** 2
        )
    )
    green_factor = jnp.where(
        wave_square > 0, -1.0 / jnp.where(wave_square > 0, wave_square, 1.0), 0.0
    )
    inverse_real_part = real_part * green_factor
    inverse_imag_part = imag_part * green_factor
    real_next = along_first(inverse_real_part, cosine) - along_first(inverse_imag_part, sine_table)
    imag_next = along_first(inverse_imag_part, cosine) + along_first(inverse_real_part, sine_table)
    returned = lax.all_to_all(
        jnp.stack([real_next, imag_next]), "cells", split_axis=1, concat_axis=2, tiled=True
    )
    real_part = returned[0]
    imag_part = returned[1]
    real_part, imag_part = (
        along_middle(real_part, cosine) - along_middle(imag_part, sine_table),
        along_middle(imag_part, cosine) + along_middle(real_part, sine_table),
    )
    potential = (
        jnp.matmul(real_part, cosine, precision=highest)
        - jnp.matmul(imag_part, sine_table, precision=highest)
    ) / float(M) ** 3
    return (density.reshape(-1), acceleration, heating, potential)


def solution(mesh):
    in_specs = (
        P(None, "cells"),
        P(None, "cells"),
        P("cells"),
        P("cells"),
        P("cells"),
        P("cells"),
        P(None, "cells"),
        P("cells", None, None),
        P("cells", None),
        P("cells"),
    )
    out_specs = (P("cells"), P(None, "cells"), P("cells"), P("cells", None, None))
    return jax.shard_map(
        per_device, mesh=mesh, in_specs=in_specs, out_specs=out_specs, check_vma=False
    )
```

profile of v0, /device:TPU:1, one launch (start us, length us, event | category | flops | bytes accessed | tf_op | source)
XLA Modules:
  0.0 714.3 jit_solution(13162851586471419803)
XLA Ops:
  33.2 30.5 %scatter_custom_fusion.1 = f32[32768]{0:T(1024)S(1)} fusion(s32[8192]{0:T(1024)S(1)} %get-tuple-element.467, f32[8192]{0:T(1024)S(1)} %broadcast_select_fusion.2, f32[]{:T(128)} %constant.242.clone.1), kind=kCustom, calls=%fused_computation.276 | custom fusion | bytes 131076
  63.7 30.5 %scatter_fusion = f32[32768]{0:T(1024)S(1)} fusion(f32[32768]{0:T(1024)S(1)} %scatter_custom_fusion.1, s32[8192]{0:T(1024)S(1)} %get-tuple-element.466, f32[8192]{0:T(1024)S(1)} %convert_element_type.114), kind=kCustom, calls=%fused_computation.10 | custom fusion | bytes 131072
  95.0 9.3 %all-to-all-start = ((f32[2,128,128]{2,0,1:T(2,128)}), f32[2,128,128]{2,0,1:T(2,128)S(1)}, u32[]{:S(2)}, u32[]{:S(2)}) async-start(f32[2,128,128]{2,0,1:T(2,128)} %copy.165), calls=%async_computation | async-start | bytes 262144 | tf_op jit(solution)/shard_map/all_to_all | solution.py:216
  106.1 11.5 %while.46 = (s32[]{:T(128)}, f32[2,16,256]{2,1,0:T(8,128)S(1)}, f32[2,16,256]{2,1,0:T(8,128)S(1)}, f32[2,16,3,256]{3,2,1,0:T(4,128)S(1)}, f32[2,16,256]{2,1,0:T(8,128)S(1)}) while((s32[]{:T(128)}, f32[2,16,256]{2,1,0:T(8,128)S(1)}, f32[2,16,256]{2,1,0:T(8,128)S(1)}, f32[2,16,3,256]{3,2,1,0:T(4,128)S(1)}, ...), condition=%wide.region_3.4_spmd.clone, body=%wide.region_0.3_spmd.sunk.clone | while | flops 25178112 | bytes 8699985 | solution.py:77
  164.5 9.8 %collective-permute-start.25 = (f32[8,4,256]{2,1,0:T(4,128)S(1)}, f32[8,4,256]{2,1,0:T(4,128)S(1)}, u32[]{:S(2)}, u32[]{:S(2)}) collective-permute-start(f32[8,4,256]{2,1,0:T(4,128)S(1)} %get-tuple-element.425), channel_id=1, source_target_pairs={{0,115},{1,116},{2,117},{3,118},{4,119},{5,120},{6,121},{7,122},{8... | collective-permute-start | bytes 98312 | tf_op jit(solution)/shard_map/ppermute | solution.py:19
  180.3 46.2 %while.47 = (s32[]{:T(128)}, f32[8,16,256]{2,1,0:T(8,128)S(1)}, f32[8,16,256]{2,1,0:T(8,128)S(1)}, f32[8,16,3,256]{3,2,1,0:T(4,128)S(1)}, f32[8,16,3,256]{3,2,1,0:T(4,128)S(1)}, /*index=5*/f32[8,16,256]{2,1,0:T(8,128)S(1)}) while((s32[]{:T(128)}, f32[8,16,256]{2,1,0:T(8,128)S(1)}, f32[8,16,256]{2,1,0:T(8,128)S(1)}, ...), condition=%wide.region_7.8_spmd.clone, body=%wide.region_4.7_spmd.sunk.clone | while | flops 25178112 | bytes 8847449 | solution.py:77
  227.3 38.0 %while.48 = (s32[]{:T(128)}, f32[2,16,4,256]{3,1,0,2:T(8,128)S(1)}, f32[2,16,256]{2,1,0:T(8,128)S(1)}, f32[2,16,256]{2,1,0:T(8,128)S(1)}, f32[2,16,3,256]{3,2,1,...) while((s32[]{:T(128)}, f32[2,16,4,256]{3,1,0,2:T(8,128)S(1)}, ...), condition=%wide.region_13.14_spmd.clone, body=%wide.region_8.13_spmd.sunk.clone | while | flops 77623296 | bytes 30441580 | solution.py:77
  229.6 6.1 add_multiply_fusion.6
  235.7 6.1 fusion.273
  248.6 6.1 add_multiply_fusion.6
  254.7 6.1 fusion.273
  311.3 6.8 collective-permute-start.40
  353.5 95.4 %scatter_custom_fusion = f32[131072]{0:T(1024)S(1)} fusion(s32[16384]{0:T(1024)S(1)} %bitcast.589, f32[16384]{0:T(1024)S(1)} %bitcast.588, f32[]{:T(128)} %constant.242.clone.1), kind=kCustom, calls=%fused_computation.175 | custom fusion | flops 16384 | bytes 524292 | tf_op jit(solution)/shard_map/scatter-add | solution.py:217
  460.3 22.8 %all-to-all-start.1 = ((f32[2,2,256,256]{3,1,0,2:T(2,128)}), f32[2,2,256,256]{3,1,0,2:T(2,128)S(1)}, u32[]{:S(2)}, u32[]{:S(2)}) async-start(f32[2,2,256,256]{3,1,0,2:T(2,128)} %copy.170), calls=%async_computation.1 | async-start | bytes 2097152 | tf_op jit(solution)/shard_map/all_to_all | solution.py:234
  490.9 11.4 %all-to-all-done.1 = f32[2,2,256,256]{3,1,0,2:T(2,128)S(1)} async-done(((f32[2,2,256,256]{3,1,0,2:T(2,128)}), f32[2,2,256,256]{3,1,0,2:T(2,128)S(1)}, u32[]{:S(2)}, u32[]{:S(2)}) %all-to-all-start.1) | async-done | bytes 1048608 | tf_op jit(solution)/shard_map/all_to_all | solution.py:234
  523.2 177.5 %while.49 = (s32[]{:T(128)}, f32[8,16,4,256]{3,2,1,0:T(4,128)S(1)}, f32[8,16,256]{2,1,0:T(8,128)}, f32[8,16,256]{2,1,0:T(8,128)S(1)}, f32[8,16,3,256]{3,2,1,0:T(...) while((s32[]{:T(128)}, f32[8,16,4,256]{3,2,1,0:T(4,128)S(1)}, ...), condition=%wide.region_19.20_spmd.clone, body=%wide.region_14.19_spmd.sunk.clone | while | flops 77635584 | bytes 30802064 | solution.py:77
  527.8 6.0 add_multiply_fusion.7
  534.8 6.1 fusion.277
  550.0 6.0 add_multiply_fusion.7
  556.9 6.1 fusion.277
  572.1 6.0 add_multiply_fusion.7
  579.1 6.1 fusion.277
  594.3 6.0 add_multiply_fusion.7
  601.2 6.1 fusion.277
  616.4 6.0 add_multiply_fusion.7
  623.4 6.1 fusion.277
  638.6 6.0 add_multiply_fusion.7
  645.5 6.1 fusion.277
  660.7 6.0 add_multiply_fusion.7
  667.7 6.1 fusion.277
  682.9 6.0 add_multiply_fusion.7
  689.8 6.1 fusion.277
  (487 shorter events, 372.7 us)
Async XLA Ops:
  7.0 114.8 %collective-permute-start = (f32[8,4,256]{2,1,0:T(4,128)S(1)}, f32[8,4,256]{2,1,0:T(4,128)S(1)}, u32[]{:S(2)}, u32[]{:S(2)}) collective-permute-start(f32[8,4,256]{2,1,0:T(4,128)S(1)} %get-tuple-element.450), channel_id=1, source_target_pairs={{0,13},{1,14},{2,15},{3,16},{4,17},{5,18},{6,19},{7,20},{8,21},{9,... | collective-permute-start | bytes 98312 | tf_op jit(solution)/shard_map/ppermute | solution.py:19
  11.9 112.6 %collective-permute-start.1 = (f32[8,4,256]{2,1,0:T(4,128)S(1)}, f32[8,4,256]{2,1,0:T(4,128)}, u32[]{:S(2)}, u32[]{:S(2)}) collective-permute-start(f32[8,4,256]{2,1,0:T(4,128)S(1)} %get-tuple-element.449), channel_id=1, source_target_pairs={{0,12},{1,13},{2,14},{3,15},{4,16},{5,17},{6,18},{7,19},{8,20},{9,... | collective-permute-start | bytes 98312 | tf_op jit(solution)/shard_map/ppermute | solution.py:19
  14.2 112.8 %collective-permute-start.2 = (f32[8,4,256]{2,1,0:T(4,128)S(1)}, f32[8,4,256]{2,1,0:T(4,128)}, u32[]{:S(2)}, u32[]{:S(2)}) collective-permute-start(f32[8,4,256]{2,1,0:T(4,128)S(1)} %get-tuple-element.448), channel_id=1, source_target_pairs={{0,11},{1,12},{2,13},{3,14},{4,15},{5,16},{6,17},{7,18},{8,19},{9,... | collective-permute-start | bytes 98312 | tf_op jit(solution)/shard_map/ppermute | solution.py:19
  17.9 112.3 %collective-permute-start.3 = (f32[8,4,256]{2,1,0:T(4,128)S(1)}, f32[8,4,256]{2,1,0:T(4,128)}, u32[]{:S(2)}, u32[]{:S(2)}) collective-permute-start(f32[8,4,256]{2,1,0:T(4,128)S(1)} %get-tuple-element.447), channel_id=1, source_target_pairs={{0,10},{1,11},{2,12},{3,13},{4,14},{5,15},{6,16},{7,17},{8,18},{9,... | collective-permute-start | bytes 98312 | tf_op jit(solution)/shard_map/ppermute | solution.py:19
  18.6 113.7 %collective-permute-start.4 = (f32[8,4,256]{2,1,0:T(4,128)S(1)}, f32[8,4,256]{2,1,0:T(4,128)}, u32[]{:S(2)}, u32[]{:S(2)}) collective-permute-start(f32[8,4,256]{2,1,0:T(4,128)S(1)} %get-tuple-element.446), channel_id=1, source_target_pairs={{0,9},{1,10},{2,11},{3,12},{4,13},{5,14},{6,15},{7,16},{8,17},{9,1... | collective-permute-start | bytes 98312 | tf_op jit(solution)/shard_map/ppermute | solution.py:19
  95.0 258.3 %all-to-all-start = ((f32[2,128,128]{2,0,1:T(2,128)}), f32[2,128,128]{2,0,1:T(2,128)S(1)}, u32[]{:S(2)}, u32[]{:S(2)}) async-start(f32[2,128,128]{2,0,1:T(2,128)} %copy.165), calls=%async_computation | async-start | bytes 262144 | tf_op jit(solution)/shard_map/all_to_all | solution.py:216
  122.3 13.3 %collective-permute-start.5 = (f32[8,4,256]{2,1,0:T(4,128)S(1)}, f32[8,4,256]{2,1,0:T(4,128)S(1)}, u32[]{:S(2)}, u32[]{:S(2)}) collective-permute-start(f32[8,4,256]{2,1,0:T(4,128)S(1)} %get-tuple-element.445), channel_id=1, source_target_pairs={{0,8},{1,9},{2,10},{3,11},{4,12},{5,13},{6,14},{7,15},{8,16},{9,17... | collective-permute-start | bytes 98312 | tf_op jit(solution)/shard_map/ppermute | solution.py:19
  155.9 18.4 %collective-permute-start.21 = (f32[8,4,256]{2,1,0:T(4,128)S(1)}, f32[8,4,256]{2,1,0:T(4,128)S(1)}, u32[]{:S(2)}, u32[]{:S(2)}) collective-permute-start(f32[8,4,256]{2,1,0:T(4,128)S(1)} %get-tuple-element.429), channel_id=1, source_target_pairs={{0,119},{1,120},{2,121},{3,122},{4,123},{5,124},{6,125},{7,126},{8... | collective-permute-start | bytes 98312 | tf_op jit(solution)/shard_map/ppermute | solution.py:19
  156.3 18.0 %collective-permute-start.22 = (f32[8,4,256]{2,1,0:T(4,128)S(1)}, f32[8,4,256]{2,1,0:T(4,128)S(1)}, u32[]{:S(2)}, u32[]{:S(2)}) collective-permute-start(f32[8,4,256]{2,1,0:T(4,128)S(1)} %get-tuple-element.428), channel_id=1, source_target_pairs={{0,118},{1,119},{2,120},{3,121},{4,122},{5,123},{6,124},{7,125},{8... | collective-permute-start | bytes 98312 | tf_op jit(solution)/shard_map/ppermute | solution.py:19
  158.7 15.7 %collective-permute-start.23 = (f32[8,4,256]{2,1,0:T(4,128)S(1)}, f32[8,4,256]{2,1,0:T(4,128)S(1)}, u32[]{:S(2)}, u32[]{:S(2)}) collective-permute-start(f32[8,4,256]{2,1,0:T(4,128)S(1)} %get-tuple-element.427), channel_id=1, source_target_pairs={{0,117},{1,118},{2,119},{3,120},{4,121},{5,122},{6,123},{7,124},{8... | collective-permute-start | bytes 98312 | tf_op jit(solution)/shard_map/ppermute | solution.py:19
  164.5 14.3 %collective-permute-start.25 = (f32[8,4,256]{2,1,0:T(4,128)S(1)}, f32[8,4,256]{2,1,0:T(4,128)S(1)}, u32[]{:S(2)}, u32[]{:S(2)}) collective-permute-start(f32[8,4,256]{2,1,0:T(4,128)S(1)} %get-tuple-element.425), channel_id=1, source_target_pairs={{0,115},{1,116},{2,117},{3,118},{4,119},{5,120},{6,121},{7,122},{8... | collective-permute-start | bytes 98312 | tf_op jit(solution)/shard_map/ppermute | solution.py:19
  270.7 14.1 %collective-permute-start.26 = (f32[8,10,256]{2,1,0:T(8,128)S(1)}, f32[8,10,256]{2,1,0:T(8,128)}, u32[]{:S(2)}, u32[]{:S(2)}) collective-permute-start(f32[8,10,256]{2,1,0:T(8,128)S(1)} %get-tuple-element.415), channel_id=1, source_target_pairs={{0,13},{1,14},{2,15},{3,16},{4,17},{5,18},{6,19},{7,20},{8,21},{9,... | collective-permute-start | bytes 245768 | tf_op jit(solution)/shard_map/ppermute | solution.py:19
  282.4 17.1 %collective-permute-start.30 = (f32[8,10,256]{2,1,0:T(8,128)S(1)}, f32[8,10,256]{2,1,0:T(8,128)S(1)}, u32[]{:S(2)}, u32[]{:S(2)}) collective-permute-start(f32[8,10,256]{2,1,0:T(8,128)S(1)} %get-tuple-element.411), channel_id=1, source_target_pairs={{0,9},{1,10},{2,11},{3,12},{4,13},{5,14},{6,15},{7,16},{8,17},{9,1... | collective-permute-start | bytes 245768 | tf_op jit(solution)/shard_map/ppermute | solution.py:19
  284.9 20.0 %collective-permute-start.31 = (f32[8,10,256]{2,1,0:T(8,128)S(1)}, f32[8,10,256]{2,1,0:T(8,128)S(1)}, u32[]{:S(2)}, u32[]{:S(2)}) collective-permute-start(f32[8,10,256]{2,1,0:T(8,128)S(1)} %get-tuple-element.410), channel_id=1, source_target_pairs={{0,8},{1,9},{2,10},{3,11},{4,12},{5,13},{6,14},{7,15},{8,16},{9,17... | collective-permute-start | bytes 245768 | tf_op jit(solution)/shard_map/ppermute | solution.py:19
  286.5 20.8 %collective-permute-start.32 = (f32[8,10,256]{2,1,0:T(8,128)S(1)}, f32[8,10,256]{2,1,0:T(8,128)S(1)}, u32[]{:S(2)}, u32[]{:S(2)}) collective-permute-start(f32[8,10,256]{2,1,0:T(8,128)S(1)} %get-tuple-element.409), channel_id=1, source_target_pairs={{0,7},{1,8},{2,9},{3,10},{4,11},{5,12},{6,13},{7,14},{8,15},{9,16}... | collective-permute-start | bytes 245768 | tf_op jit(solution)/shard_map/ppermute | solution.py:19
  288.0 20.0 %collective-permute-start.33 = (f32[8,10,256]{2,1,0:T(8,128)}, f32[8,10,256]{2,1,0:T(8,128)S(1)}, u32[]{:S(2)}, u32[]{:S(2)}) collective-permute-start(f32[8,10,256]{2,1,0:T(8,128)} %get-tuple-element.408), channel_id=1, source_target_pairs={{0,6},{1,7},{2,8},{3,9},{4,10},{5,11},{6,12},{7,13},{8,14},{9,15},... | collective-permute-start | bytes 245768 | tf_op jit(solution)/shard_map/ppermute | solution.py:19
  293.3 17.0 %collective-permute-start.34 = (f32[8,10,256]{2,1,0:T(8,128)}, f32[8,10,256]{2,1,0:T(8,128)S(1)}, u32[]{:S(2)}, u32[]{:S(2)}) collective-permute-start(f32[8,10,256]{2,1,0:T(8,128)} %get-tuple-element.407), channel_id=1, source_target_pairs={{0,5},{1,6},{2,7},{3,8},{4,9},{5,10},{6,11},{7,12},{8,13},{9,14},{... | collective-permute-start | bytes 245768 | tf_op jit(solution)/shard_map/ppermute | solution.py:19
  304.8 13.9 %collective-permute-start.36 = (f32[8,10,256]{2,1,0:T(8,128)}, f32[8,10,256]{2,1,0:T(8,128)S(1)}, u32[]{:S(2)}, u32[]{:S(2)}) collective-permute-start(f32[8,10,256]{2,1,0:T(8,128)} %get-tuple-element.405), channel_id=1, source_target_pairs={{0,3},{1,4},{2,5},{3,6},{4,7},{5,8},{6,9},{7,10},{8,11},{9,12},{10... | collective-permute-start | bytes 245768 | tf_op jit(solution)/shard_map/ppermute | solution.py:19
  307.3 13.7 %collective-permute-start.37 = (f32[8,10,256]{2,1,0:T(8,128)S(1)}, f32[8,10,256]{2,1,0:T(8,128)S(1)}, u32[]{:S(2)}, u32[]{:S(2)}) collective-permute-start(f32[8,10,256]{2,1,0:T(8,128)S(1)} %get-tuple-element.404), channel_id=1, source_target_pairs={{0,2},{1,3},{2,4},{3,5},{4,6},{5,7},{6,8},{7,9},{8,10},{9,11},{10,... | collective-permute-start | bytes 245768 | tf_op jit(solution)/shard_map/ppermute | solution.py:19
  308.0 14.1 %collective-permute-start.38 = (f32[8,10,256]{2,1,0:T(8,128)S(1)}, f32[8,10,256]{2,1,0:T(8,128)S(1)}, u32[]{:S(2)}, u32[]{:S(2)}) collective-permute-start(f32[8,10,256]{2,1,0:T(8,128)S(1)} %get-tuple-element.403), channel_id=1, source_target_pairs={{0,1},{1,2},{2,3},{3,4},{4,5},{5,6},{6,7},{7,8},{8,9},{9,10},{10,1... | collective-permute-start | bytes 245768 | tf_op jit(solution)/shard_map/ppermute | solution.py:19
  310.3 13.6 %collective-permute-start.39 = (f32[8,10,256]{2,1,0:T(8,128)S(1)}, f32[8,10,256]{2,1,0:T(8,128)S(1)}, u32[]{:S(2)}, u32[]{:S(2)}) collective-permute-start(f32[8,10,256]{2,1,0:T(8,128)S(1)} %get-tuple-element.402), channel_id=1, source_target_pairs={{0,127},{1,0},{2,1},{3,2},{4,3},{5,4},{6,5},{7,6},{8,7},{9,8},{10,... | collective-permute-start | bytes 245768 | tf_op jit(solution)/shard_map/ppermute | solution.py:19
  311.3 13.8 %collective-permute-start.40 = (f32[8,10,256]{2,1,0:T(8,128)S(1)}, f32[8,10,256]{2,1,0:T(8,128)S(1)}, u32[]{:S(2)}, u32[]{:S(2)}) collective-permute-start(f32[8,10,256]{2,1,0:T(8,128)S(1)} %get-tuple-element.401), channel_id=1, source_target_pairs={{0,126},{1,127},{2,0},{3,1},{4,2},{5,3},{6,4},{7,5},{8,6},{9,7},{1... | collective-permute-start | bytes 245768 | tf_op jit(solution)/shard_map/ppermute | solution.py:19
  323.9 14.7 %collective-permute-start.44 = (f32[8,10,256]{2,1,0:T(8,128)S(1)}, f32[8,10,256]{2,1,0:T(8,128)S(1)}, u32[]{:S(2)}, u32[]{:S(2)}) collective-permute-start(f32[8,10,256]{2,1,0:T(8,128)S(1)} %get-tuple-element.397), channel_id=1, source_target_pairs={{0,122},{1,123},{2,124},{3,125},{4,126},{5,127},{6,0},{7,1},{8,2},... | collective-permute-start | bytes 245768 | tf_op jit(solution)/shard_map/ppermute | solution.py:19
  325.1 19.4 %collective-permute-start.45 = (f32[8,10,256]{2,1,0:T(8,128)S(1)}, f32[8,10,256]{2,1,0:T(8,128)S(1)}, u32[]{:S(2)}, u32[]{:S(2)}) collective-permute-start(f32[8,10,256]{2,1,0:T(8,128)S(1)} %get-tuple-element.396), channel_id=1, source_target_pairs={{0,121},{1,122},{2,123},{3,124},{4,125},{5,126},{6,127},{7,0},{8,1... | collective-permute-start | bytes 245768 | tf_op jit(solution)/shard_map/ppermute | solution.py:19
  330.8 14.4 %collective-permute-start.46 = (f32[8,10,256]{2,1,0:T(8,128)S(1)}, f32[8,10,256]{2,1,0:T(8,128)S(1)}, u32[]{:S(2)}, u32[]{:S(2)}) collective-permute-start(f32[8,10,256]{2,1,0:T(8,128)S(1)} %get-tuple-element.395), channel_id=1, source_target_pairs={{0,120},{1,121},{2,122},{3,123},{4,124},{5,125},{6,126},{7,127},{8... | collective-permute-start | bytes 245768 | tf_op jit(solution)/shard_map/ppermute | solution.py:19
  331.5 15.8 %collective-permute-start.47 = (f32[8,10,256]{2,1,0:T(8,128)S(1)}, f32[8,10,256]{2,1,0:T(8,128)S(1)}, u32[]{:S(2)}, u32[]{:S(2)}) collective-permute-start(f32[8,10,256]{2,1,0:T(8,128)S(1)} %get-tuple-element.394), channel_id=1, source_target_pairs={{0,119},{1,120},{2,121},{3,122},{4,123},{5,124},{6,125},{7,126},{8... | collective-permute-start | bytes 245768 | tf_op jit(solution)/shard_map/ppermute | solution.py:19
  332.1 15.7 %collective-permute-start.48 = (f32[8,10,256]{2,1,0:T(8,128)S(1)}, f32[8,10,256]{2,1,0:T(8,128)S(1)}, u32[]{:S(2)}, u32[]{:S(2)}) collective-permute-start(f32[8,10,256]{2,1,0:T(8,128)S(1)} %get-tuple-element.393), channel_id=1, source_target_pairs={{0,118},{1,119},{2,120},{3,121},{4,122},{5,123},{6,124},{7,125},{8... | collective-permute-start | bytes 245768 | tf_op jit(solution)/shard_map/ppermute | solution.py:19
  338.6 14.1 %collective-permute-start.49 = (f32[8,10,256]{2,1,0:T(8,128)S(1)}, f32[8,10,256]{2,1,0:T(8,128)S(1)}, u32[]{:S(2)}, u32[]{:S(2)}) collective-permute-start(f32[8,10,256]{2,1,0:T(8,128)S(1)} %get-tuple-element.392), channel_id=1, source_target_pairs={{0,117},{1,118},{2,119},{3,120},{4,121},{5,122},{6,123},{7,124},{8... | collective-permute-start | bytes 245768 | tf_op jit(solution)/shard_map/ppermute | solution.py:19
  344.5 138.7 %collective-permute-start.50 = (f32[8,10,256]{2,1,0:T(8,128)S(1)}, f32[8,10,256]{2,1,0:T(8,128)S(1)}, u32[]{:S(2)}, u32[]{:S(2)}) collective-permute-start(f32[8,10,256]{2,1,0:T(8,128)S(1)} %get-tuple-element.391), channel_id=1, source_target_pairs={{0,116},{1,117},{2,118},{3,119},{4,120},{5,121},{6,122},{7,123},{8... | collective-permute-start | bytes 245768 | tf_op jit(solution)/shard_map/ppermute | solution.py:19
  345.2 138.7 %collective-permute-start.51 = (f32[8,10,256]{2,1,0:T(8,128)S(1)}, f32[8,10,256]{2,1,0:T(8,128)S(1)}, u32[]{:S(2)}, u32[]{:S(2)}) collective-permute-start(f32[8,10,256]{2,1,0:T(8,128)S(1)} %get-tuple-element.390), channel_id=1, source_target_pairs={{0,115},{1,116},{2,117},{3,118},{4,119},{5,120},{6,121},{7,122},{8... | collective-permute-start | bytes 245768 | tf_op jit(solution)/shard_map/ppermute | solution.py:19
  460.3 42.0 %all-to-all-start.1 = ((f32[2,2,256,256]{3,1,0,2:T(2,128)}), f32[2,2,256,256]{3,1,0,2:T(2,128)S(1)}, u32[]{:S(2)}, u32[]{:S(2)}) async-start(f32[2,2,256,256]{3,1,0,2:T(2,128)} %copy.170), calls=%async_computation.1 | async-start | bytes 2097152 | tf_op jit(solution)/shard_map/all_to_all | solution.py:234
  518.8 183.9 %all-to-all-start.2 = ((f32[2,256,2,256]{3,2,0,1:T(2,128)}), f32[2,256,2,256]{3,2,0,1:T(2,128)S(1)}, u32[]{:S(2)}, u32[]{:S(2)}) async-start(f32[2,256,2,256]{3,2,0,1:T(2,128)} %copy.180), calls=%async_computation.2 | async-start | bytes 2097152 | tf_op jit(solution)/shard_map/all_to_all | solution.py:259
  (52 other events, 1121.1 us)
where the time goes:
time: 726 us; the launch traced here: 714 us
  other arithmetic  363 us (50%)
  starting transfers between devices  144 us (20%)
  local copies, waits for them, and re-layouts  137 us (19%)
  waiting for transfers between devices  33.4 us (5%)
  matrix products  33.2 us (5%)
    ppermute x52, starting transfers between devices, shifted(): return lax.ppermute(value, axis, pairs)  107 us
    scatter-add x1, other arithmetic, per_device(): jax.ops.segment_sum(incoming[0].reshape(-1), incoming[1].reshape(-1).asty...  95.4 us
    unnamed x120, local copies, waits for them, and re-layouts  90.3 us
    reduce_sum x10, other arithmetic, force_terms(): push = -jnp.sum(coefficient[:, None] * separation, axis=3)  60.8 us
    mul x10, other arithmetic, force_terms(): far_weight[:, None, :]  60.4 us
    reduce_sum x10, other arithmetic, force_terms(): jnp.sum(far_weight[:, None, :] * own_slope * closing, axis=2)  43.6 us
    reduce_sum x10, other arithmetic, density_terms(): jnp.sum(spline_value(scaled_dist) * far_weight[:, None, :], axis=2)  34.6 us
    all_to_all x1, starting transfers between devices, per_device(): lax.all_to_all(jnp.stack([real_next, imag_next]), 'cells', split_axis=2,...  22.8 us
  transfers between devices with their start and end apart: 55, of which 9 were waited for; matrix products, arithmetic and copies ran while one was open for 69% of the time, Pallas kernels for 0%

commit v1 on v0

v1 whole, which is shorter than its diff:
```python
import functools
import math

import jax
import jax.numpy as jnp
import numpy as np
from jax import lax
from jax.experimental import pallas as pl
from jax.experimental.pallas import tpu as pltpu
from jax.sharding import PartitionSpec as P

M = 256
GROUP = 32
CAP = 8
HALF = 13
CELLS = 32
SLOTS = 256
STRIP = 32
F32 = jnp.float32
BF16 = jnp.bfloat16
NORM = 8.0 / math.pi
TINY = 1e-30
VMEM = pl.BlockSpec(memory_space=pltpu.VMEM)
SMEM = pl.BlockSpec(memory_space=pltpu.SMEM)
NT = (((1,), (1,)), ((), ()))
NN = (((1,), (0,)), ((), ()))
highest = lax.Precision.HIGHEST


def params(mib):
    return pltpu.CompilerParams(vmem_limit_bytes=mib * 1024 * 1024)


def cost(flops, nbytes):
    return pl.CostEstimate(flops=int(flops), bytes_accessed=int(nbytes), transcendentals=0)


def row_index(shape):
    return lax.broadcasted_iota(jnp.int32, shape, 0)


def rounded(value):
    return value.astype(BF16).astype(F32)


def thirds(value):
    first = rounded(value)
    rest = value - first
    second = rounded(rest)
    return first, second, rest - second


def place_rows(block, shift):
    row = row_index(block.shape)
    moved = jnp.where(row == 0, shift[0], jnp.where(row == 1, shift[1], shift[2])) - 0.5
    return row, jnp.where(row < 3, block + moved, 0.0)


def far_stack(basis):
    first, second, third = thirds(basis)
    return jnp.concatenate([first, second, first, second, third, first], axis=0)


def own_stack(basis):
    first, second, third = thirds(basis)
    return jnp.concatenate([first, first, second, second, first, third], axis=0)


def far_basis(block, shift):
    row, place = place_rows(block, shift)
    square = jnp.sum(place * place, axis=0, keepdims=True)
    basis = jnp.where(row == 3, square, jnp.where(row == 4, 1.0, place))
    return row, place, basis


def own_tables(own_ref, table_ref):
    zeros = jnp.zeros((16, SLOTS), F32)

    def one_cell(cell):
        block = own_ref[cell]
        row, place = place_rows(block, (0.0, 0.0, 0.0))
        square = jnp.sum(place * place, axis=0, keepdims=True)
        reach = block[7:8]
        inverse = 1.0 / (reach * reach)
        basis = jnp.where(
            row < 3, -2.0 * place, jnp.where(row == 3, 1.0, jnp.where(row == 4, square, 0.0))
        )
        stacked = jnp.concatenate(
            [own_stack(basis * inverse), zeros, own_stack(basis), zeros], axis=0
        )
        table_ref[cell] = stacked.T.astype(BF16)

    def some_cells(step, carry):
        for part in range(4):
            one_cell(step * 4 + part)
        return carry

    lax.fori_loop(0, CELLS // 4, some_cells, 0)


def kernel_half(square):
    square = jnp.maximum(square, TINY)
    dist = square * lax.rsqrt(square)
    left = jnp.maximum(1.0 - dist, 0.0)
    inner = 0.5 - 3.0 * square * left
    outer = left * left * left
    return jnp.where(square <= 0.25, inner, outer)


def slope_sixth(square):
    square = jnp.minimum(jnp.maximum(square, TINY), 1.0)
    inverse = lax.rsqrt(square)
    dist = square * inverse
    inner = 3.0 * dist - 2.0
    outer = (2.0 - dist) - inverse
    return jnp.where(square <= 0.25, inner, outer)


def in_turn(amount, first_half, second_half):
    first_half(0, 0)

    def two_pairs(step, carry):
        pair = 2 * step
        first_half(pair + 1, 1)
        second_half(pair, 0)
        first_half(jnp.minimum(pair + 2, amount - 1), 0)
        second_half(pair + 1, 1)
        return carry

    lax.fori_loop(0, amount // 2, two_pairs, 0)


def density_first(table_ref, square_ref, owner, block, shift):
    _, _, basis = far_basis(block, shift)
    far = jnp.concatenate([far_stack(basis), jnp.zeros((80, SLOTS), F32)], axis=0).astype(BF16)
    square_ref[...] = lax.dot_general(table_ref[owner], far, NN, preferred_element_type=F32)


def density_second(total_ref, square_ref, owner, weight):
    for start in range(0, SLOTS, STRIP):
        terms = kernel_half(square_ref[start : start + STRIP, :]) * weight
        total_ref[owner, start : start + STRIP, :] += terms[:, 0:128] + terms[:, 128:256]


def listed(which, info_ref, list_ref):
    pairs = info_ref.shape[1]

    def one_pair(pair, found):
        list_ref[found] = pair
        return found + (info_ref[2, pair] == which).astype(jnp.int32)

    found = lax.fori_loop(0, pairs, one_pair, jnp.int32(0))
    list_ref[found] = pairs
    list_ref[found + 1] = pairs
    return (found + 1) // 2 * 2


def pair_at(list_ref, info_ref, shift_ref, place):
    pair = list_ref[place]
    real = pair < info_ref.shape[1]
    pair = jnp.minimum(pair, info_ref.shape[1] - 1)
    owner = info_ref[0, pair]
    shift = (shift_ref[0, pair], shift_ref[1, pair], shift_ref[2, pair])
    return owner, jnp.where(real, owner, CELLS), info_ref[1, pair], shift


NO_SHIFT = (0.0, 0.0, 0.0)


def density_self_kernel(own_ref, table_ref, total_ref, even_ref, odd_ref):
    own_tables(own_ref, table_ref)
    total_ref[...] = jnp.zeros_like(total_ref)
    buffers = (even_ref, odd_ref)

    def first_half(cell, buffer):
        density_first(table_ref, buffers[buffer], cell, own_ref[cell], NO_SHIFT)

    def second_half(cell, buffer):
        density_second(total_ref, buffers[buffer], cell, own_ref[cell, 3:4, :])

    in_turn(CELLS, first_half, second_half)


def density_cross_kernel(which, finish, count_ref, info_ref, shift_ref, table_ref, far_ref, *refs):
    if finish:
        own_ref, heat_ref, before_ref, total_ref, density_ref, factor_ref = refs[:6]
    else:
        before_ref, total_ref = refs[:2]
    list_ref, even_ref, odd_ref = refs[-3:]
    buffers = (even_ref, odd_ref)
    amount = listed(which, info_ref, list_ref)

    def first_half(place, buffer):
        owner, _, source, shift = pair_at(list_ref, info_ref, shift_ref, place)
        density_first(table_ref, buffers[buffer], owner, far_ref[source], shift)

    def second_half(place, buffer):
        _, target, source, _ = pair_at(list_ref, info_ref, shift_ref, place)
        density_second(total_ref, buffers[buffer], target, far_ref[source, 3:4, :])

    in_turn(amount, first_half, second_half)
    if not finish:
        return

    lane = lax.broadcasted_iota(jnp.int32, (1, SLOTS), 1)

    def one_cell(cell):
        raw = jnp.sum(total_ref[cell].T, axis=0, keepdims=True)
        reach = own_ref[cell, 7:8, :]
        raw = raw * (2.0 * NORM) / (reach * reach * reach)
        density = jnp.where(lane < count_ref[cell], raw, 1.0)
        density_ref[pl.ds(cell, 1), :] = density
        factor_ref[pl.ds(cell, 1), :] = 2.0 / 3.0 * heat_ref[pl.ds(cell, 1), :] / density

    def some_cells(step, carry):
        for part in range(4):
            one_cell(step * 4 + part)
        return carry

    lax.fori_loop(0, CELLS // 4, some_cells, 0)


def force_first(table_ref, own_square_ref, far_square_ref, column_ref, owner, block, factor, shift):
    row, place, basis = far_basis(block, shift)
    reach = block[7:8]
    weight = block[3:4]
    inverse = 1.0 / (reach * reach)
    pad_low = jnp.zeros((80, SLOTS), F32)
    pad_high = jnp.zeros((64, SLOTS), F32)
    pad_end = jnp.zeros((16, SLOTS), F32)
    far_own = jnp.concatenate([far_stack(basis), pad_low], axis=0).astype(BF16)
    far_far = jnp.concatenate([pad_high, far_stack(basis * inverse), pad_end], axis=0).astype(BF16)
    table = table_ref[owner]
    own_square_ref[...] = lax.dot_general(table, far_own, NN, preferred_element_type=F32)
    far_square_ref[...] = lax.dot_general(table, far_far, NN, preferred_element_type=F32)
    swirl = jnp.sum(place[0:3] * block[4:7], axis=0, keepdims=True)
    own_side = jnp.where(
        row < 3, place, jnp.where(row == 3, 1.0, jnp.where(row == 7, swirl, block))
    )
    own_side = own_side * weight
    far_side = jnp.where(row < 3, place, jnp.where(row == 3, 1.0, 0.0))
    far_side = far_side * (weight * factor * (6.0 * NORM) * inverse * inverse / reach)
    own_first = rounded(own_side)
    own_second = own_side - own_first
    far_first = rounded(far_side)
    far_second = far_side - far_first
    none = jnp.zeros((8, SLOTS), F32)
    column_ref[...] = jnp.concatenate(
        [
            jnp.concatenate([own_first, own_second, none, none], axis=0),
            jnp.concatenate([own_first, none, none, none], axis=0),
            jnp.concatenate([none, none, far_first, far_second], axis=0),
            jnp.concatenate([none, none, far_first, none], axis=0),
        ],
        axis=1,
    ).astype(BF16)


def split(slope):
    high = slope.astype(BF16)
    return high, (slope - high.astype(F32)).astype(BF16)


def force_second(total_ref, own_square_ref, far_square_ref, column_ref, slope_ref, owner):
    for start in range(0, SLOTS, STRIP):
        rows = slice(start, start + STRIP)
        own_high, own_low = split(slope_sixth(own_square_ref[rows, :]))
        slope_ref[rows, 0:256] = own_high
        slope_ref[rows, 256:512] = own_low
        far_high, far_low = split(slope_sixth(far_square_ref[rows, :]))
        slope_ref[rows, 512:768] = far_high
        slope_ref[rows, 768:1024] = far_low
    total_ref[owner, :, 0:32] += lax.dot_general(
        slope_ref[...], column_ref[...], NT, preferred_element_type=F32
    )


def force_scratch():
    square = pltpu.VMEM((SLOTS, SLOTS), F32)
    return [square, square, square, square] + [pltpu.VMEM((32, 4 * SLOTS), BF16)] * 2 + [
        pltpu.VMEM((SLOTS, 4 * SLOTS), BF16)
    ] * 2


def force_self_kernel(own_ref, factor_ref, table_ref, total_ref, *refs):
    total_ref[...] = jnp.zeros_like(total_ref)

    def first_half(cell, buffer):
        factor = factor_ref[pl.ds(cell, 1), :]
        force_first(
            table_ref, refs[buffer], refs[2 + buffer], refs[4 + buffer], cell, own_ref[cell], factor, NO_SHIFT
        )

    def second_half(cell, buffer):
        force_second(total_ref, refs[buffer], refs[2 + buffer], refs[4 + buffer], refs[6 + buffer], cell)

    in_turn(CELLS, first_half, second_half)


def force_cross_kernel(
    which, finish, count_ref, info_ref, shift_ref, table_ref, far_ref, far_factor_ref, *refs
):
    if finish:
        own_ref, factor_ref, before_ref, total_ref, push_ref = refs[:5]
    else:
        before_ref, total_ref = refs[:2]
    list_ref, *refs = refs[-9:]
    amount = listed(which, info_ref, list_ref)

    def first_half(place, buffer):
        owner, _, source, shift = pair_at(list_ref, info_ref, shift_ref, place)
        factor = far_factor_ref[pl.ds(source, 1), :]
        force_first(
            table_ref, refs[buffer], refs[2 + buffer], refs[4 + buffer], owner, far_ref[source], factor, shift
        )

    def second_half(place, buffer):
        _, target, _, _ = pair_at(list_ref, info_ref, shift_ref, place)
        force_second(total_ref, refs[buffer], refs[2 + buffer], refs[4 + buffer], refs[6 + buffer], target)

    in_turn(amount, first_half, second_half)
    if not finish:
        return

    lane = lax.broadcasted_iota(jnp.int32, (1, SLOTS), 1)

    def one_cell(cell):
        sums = total_ref[cell].T
        own = sums[0:8] + sums[8:16]
        far = sums[16:24] + sums[24:32]
        block = own_ref[cell]
        _, place = place_rows(block, NO_SHIFT)
        reach = block[7:8]
        inverse = 1.0 / (reach * reach)
        scale = factor_ref[pl.ds(cell, 1), :] * (6.0 * NORM) * inverse * inverse / reach
        place = place[0:3]
        speed = block[4:7]
        push = scale * (own[0:3] - place * own[3:4]) + (far[0:3] - place * far[3:4])
        warm = jnp.sum(
            speed * place * own[3:4] - speed * own[0:3] - place * own[4:7], axis=0, keepdims=True
        )
        warm = scale * (warm + own[7:8])
        live = lane < count_ref[cell]
        push_ref[cell, 0:3, :] = jnp.where(live, push, 0.0)
        push_ref[cell, 3:4, :] = jnp.where(live, warm, 0.0)

    def some_cells(step, carry):
        for part in range(4):
            one_cell(step * 4 + part)
        return carry

    lax.fori_loop(0, CELLS // 4, some_cells, 0)


def sort_kernel(owner_ref, cell_ref, mass_ref, mass_out, cell_out, parts_ref):
    span = 256
    devices = 128
    device_row = row_index((devices, span))
    before = (row_index((span, span)) <= lax.broadcasted_iota(jnp.int32, (span, span), 1)).astype(BF16)
    parts_ref[...] = jnp.zeros_like(parts_ref)

    def chunk(step, taken):
        owner = owner_ref[pl.ds(step, 1), :]
        cell = cell_ref[pl.ds(step, 1), :]
        mass = mass_ref[pl.ds(step, 1), :]
        chosen = device_row == owner
        ones = chosen.astype(F32)
        upto = lax.dot_general(ones.astype(BF16), before, NN, preferred_element_type=F32)
        rank = jnp.sum(ones * (upto + taken), axis=0, keepdims=True) - 1.0
        slot = (device_row.astype(F32) == rank).astype(F32).astype(BF16)
        mass_parts = thirds(mass)
        cell_parts = (
            (cell & 63).astype(F32),
            ((cell >> 6) & 63).astype(F32),
            (cell >> 12).astype(F32),
        )
        values = [jnp.where(chosen, part, 0.0).astype(BF16) for part in mass_parts + cell_parts]
        parts_ref[...] += lax.dot_general(
            jnp.concatenate(values, axis=0), slot, NT, preferred_element_type=F32
        )
        return taken + upto[:, span - 1 : span]

    lax.fori_loop(0, owner_ref.shape[0], chunk, jnp.zeros((devices, 1), F32))
    n = devices
    mass_out[...] = (parts_ref[0:n] + parts_ref[n : 2 * n]) + parts_ref[2 * n : 3 * n]
    cell_out[...] = (
        parts_ref[3 * n : 4 * n]
        + 64.0 * parts_ref[4 * n : 5 * n]
        + 4096.0 * parts_ref[5 * n : 6 * n]
    )


def put_line(ref, line, rows):
    ref[pl.Slice(line, 128, 16), :] = rows[:, 0:128]
    ref[pl.Slice(8 + line, 128, 16), :] = rows[:, 128:256]


def get_line(ref, line):
    return jnp.concatenate(
        [ref[pl.Slice(line, 128, 16), :], ref[pl.Slice(8 + line, 128, 16), :]], axis=1
    )


def dot32(left, right):
    return lax.dot_general(left, right, NN, precision=highest, preferred_element_type=F32)


def deposit_kernel(mass_ref, cell_ref, z_ref, y_ref, out_ref, grid_ref):
    lanes = 128
    planes = grid_ref.shape[0]
    rows_at = row_index((planes, lanes))
    deep_at = row_index((M, lanes))
    grid_ref[...] = jnp.zeros_like(grid_ref)
    group = 8

    def chunk(step, carry):
        left, first, second = [], [], []
        for part in range(group):
            cell = cell_ref[pl.ds(step * group + part, 1), :].astype(jnp.int32)
            mass = mass_ref[pl.ds(step * group + part, 1), :]
            high = rounded(mass)
            low = mass - high
            left.append((rows_at == (cell >> 8)).astype(F32).astype(BF16))
            named = deep_at == (cell & 255)
            first.append(jnp.where(named, high, 0.0).astype(BF16))
            second.append(jnp.where(named, low, 0.0).astype(BF16))
        left = jnp.concatenate(left + left, axis=1)
        right = jnp.concatenate(first + second, axis=1)
        grid_ref[...] += lax.dot_general(left, right, NT, preferred_element_type=F32)
        return carry

    lax.fori_loop(0, mass_ref.shape[0] // group, chunk, 0)
    for plane in range(planes // M):
        piece = grid_ref[plane * M : (plane + 1) * M, :]
        turned = jnp.concatenate(
            [dot32(piece, z_ref[:, 0:M]), dot32(piece, z_ref[:, M : 2 * M])], axis=0
        )
        for part in range(4):
            rows = dot32(y_ref[part * 128 : (part + 1) * 128, :], turned)
            put_line(out_ref, plane * 4 + part, rows)


def filter_kernel(first_ref, in_ref, forward_ref, back_ref, out_ref):
    for line in range(2):
        pieces = [
            get_line(in_ref, plane * 4 + part * 2 + line)
            for part in range(2)
            for plane in range(2)
        ]
        spectrum = dot32(forward_ref[...], jnp.concatenate(pieces, axis=0))
        along_x = row_index((M, M))
        along_z = lax.broadcasted_iota(jnp.int32, (M, M), 1)
        along_x = jnp.where(along_x < M // 2, along_x, along_x - M)
        along_z = jnp.where(along_z < M // 2, along_z, along_z - M)
        along_y = first_ref[0] + line
        along_y = jnp.where(along_y < M // 2, along_y, along_y - M)
        square = (along_x * along_x + along_z * along_z + along_y * along_y).astype(F32)
        step = 2.0 * math.pi / M
        green = jnp.where(square > 0, -1.0 / (step * step * jnp.maximum(square, 1.0)), 0.0)
        spectrum = jnp.concatenate([spectrum[0:M] * green, spectrum[M : 2 * M] * green], axis=0)
        result = dot32(back_ref[...], spectrum)
        for piece in range(4):
            part, plane = piece // 2, piece % 2
            put_line(
                out_ref, plane * 4 + part * 2 + line, result[piece * 128 : (piece + 1) * 128]
            )


def potential_kernel(in_ref, y_ref, z_ref, out_ref):
    for plane in range(2):
        pieces = [get_line(in_ref, plane * 4 + part) for part in range(4)]
        turned = dot32(y_ref[...], jnp.concatenate(pieces, axis=0))
        out_ref[plane] = dot32(turned[0:M], z_ref[0:M, :]) + dot32(
            turned[M : 2 * M], z_ref[M : 2 * M, :]
        )


def wave_tables():
    index = np.arange(M)
    angle = 2.0 * np.pi / M * (np.outer(index, index) % M)
    cosine, sine = np.cos(angle), np.sin(angle)
    pairs = np.concatenate([index[0::2], index[1::2]])
    z_forward = np.concatenate([cosine, -sine], axis=1)
    y_forward = np.block([[cosine[pairs], sine[pairs]], [-sine[pairs], cosine[pairs]]])
    x_forward = np.block([[cosine[:, pairs], sine[:, pairs]], [-sine[:, pairs], cosine[:, pairs]]])
    x_back = np.block([[cosine[pairs], -sine[pairs]], [sine[pairs], cosine[pairs]]])
    y_back = np.block([[cosine[:, pairs], -sine[:, pairs]], [sine[:, pairs], cosine[:, pairs]]])
    z_back = np.concatenate([cosine, -sine], axis=0) / float(M) ** 3
    return [
        np.asarray(item, np.float32)
        for item in (z_forward, y_forward, x_forward, x_back, y_back, z_back)
    ]


def per_device(
    positions,
    velocities,
    masses,
    smoothing,
    energies,
    cell_counts,
    pair_list,
    export_list,
    mesh_owner,
    mesh_cell,
):
    devices = lax.axis_size("cells")
    me = lax.axis_index("cells").astype(jnp.int32)
    slots_iota = jnp.arange(SLOTS, dtype=jnp.int32)
    live = (slots_iota[None, :] < cell_counts[:, None]).astype(F32)
    heat = energies.reshape(CELLS, SLOTS)
    mass = masses.reshape(CELLS, SLOTS) * live
    own = jnp.concatenate(
        [
            positions.reshape(3, CELLS, SLOTS),
            (mass / SLOTS)[None],
            velocities.reshape(3, CELLS, SLOTS),
            smoothing.reshape(1, CELLS, SLOTS),
        ],
        axis=0,
    ).transpose(1, 0, 2)

    groups_a = [list(range(g, g + GROUP)) for g in range(0, devices, GROUP)]
    groups_b = [[(i + GROUP // 2) % devices for i in g] for g in groups_a]
    exports = export_list[0]
    lane32 = jnp.arange(GROUP, dtype=jnp.int32)

    def wanted(others):
        step = (me - others + devices // 2) % devices - devices // 2
        row = jnp.where(step < 0, step + HALF, step + HALF - 1)
        row = jnp.clip(row, 0, 2 * HALF - 1)
        return jnp.maximum(jnp.take(exports, row, axis=0), 0).reshape(-1)

    to_a = wanted(me // GROUP * GROUP + lane32)
    start_b = (me - GROUP // 2) % devices // GROUP * GROUP + GROUP // 2
    to_b = wanted((start_b + lane32) % devices)

    def swap(data, groups):
        return lax.all_to_all(data, "cells", 0, 0, axis_index_groups=groups, tiled=True)

    far_a = swap(jnp.take(own, to_a, axis=0), groups_a)
    far_b = swap(jnp.take(own, to_b, axis=0), groups_b)

    owner_cell, neighbour, slot, direction = (pair_list[i] for i in range(4))
    step = jnp.where(neighbour < HALF, neighbour - HALF, neighbour - HALF + 1)
    other = (me + step) % devices
    in_a = other // GROUP == me // GROUP
    place = jnp.where(in_a, other % GROUP, (other - GROUP // 2) % GROUP)
    info = jnp.stack([owner_cell, place * CAP + slot, jnp.where(in_a, 0, 1)]).astype(jnp.int32)
    shift = jnp.stack([direction // 9 - 1, direction // 3 % 3 - 1, direction % 3 - 1]).astype(F32)

    lines = CELLS * SLOTS // 256
    mass_sent, cell_sent = pl.pallas_call(
        sort_kernel,
        out_shape=[jax.ShapeDtypeStruct((devices, 128), F32)] * 2,
        in_specs=[VMEM] * 3,
        out_specs=[VMEM] * 2,
        scratch_shapes=[pltpu.VMEM((6 * 128, 128), F32)],
        compiler_params=params(32),
        cost_estimate=cost(6e9, 1e6),
        name="sort_masses",
    )(mesh_owner.reshape(lines, 256), mesh_cell.reshape(lines, 256), mass.reshape(lines, 256))

    table, total = pl.pallas_call(
        density_self_kernel,
        out_shape=[
            jax.ShapeDtypeStruct((CELLS, SLOTS, 128), BF16),
            jax.ShapeDtypeStruct((CELLS + 1, SLOTS, 128), F32),
        ],
        in_specs=[VMEM],
        out_specs=[VMEM] * 2,
        scratch_shapes=[pltpu.VMEM((SLOTS, SLOTS), F32)] * 2,
        compiler_params=params(32),
        cost_estimate=cost(8e9, 1e6),
        name="density_self",
    )(own)

    def density_cross(which, far, total, finish):
        out_shape = [jax.ShapeDtypeStruct((CELLS + 1, SLOTS, 128), F32)]
        extra = (total,)
        if finish:
            out_shape += [jax.ShapeDtypeStruct((CELLS, SLOTS), F32)] * 2
            extra = (own, heat, total)
        return pl.pallas_call(
            functools.partial(density_cross_kernel, which, finish),
            out_shape=out_shape,
            in_specs=[SMEM] * 3 + [VMEM] * (2 + len(extra)),
            out_specs=[VMEM] * len(out_shape),
            input_output_aliases={4 + len(extra): 0},
            scratch_shapes=[pltpu.SMEM((256,), jnp.int32)] + [pltpu.VMEM((SLOTS, SLOTS), F32)] * 2,
            compiler_params=params(40),
            cost_estimate=cost(1e10, 1e6),
            name="density_cross",
        )(cell_counts, info, shift, table, far, *extra)

    (total,) = density_cross(0, far_a, total, False)
    _, density, factor = density_cross(1, far_b, total, True)

    factor_a = swap(jnp.take(factor, to_a, axis=0), groups_a)
    factor_b = swap(jnp.take(factor, to_b, axis=0), groups_b)

    total = pl.pallas_call(
        force_self_kernel,
        out_shape=jax.ShapeDtypeStruct((CELLS + 1, SLOTS, 128), F32),
        in_specs=[VMEM] * 3,
        out_specs=VMEM,
        scratch_shapes=force_scratch(),
        compiler_params=params(40),
        cost_estimate=cost(1.5e10, 1e6),
        name="force_self",
    )(own, factor, table)

    def force_cross(which, far, far_factor, total, finish):
        out_shape = [jax.ShapeDtypeStruct((CELLS + 1, SLOTS, 128), F32)]
        extra = (total,)
        if finish:
            out_shape += [jax.ShapeDtypeStruct((CELLS, 4, SLOTS), F32)]
            extra = (own, factor, total)
        return pl.pallas_call(
            functools.partial(force_cross_kernel, which, finish),
            out_shape=out_shape,
            in_specs=[SMEM] * 3 + [VMEM] * (3 + len(extra)),
            out_specs=[VMEM] * len(out_shape),
            input_output_aliases={5 + len(extra): 0},
            scratch_shapes=[pltpu.SMEM((256,), jnp.int32)] + force_scratch(),
            compiler_params=params(40),
            cost_estimate=cost(3e10, 1e6),
            name="force_cross",
        )(cell_counts, info, shift, table, far, far_factor, *extra)

    (total,) = force_cross(0, far_a, factor_a, total, False)
    _, push = force_cross(1, far_b, factor_b, total, True)
    acceleration = push[:, 0:3].transpose(1, 0, 2).reshape(3, -1)
    heating = push[:, 3].reshape(-1)

    z_forward, y_forward, x_forward, x_back, y_back, z_back = wave_tables()
    swapped = swap(jnp.stack([mass_sent, cell_sent], axis=1), None)
    wide = jax.ShapeDtypeStruct((devices * 16, M // 2), F32)
    half_way = pl.pallas_call(
        deposit_kernel,
        out_shape=wide,
        in_specs=[VMEM] * 4,
        out_specs=VMEM,
        scratch_shapes=[pltpu.VMEM((2 * M, M), F32)],
        compiler_params=params(48),
        cost_estimate=cost(1.5e10, 1e6),
        name="deposit",
    )(swapped[:, 0], swapped[:, 1], z_forward, y_forward)
    half_way = swap(half_way.reshape(devices, 16, M // 2), None)
    back = pl.pallas_call(
        filter_kernel,
        out_shape=wide,
        in_specs=[SMEM] + [VMEM] * 3,
        out_specs=VMEM,
        compiler_params=params(48),
        cost_estimate=cost(5e9, 1e6),
        name="filter",
    )((2 * me).reshape(1), half_way.reshape(devices * 16, M // 2), x_forward, x_back)
    back = swap(back.reshape(devices, 16, M // 2), None)
    potential = pl.pallas_call(
        potential_kernel,
        out_shape=jax.ShapeDtypeStruct((2, M, M), F32),
        in_specs=[VMEM] * 3,
        out_specs=VMEM,
        compiler_params=params(48),
        cost_estimate=cost(4e9, 1e6),
        name="potential",
    )(back.reshape(devices * 16, M // 2), y_back, z_back)
    return (density.reshape(-1), acceleration, heating, potential)


def solution(mesh):
    in_specs = (
        P(None, "cells"),
        P(None, "cells"),
        P("cells"),
        P("cells"),
        P("cells"),
        P("cells"),
        P(None, "cells"),
        P("cells", None, None),
        P("cells", None),
        P("cells"),
    )
    out_specs = (P("cells"), P(None, "cells"), P("cells"), P("cells", None, None))
    return jax.shard_map(
        per_device, mesh=mesh, in_specs=in_specs, out_specs=out_specs, check_vma=False
    )
```

time: 726 us -> 311 us (0.43); the launches traced: 714 us -> 310 us
  other arithmetic: 363 us -> 11.2 us
  Pallas kernels: 0 us -> 154 us
  local copies, waits for them, and re-layouts: 137 us -> 34.6 us
  starting transfers between devices: 144 us -> 61.3 us
  matrix products: 33.2 us -> 0 us
  waiting for transfers between devices: 33.4 us -> 47.5 us
    reduce_sum x51 -> x0, other arithmetic: 186 us -> none  [the longest x10 60.8 us: force_terms(): push = -jnp.sum(coefficient[:, None] * separation, axis=3)]
    pallas_call x0 -> x10, Pallas kernels: none -> 154 us  [the longest x2 59.9 us: force_cross(): pl.pallas_call(functools.partial(force_cross_kernel, which, finish), out_...]
    ppermute x52 -> x0, starting transfers between devices: 107 us -> none  [shifted(): return lax.ppermute(value, axis, pairs)]
    scatter-add x1 -> x0, other arithmetic: 95.4 us -> none  [per_device(): jax.ops.segment_sum(incoming[0].reshape(-1), incoming[1].reshape(-1).asty...]
    mul x34 -> x1, other arithmetic: 69.5 us -> 0.73 us  [per_device(): mass = masses.reshape(CELLS, SLOTS) * live]
    unnamed x120 -> x53, local copies, waits for them, and re-layouts: 90.3 us -> 22.6 us
    all_to_all x3 -> x7, waiting for transfers between devices: 11.4 us -> 47.5 us  [swap(): lax.all_to_all(data, 'cells', 0, 0, axis_index_groups=groups, tiled=True)]
    dot_general x22 -> x0, matrix products: 33.2 us -> none  [the longest x8 13 us: along_first(): return jnp.einsum('xyz,xk->kyz', field, table, precision=highest)]
  transfers between devices with their start and end apart: 55 -> 7, of which waited for: 9 -> 4; matrix products, arithmetic and copies ran while one was open for 69% -> 6% of each run, Pallas kernels for 0% -> 30%
where the time goes in v1:
time: 311 us; the launch traced here: 310 us
  Pallas kernels  154 us (50%)
  starting transfers between devices  61.3 us (20%)
  waiting for transfers between devices  47.5 us (15%)
  local copies, waits for them, and re-layouts  34.6 us (11%)
  other arithmetic  11.2 us (4%)
    all_to_all x7, starting transfers between devices, swap(): lax.all_to_all(data, 'cells', 0, 0, axis_index_groups=groups, tiled=True)  61.3 us
    pallas_call x2, Pallas kernels, force_cross(): pl.pallas_call(functools.partial(force_cross_kernel, which, finish), out_...  59.9 us
    all_to_all x7, waiting for transfers between devices, swap(): lax.all_to_all(data, 'cells', 0, 0, axis_index_groups=groups, tiled=True)  47.5 us
    pallas_call x2, Pallas kernels, density_cross(): pl.pallas_call(functools.partial(density_cross_kernel, which, finish), ou...  29.6 us
    unnamed x53, local copies, waits for them, and re-layouts  22.6 us
    pallas_call x1, Pallas kernels, per_device(): pl.pallas_call(deposit_kernel, out_shape=wide, in_specs=[VMEM] * 4, out_s...  16.3 us
    pallas_call x1, Pallas kernels, per_device(): pl.pallas_call(sort_kernel, out_shape=[jax.ShapeDtypeStruct((devices, 128...  15.2 us
    pallas_call x1, Pallas kernels, per_device(): pl.pallas_call(force_self_kernel, out_shape=jax.ShapeDtypeStruct((CELLS +...  13.2 us
  transfers between devices with their start and end apart: 7, of which 4 were waited for; matrix products, arithmetic and copies ran while one was open for 6% of the time, Pallas kernels for 30%

profile of v1, /device:TPU:1, one launch (start us, length us, event | category | flops | bytes accessed | tf_op | source)
XLA Modules:
  0.0 310.1 jit_solution(577812188504893715)
XLA Ops:
  4.9 15.2 %sort_masses.1 = (f32[128,128]{1,0:T(8,128)S(1)}, f32[128,128]{1,0:T(8,128)S(1)}) custom-call(s32[32,256]{1,0:T(8,128)S(1)} %reshape.128.owner_ref, s32[32,256]{1,0:T(8,128)S(1)} %reshape.129.cell_ref, f32[32,256]{1,0:T(8,128)S(1)} %fusion.1.mass_ref), custom_call_target="tpu_custom_call" | custom-call | flops 6000000000 | bytes 1000000 | tf_op jit(solution)/shard_map/sort_masses/pallas_call | solution.py:553
  20.9 11.5 %all-to-all-start.4 = ((f32[128,2,128]{2,1,0:T(2,128)}), f32[128,2,128]{2,1,0:T(2,128)S(1)}, u32[]{:S(2)}, u32[]{:S(2)}) async-start(f32[128,2,128]{2,1,0:T(2,128)} %copy.27), calls=%async_computation.4 | async-start | bytes 262144 | tf_op jit(solution)/shard_map/all_to_all | solution.py:539
  33.4 9.1 %all-to-all-done.4 = f32[128,2,128]{2,1,0:T(2,128)S(1)} async-done(((f32[128,2,128]{2,1,0:T(2,128)}), f32[128,2,128]{2,1,0:T(2,128)S(1)}, u32[]{:S(2)}, u32[]{:S(2)}) %all-to-all-start.4) | async-done | bytes 131104 | tf_op jit(solution)/shard_map/all_to_all | solution.py:539
  42.6 16.3 %deposit.1 = f32[2048,128]{1,0:T(8,128)} custom-call(f32[128,128]{1,0:T(8,128)S(1)} %bitcast.40, f32[128,128]{1,0:T(8,128)S(1)} %bitcast.39, f32[256,512]{1,0:T(8,128)S(1)} %copy-done.6, f32[512,512]{1,0:T(8,128)S(1)} %copy-done.4), custom_call_target="tpu_custom_call" | custom-call | flops 15000000512 | bytes 1000000 | tf_op jit(solution)/shard_map/deposit/pallas_call | solution.py:639
  58.9 4.2 %all-to-all-start.5 = ((f32[128,16,128]{2,1,0:T(8,128)}), f32[128,16,128]{2,1,0:T(8,128)S(1)}, u32[]{:S(2)}, u32[]{:S(2)}) async-start(f32[128,16,128]{2,1,0:T(8,128)} %bitcast.18), calls=%async_computation.5 | async-start | bytes 2097152 | tf_op jit(solution)/shard_map/all_to_all | solution.py:539
  64.5 1.7 broadcast_select_fusion
  66.2 16.3 %all-to-all-done.5 = f32[128,16,128]{2,1,0:T(8,128)S(1)} async-done(((f32[128,16,128]{2,1,0:T(8,128)}), f32[128,16,128]{2,1,0:T(8,128)S(1)}, u32[]{:S(2)}, u32[]{:S(2)}) %all-to-all-start.5) | async-done | bytes 1048608 | tf_op jit(solution)/shard_map/all_to_all | solution.py:539
  82.5 4.5 %all-to-all-start.1 = ((f32[256,8,256]{2,1,0:T(8,128)}), f32[256,8,256]{2,1,0:T(8,128)S(1)}, u32[]{:S(2)}, u32[]{:S(2)}) async-start(f32[256,8,256]{2,1,0:T(8,128)} %broadcast_select_fusion), calls=%async_computation.1 | async-start | bytes 4194304 | tf_op jit(solution)/shard_map/all_to_all | solution.py:539
  87.8 2.3 gather_fusion.1
  90.3 3.3 %broadcast_select_fusion.1 = f32[256,8,256]{2,1,0:T(8,128)} fusion(f32[256,8,256]{2,1,0:T(8,128)} %gather_fusion.1, pred[256]{0:T(512)(128)(4,1)S(1)} %compare_and_fusion.2), kind=kLoop, calls=%fused_computation.7 | loop fusion | flops 524288 | bytes 4194560 | tf_op jit(solution)/shard_map/jit(_take)/select_n | solution.py:542
  93.5 21.4 %all-to-all-done.1.far_ref = f32[256,8,256]{2,1,0:T(8,128)S(1)} async-done(((f32[256,8,256]{2,1,0:T(8,128)}), f32[256,8,256]{2,1,0:T(8,128)S(1)}, u32[]{:S(2)}, u32[]{:S(2)}) %all-to-all-start.1) | async-done | bytes 2097184 | tf_op jit(solution)/shard_map/all_to_all | solution.py:539
  115.0 9.2 %all-to-all-start = ((f32[256,8,256]{2,1,0:T(8,128)}), f32[256,8,256]{2,1,0:T(8,128)}, u32[]{:S(2)}, u32[]{:S(2)}) async-start(f32[256,8,256]{2,1,0:T(8,128)} %broadcast_select_fusion.1), calls=%async_computation | async-start | bytes 4194304 | tf_op jit(solution)/shard_map/all_to_all | solution.py:539
  124.2 7.5 %density_self.1 = (bf16[32,256,128]{2,1,0:T(8,128)(2,1)S(1)}, f32[33,256,128]{2,1,0:T(8,128)S(1)}) custom-call(f32[32,8,256]{2,1,0:T(8,128)S(1)} %maximum_bitcast_fusion.own_ref.refs_0_), custom_call_target="tpu_custom_call" | custom-call | flops 8000000000 | bytes 1000000 | tf_op jit(solution)/shard_map/density_self/pallas_call | solution.py:564
  131.7 6.6 %filter.1 = f32[2048,128]{1,0:T(8,128)} custom-call(s32[1]{0:T(128)} %bitcast.13.first_ref, f32[2048,128]{1,0:T(8,128)S(1)} %bitcast.34, f32[512,512]{1,0:T(8,128)S(1)} %copy-done.2, f32[512,512]{1,0:T(8,128)S(1)} %copy-done.3), custom_call_target="tpu_custom_call" | custom-call | flops 5000000000 | bytes 1000000 | tf_op jit(solution)/shard_map/filter/pallas_call | solution.py:650
  138.3 14.7 %density_cross.2.refs_2_ = f32[33,256,128]{2,1,0:T(8,128)S(1)} custom-call(s32[32]{0:T(128)S(1)} %copy-done, s32[3,128]{1,0:T(4,128)S(1)} %get-tuple-element.36.info_ref, f32[3,128]{1,0:T(4,128)S(1)} %get-tuple-element.37.shift_ref, bf16[32,256,128]{2,1,0:T(8,128)(2,1)S(1)} %get-tuple-element.14.table_ref, ...), custom_call_target="tpu_custom_call", output_to_operand_aliasing={{}: (5, {})} | custom-call | flops 10000000000 | bytes 1000000 | tf_op jit(solution)/shard_map/density_cross/pallas_call | solution.py:584
  153.0 2.0 copy-done.7
  155.0 13.3 %all-to-all-start.6 = ((f32[128,16,128]{2,1,0:T(8,128)}), f32[128,16,128]{2,1,0:T(8,128)S(1)}, u32[]{:S(2)}, u32[]{:S(2)}) async-start(f32[128,16,128]{2,1,0:T(8,128)} %bitcast.20), calls=%async_computation.6 | async-start | bytes 2097152 | tf_op jit(solution)/shard_map/all_to_all | solution.py:539
  168.3 2.2 copy-done.8
  172.1 15.0 %density_cross.3 = (f32[33,256,128]{2,1,0:T(8,128)S(1)}, f32[32,256]{1,0:T(8,128)S(1)}, f32[32,256]{1,0:T(8,128)S(1)}) custom-call(s32[32]{0:T(128)S(1)} %copy-done, s32[3,128]{1,0:T(4,128)S(1)} %get-tuple-element.36.info_ref, f32[3,128]{1,0:T(4,128)S(1)} %get-tuple-element.37.shift_ref, ...), custom_call_target="tpu_custom_call", output_to_operand_aliasing={{0}: (7, {})} | custom-call | flops 10000000000 | bytes 1000000 | tf_op jit(solution)/shard_map/density_cross/pallas_call | solution.py:584
  187.1 1.7 gather_fusion.5
  190.4 1.7 select_bitcast_fusion
  192.2 1.8 select_bitcast_fusion.1
  196.2 13.2 %force_self.1.refs_0_ = f32[33,256,128]{2,1,0:T(8,128)S(1)} custom-call(f32[32,8,256]{2,1,0:T(8,128)S(1)} %maximum_bitcast_fusion.own_ref.refs_0_, f32[32,256]{1,0:T(8,128)S(1)} %get-tuple-element.17.factor_ref.refs_1_, bf16[32,256,128]{2,1,0:T(8,128)(2,1)S(1)} %copy-done.11), custom_call_target="tpu_custom_call" | custom-call | flops 15000000512 | bytes 1000000 | tf_op jit(solution)/shard_map/force_self/pallas_call | solution.py:602
  209.4 2.0 copy-done.14
  211.4 7.4 %all-to-all-start.3 = ((f32[32,8,256]{2,1,0:T(8,128)}), f32[32,8,256]{2,1,0:T(8,128)}, u32[]{:S(2)}, u32[]{:S(2)}) async-start(f32[32,8,256]{2,1,0:T(8,128)} %select_bitcast_fusion), calls=%async_computation.3 | async-start | bytes 524288 | tf_op jit(solution)/shard_map/all_to_all | solution.py:539
  221.1 6.0 %potential.1 = f32[2,256,256]{2,1,0:T(8,128)} custom-call(f32[2048,128]{1,0:T(8,128)S(1)} %bitcast.35, f32[512,512]{1,0:T(8,128)S(1)} %copy-done.1, f32[512,256]{1,0:T(8,128)S(1)} %copy-done.5), custom_call_target="tpu_custom_call" | custom-call | flops 4000000000 | bytes 1000000 | tf_op jit(solution)/shard_map/potential/pallas_call | solution.py:660
  227.8 11.2 %all-to-all-start.2 = ((f32[32,8,256]{2,1,0:T(8,128)}), f32[32,8,256]{2,1,0:T(8,128)S(1)}, u32[]{:S(2)}, u32[]{:S(2)}) async-start(f32[32,8,256]{2,1,0:T(8,128)} %select_bitcast_fusion.1), calls=%async_computation.2 | async-start | bytes 524288 | tf_op jit(solution)/shard_map/all_to_all | solution.py:539
  240.6 2.2 copy-done.15
  242.8 31.2 %force_cross.2.refs_2_ = f32[33,256,128]{2,1,0:T(8,128)S(1)} custom-call(s32[32]{0:T(128)S(1)} %copy-done, s32[3,128]{1,0:T(4,128)S(1)} %get-tuple-element.36.info_ref, f32[3,128]{1,0:T(4,128)S(1)} %get-tuple-element.37.shift_ref, bf16[32,256,128]{2,1,0:T(8,128)(2,1)S(1)} %copy-done.12, ...), custom_call_target="tpu_custom_call", output_to_operand_aliasing={{}: (6, {})} | custom-call | flops 30000001024 | bytes 1000000 | tf_op jit(solution)/shard_map/force_cross/pallas_call | solution.py:619
  274.1 2.0 copy-done.16
  277.7 2.2 copy-done.17
  279.9 28.7 %force_cross.3 = (f32[33,256,128]{2,1,0:T(8,128)S(1)}, f32[32,4,256]{2,1,0:T(4,128)}) custom-call(s32[32]{0:T(128)S(1)} %copy-done, s32[3,128]{1,0:T(4,128)S(1)} %get-tuple-element.36.info_ref, f32[3,128]{1,0:T(4,128)S(1)} %get-tuple-element.37.shift_ref, bf16[32,256,128]{2,1,0:T(8,128)(2,1)S(1)} %copy-done.13, ...), custom_call_target="tpu_custom_call", output_to_operand_aliasing={{0}: (8, {})} | custom-call | flops 30000001024 | bytes 1000000 | tf_op jit(solution)/shard_map/force_cross/pallas_call | solution.py:619
  (84 shorter events, 21.3 us)
Async XLA Ops:
  4.9 27.6 %copy-start.23 = (s32[1,26,8]{1,2,0:T(8,128)S(1)}, s32[1,26,8]{1,2,0:T(8,128)}, u32[]{:S(2)}) copy-start(s32[1,26,8]{1,2,0:T(8,128)} %param.29) | copy-start | bytes 2500
  4.9 37.6 %copy-start.4 = (f32[512,512]{1,0:T(8,128)S(1)}, f32[512,512]{1,0:T(8,128)}, u32[]{:S(2)}) copy-start(f32[512,512]{1,0:T(8,128)} %constant.200.clone.y_ref) | copy-start | bytes 3145732
  4.9 37.7 %copy-start.6 = (f32[256,512]{1,0:T(8,128)S(1)}, f32[256,512]{1,0:T(8,128)}, u32[]{:S(2)}) copy-start(f32[256,512]{1,0:T(8,128)} %constant.199.clone.z_ref) | copy-start | bytes 1572868
  20.9 21.5 %all-to-all-start.4 = ((f32[128,2,128]{2,1,0:T(2,128)}), f32[128,2,128]{2,1,0:T(2,128)S(1)}, u32[]{:S(2)}, u32[]{:S(2)}) async-start(f32[128,2,128]{2,1,0:T(2,128)} %copy.27), calls=%async_computation.4 | async-start | bytes 262144 | tf_op jit(solution)/shard_map/all_to_all | solution.py:539
  58.9 4.3 %copy-start = (s32[32]{0:T(128)S(1)}, s32[32]{0:T(128)}, u32[]{:S(2)}) copy-start(s32[32]{0:T(128)} %count_ref.7) | copy-start | bytes 388
  58.9 4.3 %copy-start.18 = (f32[8192]{0:T(1024)S(1)}, f32[8192]{0:T(1024)}, u32[]{:S(2)}) copy-start(f32[8192]{0:T(1024)} %param.24) | copy-start | bytes 98308
  58.9 4.4 %copy-start.19 = (f32[3,8192]{1,0:T(4,128)S(1)}, f32[3,8192]{1,0:T(4,128)}, u32[]{:S(2)}) copy-start(f32[3,8192]{1,0:T(4,128)} %param.23) | copy-start | bytes 294916
  58.9 4.4 %copy-start.20 = (f32[3,8192]{1,0:T(4,128)S(1)}, f32[3,8192]{1,0:T(4,128)}, u32[]{:S(2)}) copy-start(f32[3,8192]{1,0:T(4,128)} %param.22) | copy-start | bytes 294916
  58.9 4.4 %copy-start.21 = (f32[8192]{0:T(1024)S(1)}, f32[8192]{0:T(1024)}, u32[]{:S(2)}) copy-start(f32[8192]{0:T(1024)} %param.25) | copy-start | bytes 98308
  58.9 23.6 %all-to-all-start.5 = ((f32[128,16,128]{2,1,0:T(8,128)}), f32[128,16,128]{2,1,0:T(8,128)S(1)}, u32[]{:S(2)}, u32[]{:S(2)}) async-start(f32[128,16,128]{2,1,0:T(8,128)} %bitcast.18), calls=%async_computation.5 | async-start | bytes 2097152 | tf_op jit(solution)/shard_map/all_to_all | solution.py:539
  82.5 32.5 %all-to-all-start.1 = ((f32[256,8,256]{2,1,0:T(8,128)}), f32[256,8,256]{2,1,0:T(8,128)S(1)}, u32[]{:S(2)}, u32[]{:S(2)}) async-start(f32[256,8,256]{2,1,0:T(8,128)} %broadcast_select_fusion), calls=%async_computation.1 | async-start | bytes 4194304 | tf_op jit(solution)/shard_map/all_to_all | solution.py:539
  87.8 2.4 copy-start.22
  87.8 2.4 copy-start.24
  115.0 40.0 %all-to-all-start = ((f32[256,8,256]{2,1,0:T(8,128)}), f32[256,8,256]{2,1,0:T(8,128)}, u32[]{:S(2)}, u32[]{:S(2)}) async-start(f32[256,8,256]{2,1,0:T(8,128)} %broadcast_select_fusion.1), calls=%async_computation | async-start | bytes 4194304 | tf_op jit(solution)/shard_map/all_to_all | solution.py:539
  124.1 7.5 %copy-start.2 = (f32[512,512]{1,0:T(8,128)S(1)}, f32[512,512]{1,0:T(8,128)}, u32[]{:S(2)}) copy-start(f32[512,512]{1,0:T(8,128)} %constant.201.clone.forward_ref) | copy-start | bytes 3145732
  124.1 7.5 %copy-start.3 = (f32[512,512]{1,0:T(8,128)S(1)}, f32[512,512]{1,0:T(8,128)}, u32[]{:S(2)}) copy-start(f32[512,512]{1,0:T(8,128)} %constant.202.clone.back_ref) | copy-start | bytes 3145732
  131.6 6.7 %copy-start.9 = (bf16[32,256,128]{2,1,0:T(8,128)(2,1)}, bf16[32,256,128]{2,1,0:T(8,128)(2,1)S(1)}, u32[]{:S(2)}) copy-start(bf16[32,256,128]{2,1,0:T(8,128)(2,1)S(1)} %get-tuple-element.14.table_ref) | copy-start | bytes 6291460
  153.0 2.0 copy-start.7
  155.0 56.5 %all-to-all-start.6 = ((f32[128,16,128]{2,1,0:T(8,128)}), f32[128,16,128]{2,1,0:T(8,128)S(1)}, u32[]{:S(2)}, u32[]{:S(2)}) async-start(f32[128,16,128]{2,1,0:T(8,128)} %bitcast.20), calls=%async_computation.6 | async-start | bytes 2097152 | tf_op jit(solution)/shard_map/all_to_all | solution.py:539
  168.3 2.2 copy-start.8
  170.5 1.6 copy-start.10
  194.6 1.6 copy-start.11
  209.4 2.0 copy-start.14
  211.4 16.4 %all-to-all-start.3 = ((f32[32,8,256]{2,1,0:T(8,128)}), f32[32,8,256]{2,1,0:T(8,128)}, u32[]{:S(2)}, u32[]{:S(2)}) async-start(f32[32,8,256]{2,1,0:T(8,128)} %select_bitcast_fusion), calls=%async_computation.3 | async-start | bytes 524288 | tf_op jit(solution)/shard_map/all_to_all | solution.py:539
  218.9 1.2 copy-start.1
  220.1 1.0 copy-start.5
  227.8 48.3 %all-to-all-start.2 = ((f32[32,8,256]{2,1,0:T(8,128)}), f32[32,8,256]{2,1,0:T(8,128)S(1)}, u32[]{:S(2)}, u32[]{:S(2)}) async-start(f32[32,8,256]{2,1,0:T(8,128)} %select_bitcast_fusion.1), calls=%async_computation.2 | async-start | bytes 524288 | tf_op jit(solution)/shard_map/all_to_all | solution.py:539
  239.0 1.6 copy-start.12
  240.6 2.2 copy-start.15
  274.0 2.0 copy-start.16
  276.1 1.6 copy-start.13
  277.7 2.2 copy-start.17

commit v2 on v1

v2 whole, which is shorter than its diff:
```python
import functools
import math

import jax
import jax.numpy as jnp
import numpy as np
from jax import lax
from jax.experimental import pallas as pl
from jax.experimental.pallas import tpu as pltpu
from jax.sharding import PartitionSpec as P

M = 256
GROUP = 32
CAP = 8
HALF = 13
CELLS = 32
SLOTS = 256
STRIP = 32
TOGETHER = 8
F32 = jnp.float32
BF16 = jnp.bfloat16
NORM = 8.0 / math.pi
TINY = 1e-30
VMEM = pl.BlockSpec(memory_space=pltpu.VMEM)
SMEM = pl.BlockSpec(memory_space=pltpu.SMEM)
NT = (((1,), (1,)), ((), ()))
NN = (((1,), (0,)), ((), ()))
TN = (((0,), (0,)), ((), ()))
NO_SHIFT = (0.0, 0.0, 0.0)
highest = lax.Precision.HIGHEST


def params(mib):
    return pltpu.CompilerParams(vmem_limit_bytes=mib * 1024 * 1024)


def cost(flops, nbytes):
    return pl.CostEstimate(
        flops=int(flops / 6), bytes_accessed=int(nbytes / 10), transcendentals=0
    )


def row_index(shape):
    return lax.broadcasted_iota(jnp.int32, shape, 0)


def rounded(value):
    return value.astype(BF16).astype(F32)


def thirds(value):
    first = rounded(value)
    rest = value - first
    second = rounded(rest)
    return first, second, rest - second


def place_rows(block, shift):
    row = row_index(block.shape)
    moved = jnp.where(row == 0, shift[0], jnp.where(row == 1, shift[1], shift[2])) - 0.5
    return row, jnp.where(row < 3, block + moved, 0.0)


def far_stack(basis):
    first, second, third = thirds(basis)
    return jnp.concatenate([first, second, first, second, third, first], axis=0)


def own_stack(basis):
    first, second, third = thirds(basis)
    return jnp.concatenate([first, first, second, second, first, third], axis=0)


def far_basis(block, shift):
    row, place = place_rows(block, shift)
    square = jnp.sum(place * place, axis=0, keepdims=True)
    basis = jnp.where(row == 3, square, jnp.where(row == 4, 1.0, place))
    return row, place, basis


def own_tables(own_ref, scaled_ref, table_ref):
    zeros = jnp.zeros((80, SLOTS), F32)

    def some_cells(step, carry):
        for part in range(4):
            cell = step * 4 + part
            row, place = place_rows(own_ref[cell], NO_SHIFT)
            square = jnp.sum(place * place, axis=0, keepdims=True)
            basis = jnp.where(
                row < 3, -2.0 * place, jnp.where(row == 3, 1.0, jnp.where(row == 4, square, 0.0))
            )
            table_ref[cell] = own_stack(basis).astype(BF16)
            scaled = own_stack(basis * own_inverse(own_ref, cell))
            scaled_ref[cell] = jnp.concatenate([scaled, zeros], axis=0).T.astype(BF16)
        return carry

    lax.fori_loop(0, CELLS // 4, some_cells, 0)


def kernel_half(square):
    square = jnp.maximum(square, TINY)
    dist = square * lax.rsqrt(square)
    left = jnp.maximum(1.0 - dist, 0.0)
    inner = 0.5 - 3.0 * square * left
    outer = left * left * left
    return jnp.where(square <= 0.25, inner, outer)


def slope_sixth(square):
    square = jnp.minimum(square, 1.0)
    inverse = lax.rsqrt(square)
    dist = square * inverse
    inner = 3.0 * dist - 2.0
    outer = (2.0 - dist) - inverse
    return jnp.where(square <= 0.25, inner, outer)


def together(amount, first_half, second_half):
    def some_pairs(step, carry):
        for part in range(TOGETHER):
            first_half(step * TOGETHER + part, part)
        for part in range(TOGETHER):
            second_half(step * TOGETHER + part, part)
        return carry

    lax.fori_loop(0, amount // TOGETHER, some_pairs, 0)


def density_pairs(amount, scaled_ref, total_ref, square_refs, pair):
    def first_half(place, part):
        owner, _, block, shift = pair(place)
        _, _, basis = far_basis(block, shift)
        square_refs[part][...] = lax.dot_general(
            scaled_ref[owner, :, 0:48],
            far_stack(basis).astype(BF16),
            NN,
            preferred_element_type=F32,
        )

    def second_half(place, part):
        _, target, block, _ = pair(place)
        weight = block[3:4]
        for start in range(0, SLOTS, STRIP):
            rows = slice(start, start + STRIP)
            terms = kernel_half(square_refs[part][rows, :]) * weight
            total_ref[target, rows, :] += terms[:, 0:128] + terms[:, 128:256]

    together(amount, first_half, second_half)


def own_inverse(own_ref, owner):
    reach = own_ref[owner, 7:8, :]
    return 1.0 / (reach * reach)


def listed(which, info_ref, list_ref):
    pairs = info_ref.shape[1]

    def one_pair(pair, found):
        list_ref[found] = pair
        return found + (info_ref[2, pair] == which).astype(jnp.int32)

    found = lax.fori_loop(0, pairs, one_pair, jnp.int32(0))
    for spare in range(TOGETHER - 1):
        list_ref[found + spare] = pairs
    return (found + TOGETHER - 1) // TOGETHER * TOGETHER


def pair_at(list_ref, info_ref, shift_ref, place):
    pair = list_ref[place]
    real = pair < info_ref.shape[1]
    pair = jnp.minimum(pair, info_ref.shape[1] - 1)
    owner = info_ref[0, pair]
    shift = (shift_ref[0, pair], shift_ref[1, pair], shift_ref[2, pair])
    return owner, jnp.where(real, owner, CELLS), info_ref[1, pair], shift


def density_scratch():
    return [pltpu.VMEM((SLOTS, SLOTS), F32)] * TOGETHER


def summed(total_ref, cell):
    return jnp.sum(total_ref[cell].T, axis=0, keepdims=True)


def density_self_kernel(own_ref, scaled_ref, table_ref, sum_ref, total_ref, *square_refs):
    own_tables(own_ref, scaled_ref, table_ref)
    total_ref[...] = jnp.zeros_like(total_ref)
    density_pairs(
        CELLS,
        scaled_ref,
        total_ref,
        square_refs,
        lambda cell: (cell, cell, own_ref[cell], NO_SHIFT),
    )

    def some_cells(step, carry):
        for part in range(4):
            cell = step * 4 + part
            sum_ref[pl.ds(cell, 1), :] = summed(total_ref, cell)
        return carry

    lax.fori_loop(0, CELLS // 4, some_cells, 0)


def density_cross_kernel(
    which, finish, count_ref, info_ref, shift_ref, scaled_ref, own_ref, far_ref, *refs
):
    if finish:
        heat_ref, before_ref, density_ref, factor_ref = refs[:4]
    else:
        before_ref, sum_ref = refs[:2]
    total_ref, list_ref, *square_refs = refs[-2 - TOGETHER :]
    amount = listed(which, info_ref, list_ref)
    total_ref[...] = jnp.zeros_like(total_ref)

    def pair(place):
        owner, target, source, shift = pair_at(list_ref, info_ref, shift_ref, place)
        return owner, target, far_ref[source], shift

    density_pairs(amount, scaled_ref, total_ref, square_refs, pair)
    lane = lax.broadcasted_iota(jnp.int32, (1, SLOTS), 1)

    def some_cells(step, carry):
        for part in range(4):
            cell = step * 4 + part
            line = pl.ds(cell, 1)
            raw = summed(total_ref, cell) + before_ref[line, :]
            if not finish:
                sum_ref[line, :] = raw
                continue
            reach = own_ref[cell, 7:8, :]
            raw = raw * (2.0 * NORM) / (reach * reach * reach)
            density = jnp.where(lane < count_ref[cell], raw, 1.0)
            density_ref[line, :] = density
            factor_ref[line, :] = 2.0 / 3.0 * heat_ref[line, :] / density
        return carry

    lax.fori_loop(0, CELLS // 4, some_cells, 0)


def force_first(table_ref, square_ref, column_ref, line_ref, owner, block, factor, shift):
    row, place, basis = far_basis(block, shift)
    square_ref[...] = lax.dot_general(
        far_stack(basis).astype(BF16), table_ref[owner], TN, preferred_element_type=F32
    )
    reach = block[7:8]
    weight = block[3:4]
    inverse = 1.0 / (reach * reach)
    column_ref[...] = jnp.broadcast_to(jnp.broadcast_to(inverse, (8, SLOTS)).T[:, 0:1], (SLOTS, 128))
    swirl = jnp.sum(place[0:3] * block[4:7], axis=0, keepdims=True)
    own_side = jnp.where(
        row < 3, place, jnp.where(row == 3, 1.0, jnp.where(row == 7, swirl, block))
    )
    own_side = own_side * weight
    far_side = jnp.where(row < 3, place, jnp.where(row == 3, 1.0, 0.0))
    far_side = far_side * (weight * factor * (6.0 * NORM) * inverse * inverse / reach)
    own_first = rounded(own_side)
    own_second = own_side - own_first
    far_first = rounded(far_side)
    far_second = far_side - far_first
    none = jnp.zeros((8, SLOTS), F32)
    line_ref[...] = jnp.concatenate(
        [
            jnp.concatenate([own_first, own_second, none, none], axis=0),
            jnp.concatenate([own_first, none, none, none], axis=0),
            jnp.concatenate([none, none, far_first, far_second], axis=0),
            jnp.concatenate([none, none, far_first, none], axis=0),
        ],
        axis=1,
    ).astype(BF16)


def split(slope):
    high = slope.astype(BF16)
    return high, (slope - high.astype(F32)).astype(BF16)


def force_second(total_ref, square_ref, column_ref, line_ref, slope_ref, target, inverse):
    for start in range(0, SLOTS, STRIP):
        rows = slice(start, start + STRIP)
        square = jnp.maximum(square_ref[rows, :], TINY)
        far_inverse = column_ref[rows, :]
        far_inverse = jnp.concatenate([far_inverse, far_inverse], axis=1)
        own_high, own_low = split(slope_sixth(square * inverse))
        far_high, far_low = split(slope_sixth(square * far_inverse))
        for part, piece in enumerate((own_high, own_low, far_high, far_low)):
            slope_ref[part * SLOTS + start : part * SLOTS + start + STRIP, :] = piece
    total_ref[target] += lax.dot_general(
        line_ref[...], slope_ref[...], NN, preferred_element_type=F32
    )


def force_scratch():
    return (
        [pltpu.VMEM((SLOTS, SLOTS), F32)] * TOGETHER
        + [pltpu.VMEM((SLOTS, 128), F32)] * TOGETHER
        + [pltpu.VMEM((32, 4 * SLOTS), BF16)] * TOGETHER
        + [pltpu.VMEM((4 * SLOTS, SLOTS), BF16)] * TOGETHER
    )


def force_pairs(amount, table_ref, own_ref, total_ref, refs, pair):
    def first_half(place, part):
        owner, _, block, factor, shift = pair(place)
        force_first(
            table_ref, *refs[part : 3 * TOGETHER : TOGETHER], owner, block, factor, shift
        )

    def second_half(place, part):
        owner, target, _, _, _ = pair(place)
        force_second(total_ref, *refs[part::TOGETHER], target, own_inverse(own_ref, owner))

    together(amount, first_half, second_half)


def force_self_kernel(own_ref, factor_ref, table_ref, total_ref, *refs):
    total_ref[...] = jnp.zeros_like(total_ref)

    def pair(cell):
        return cell, cell, own_ref[cell], factor_ref[pl.ds(cell, 1), :], NO_SHIFT

    force_pairs(CELLS, table_ref, own_ref, total_ref, refs, pair)


def force_cross_kernel(
    count_ref,
    info_ref,
    shift_ref,
    table_ref,
    own_ref,
    far_a_ref,
    far_b_ref,
    far_factor_ref,
    factor_ref,
    before_ref,
    push_ref,
    total_ref,
    list_ref,
    *refs,
):
    total_ref[...] = before_ref[...]
    for which, far_ref in enumerate((far_a_ref, far_b_ref)):
        amount = listed(which, info_ref, list_ref)

        def pair(place, far_ref=far_ref):
            owner, target, source, shift = pair_at(list_ref, info_ref, shift_ref, place)
            line = info_ref[3, jnp.minimum(list_ref[place], info_ref.shape[1] - 1)]
            return owner, target, far_ref[source], far_factor_ref[pl.ds(line, 1), :], shift

        force_pairs(amount, table_ref, own_ref, total_ref, refs, pair)

    lane = lax.broadcasted_iota(jnp.int32, (1, SLOTS), 1)

    def some_cells(step, carry):
        for part in range(4):
            cell = step * 4 + part
            sums = total_ref[cell]
            own = sums[0:8] + sums[8:16]
            far = sums[16:24] + sums[24:32]
            block = own_ref[cell]
            _, place = place_rows(block, NO_SHIFT)
            reach = block[7:8]
            inverse = 1.0 / (reach * reach)
            scale = factor_ref[pl.ds(cell, 1), :] * (6.0 * NORM) * inverse * inverse / reach
            place = place[0:3]
            speed = block[4:7]
            push = scale * (own[0:3] - place * own[3:4]) + (far[0:3] - place * far[3:4])
            warm = jnp.sum(
                speed * place * own[3:4] - speed * own[0:3] - place * own[4:7],
                axis=0,
                keepdims=True,
            )
            warm = scale * (warm + own[7:8])
            live = lane < count_ref[cell]
            push = jnp.where(live, push, 0.0)
            for line in range(3):
                push_ref[line, pl.ds(cell, 1), :] = push[line : line + 1]
            push_ref[3, pl.ds(cell, 1), :] = jnp.where(live, warm, 0.0)
        return carry

    lax.fori_loop(0, CELLS // 4, some_cells, 0)


def sort_kernel(owner_ref, cell_ref, mass_ref, mass_out, cell_out, parts_ref):
    span = 256
    together = 4
    devices = 128
    device_row = row_index((devices, span))
    slot_row = device_row.astype(F32)
    before = (
        row_index((span, span)) <= lax.broadcasted_iota(jnp.int32, (span, span), 1)
    ).astype(F32).astype(BF16)
    parts_ref[...] = jnp.zeros_like(parts_ref)

    def chunk(step, taken):
        named, values = [], []
        for part in range(together):
            line = pl.ds(step * together + part, 1)
            cell = cell_ref[line, :]
            chosen = device_row == owner_ref[line, :]
            ones = chosen.astype(F32)
            upto = lax.dot_general(ones.astype(BF16), before, NN, preferred_element_type=F32)
            rank = jnp.sum(ones * (upto + taken), axis=0, keepdims=True) - 1.0
            taken = taken + upto[:, span - 1 : span]
            named.append((slot_row == rank).astype(F32).astype(BF16))
            parts = thirds(mass_ref[line, :]) + (
                (cell & 63).astype(F32),
                ((cell >> 6) & 63).astype(F32),
                (cell >> 12).astype(F32),
            )
            values.append(
                jnp.concatenate([jnp.where(chosen, item, 0.0) for item in parts], axis=0).astype(BF16)
            )
        parts_ref[...] += lax.dot_general(
            jnp.concatenate(values, axis=1),
            jnp.concatenate(named, axis=1),
            NT,
            preferred_element_type=F32,
        )
        return taken

    lax.fori_loop(0, owner_ref.shape[0] // together, chunk, jnp.zeros((devices, 1), F32))
    n = devices
    mass_out[...] = (parts_ref[0:n] + parts_ref[n : 2 * n]) + parts_ref[2 * n : 3 * n]
    cell_out[...] = (
        parts_ref[3 * n : 4 * n]
        + 64.0 * parts_ref[4 * n : 5 * n]
        + 4096.0 * parts_ref[5 * n : 6 * n]
    )


def put_line(ref, line, rows):
    ref[pl.Slice(line, 128, 16), :] = rows[:, 0:128]
    ref[pl.Slice(8 + line, 128, 16), :] = rows[:, 128:256]


def get_line(ref, line):
    return jnp.concatenate(
        [ref[pl.Slice(line, 128, 16), :], ref[pl.Slice(8 + line, 128, 16), :]], axis=1
    )


def dot32(left, right):
    return lax.dot_general(left, right, NN, precision=highest, preferred_element_type=F32)


def deposit_kernel(mass_ref, cell_ref, z_ref, y_ref, out_ref, grid_ref):
    lanes = 128
    planes = grid_ref.shape[0]
    rows_at = row_index((planes, lanes))
    deep_at = row_index((M, lanes))
    grid_ref[...] = jnp.zeros_like(grid_ref)
    group = 8

    def chunk(step, carry):
        left, first, second = [], [], []
        for part in range(group):
            cell = cell_ref[pl.ds(step * group + part, 1), :].astype(jnp.int32)
            mass = mass_ref[pl.ds(step * group + part, 1), :]
            high = rounded(mass)
            low = mass - high
            left.append((rows_at == (cell >> 8)).astype(F32).astype(BF16))
            named = deep_at == (cell & 255)
            first.append(jnp.where(named, high, 0.0).astype(BF16))
            second.append(jnp.where(named, low, 0.0).astype(BF16))
        left = jnp.concatenate(left + left, axis=1)
        right = jnp.concatenate(first + second, axis=1)
        grid_ref[...] += lax.dot_general(left, right, NT, preferred_element_type=F32)
        return carry

    lax.fori_loop(0, mass_ref.shape[0] // group, chunk, 0)
    for plane in range(planes // M):
        piece = grid_ref[plane * M : (plane + 1) * M, :]
        turned = jnp.concatenate(
            [dot32(piece, z_ref[:, 0:M]), dot32(piece, z_ref[:, M : 2 * M])], axis=0
        )
        for part in range(4):
            rows = dot32(y_ref[part * 128 : (part + 1) * 128, :], turned)
            put_line(out_ref, plane * 4 + part, rows)


def filter_kernel(first_ref, in_ref, forward_ref, back_ref, out_ref):
    for line in range(2):
        pieces = [
            get_line(in_ref, plane * 4 + part * 2 + line)
            for part in range(2)
            for plane in range(2)
        ]
        spectrum = dot32(forward_ref[...], jnp.concatenate(pieces, axis=0))
        along_x = row_index((M, M))
        along_z = lax.broadcasted_iota(jnp.int32, (M, M), 1)
        along_x = jnp.where(along_x < M // 2, along_x, along_x - M)
        along_z = jnp.where(along_z < M // 2, along_z, along_z - M)
        along_y = first_ref[0] + line
        along_y = jnp.where(along_y < M // 2, along_y, along_y - M)
        square = (along_x * along_x + along_z * along_z + along_y * along_y).astype(F32)
        step = 2.0 * math.pi / M
        green = jnp.where(square > 0, -1.0 / (step * step * jnp.maximum(square, 1.0)), 0.0)
        spectrum = jnp.concatenate([spectrum[0:M] * green, spectrum[M : 2 * M] * green], axis=0)
        result = dot32(back_ref[...], spectrum)
        for piece in range(4):
            part, plane = piece // 2, piece % 2
            put_line(
                out_ref, plane * 4 + part * 2 + line, result[piece * 128 : (piece + 1) * 128]
            )


def potential_kernel(in_ref, y_ref, z_ref, out_ref):
    for plane in range(2):
        pieces = [get_line(in_ref, plane * 4 + part) for part in range(4)]
        turned = dot32(y_ref[...], jnp.concatenate(pieces, axis=0))
        out_ref[plane] = dot32(turned[0:M], z_ref[0:M, :]) + dot32(
            turned[M : 2 * M], z_ref[M : 2 * M, :]
        )


def wave_tables():
    index = np.arange(M)
    angle = 2.0 * np.pi / M * (np.outer(index, index) % M)
    cosine, sine = np.cos(angle), np.sin(angle)
    pairs = np.concatenate([index[0::2], index[1::2]])
    z_forward = np.concatenate([cosine, -sine], axis=1)
    y_forward = np.block([[cosine[pairs], sine[pairs]], [-sine[pairs], cosine[pairs]]])
    x_forward = np.block([[cosine[:, pairs], sine[:, pairs]], [-sine[:, pairs], cosine[:, pairs]]])
    x_back = np.block([[cosine[pairs], -sine[pairs]], [sine[pairs], cosine[pairs]]])
    y_back = np.block([[cosine[:, pairs], -sine[:, pairs]], [sine[:, pairs], cosine[:, pairs]]])
    z_back = np.concatenate([cosine, -sine], axis=0) / float(M) ** 3
    return [
        np.asarray(item, np.float32)
        for item in (z_forward, y_forward, x_forward, x_back, y_back, z_back)
    ]


def per_device(
    positions,
    velocities,
    masses,
    smoothing,
    energies,
    cell_counts,
    pair_list,
    export_list,
    mesh_owner,
    mesh_cell,
):
    devices = lax.axis_size("cells")
    me = lax.axis_index("cells").astype(jnp.int32)
    slots_iota = jnp.arange(SLOTS, dtype=jnp.int32)
    live = (slots_iota[None, :] < cell_counts[:, None]).astype(F32)
    heat = energies.reshape(CELLS, SLOTS)
    mass = masses.reshape(CELLS, SLOTS) * live
    own = jnp.concatenate(
        [
            positions.reshape(3, CELLS, SLOTS),
            (mass / SLOTS)[None],
            velocities.reshape(3, CELLS, SLOTS),
            smoothing.reshape(1, CELLS, SLOTS),
        ],
        axis=0,
    ).transpose(1, 0, 2)

    groups_a = [list(range(g, g + GROUP)) for g in range(0, devices, GROUP)]
    groups_b = [[(i + GROUP // 2) % devices for i in g] for g in groups_a]
    exports = export_list[0]
    lane32 = jnp.arange(GROUP, dtype=jnp.int32)

    def wanted(others):
        step = (me - others + devices // 2) % devices - devices // 2
        row = jnp.where(step < 0, step + HALF, step + HALF - 1)
        row = jnp.clip(row, 0, 2 * HALF - 1)
        return jnp.maximum(jnp.take(exports, row, axis=0), 0).reshape(-1)

    to_a = wanted(me // GROUP * GROUP + lane32)
    start_b = (me - GROUP // 2) % devices // GROUP * GROUP + GROUP // 2
    to_b = wanted((start_b + lane32) % devices)

    def swap(data, groups):
        return lax.all_to_all(data, "cells", 0, 0, axis_index_groups=groups, tiled=True)

    def pick(data, cells):
        return jnp.take(data, cells, axis=0, mode="clip")

    def after(data, *others):
        return lax.optimization_barrier((data, *others))[0]

    sent_a = pick(own, to_a)
    sent_b = pick(own, to_b)
    far_a = swap(sent_a, groups_a)
    mesh_owner, mesh_cell, mass = lax.optimization_barrier((mesh_owner, mesh_cell, mass, sent_a))[:3]

    owner_cell, neighbour, slot, direction = (pair_list[i] for i in range(4))
    step = jnp.where(neighbour < HALF, neighbour - HALF, neighbour - HALF + 1)
    other = (me + step) % devices
    in_a = other // GROUP == me // GROUP
    place = jnp.where(in_a, other % GROUP, (other - GROUP // 2) % GROUP)
    info = jnp.stack(
        [owner_cell, place * CAP + slot, jnp.where(in_a, 0, 1), other * CAP + slot]
    ).astype(jnp.int32)
    shift = jnp.stack([direction // 9 - 1, direction // 3 % 3 - 1, direction % 3 - 1]).astype(F32)

    lines = CELLS * SLOTS // 256
    mass_sent, cell_sent = pl.pallas_call(
        sort_kernel,
        out_shape=[jax.ShapeDtypeStruct((devices, 128), F32)] * 2,
        in_specs=[VMEM] * 3,
        out_specs=[VMEM] * 2,
        scratch_shapes=[pltpu.VMEM((6 * 128, 128), F32)],
        compiler_params=params(32),
        cost_estimate=cost(6e9, 1e6),
        name="sort_masses",
    )(mesh_owner.reshape(lines, 256), mesh_cell.reshape(lines, 256), mass.reshape(lines, 256))

    many = jax.ShapeDtypeStruct((CELLS + 1, 32, SLOTS), F32)
    each = jax.ShapeDtypeStruct((CELLS, SLOTS), F32)
    wide_total = [pltpu.VMEM((CELLS + 1, SLOTS, 128), F32)]
    places = [pltpu.SMEM((256,), jnp.int32)]
    scaled, table, partial = pl.pallas_call(
        density_self_kernel,
        out_shape=[
            jax.ShapeDtypeStruct((CELLS, SLOTS, 128), BF16),
            jax.ShapeDtypeStruct((CELLS, 48, SLOTS), BF16),
            each,
        ],
        in_specs=[VMEM],
        out_specs=[VMEM] * 3,
        scratch_shapes=wide_total + density_scratch(),
        compiler_params=params(40),
        cost_estimate=cost(8e9, 1e6),
        name="density_self",
    )(own)

    swapped = swap(after(jnp.stack([mass_sent, cell_sent], axis=1), far_a, partial), None)
    far_b = swap(after(sent_b, swapped), groups_b)

    def density_cross(which, far, partial, finish):
        extra = (heat, partial) if finish else (partial,)
        out_shape = [each, each] if finish else [each]
        return pl.pallas_call(
            functools.partial(density_cross_kernel, which, finish),
            out_shape=out_shape,
            in_specs=[SMEM] * 3 + [VMEM] * (3 + len(extra)),
            out_specs=[VMEM] * len(out_shape),
            scratch_shapes=wide_total + places + density_scratch(),
            compiler_params=params(40),
            cost_estimate=cost(1e10, 1e6),
            name="density_cross",
        )(cell_counts, info, shift, scaled, own, far, *extra)

    (partial_a,) = density_cross(0, far_a, partial, False)
    density, factor = density_cross(1, far_b, partial_a, True)

    z_forward, y_forward, x_forward, x_back, y_back, z_back = wave_tables()
    wide = jax.ShapeDtypeStruct((devices * 16, M // 2), F32)
    half_way = pl.pallas_call(
        deposit_kernel,
        out_shape=wide,
        in_specs=[VMEM] * 4,
        out_specs=VMEM,
        scratch_shapes=[pltpu.VMEM((2 * M, M), F32)],
        compiler_params=params(48),
        cost_estimate=cost(1.5e10, 1e6),
        name="deposit",
    )(swapped[:, 0], swapped[:, 1], z_forward, y_forward)
    half_way = swap(after(half_way.reshape(devices, 16, M // 2), far_b, partial_a), None)
    to_all = wanted(jnp.arange(devices, dtype=jnp.int32))
    far_factor = swap(after(pick(factor, to_all), half_way), None)

    total = pl.pallas_call(
        force_self_kernel,
        out_shape=many,
        in_specs=[VMEM] * 3,
        out_specs=VMEM,
        scratch_shapes=force_scratch(),
        compiler_params=params(40),
        cost_estimate=cost(1.5e10, 1e6),
        name="force_self",
    )(own, factor, table)

    push = pl.pallas_call(
        force_cross_kernel,
        out_shape=jax.ShapeDtypeStruct((4, CELLS, SLOTS), F32),
        in_specs=[SMEM] * 3 + [VMEM] * 7,
        out_specs=VMEM,
        scratch_shapes=[pltpu.VMEM(many.shape, F32)] + places + force_scratch(),
        compiler_params=params(48),
        cost_estimate=cost(6e10, 1e6),
        name="force_cross",
    )(cell_counts, info, shift, table, own, far_a, far_b, far_factor, factor, total)
    acceleration = push[0:3].reshape(3, -1)
    heating = push[3].reshape(-1)

    back = pl.pallas_call(
        filter_kernel,
        out_shape=wide,
        in_specs=[SMEM] + [VMEM] * 3,
        out_specs=VMEM,
        compiler_params=params(48),
        cost_estimate=cost(5e9, 1e6),
        name="filter",
    )((2 * me).reshape(1), half_way.reshape(devices * 16, M // 2), x_forward, x_back)
    back = swap(after(back.reshape(devices, 16, M // 2), far_factor), None)
    potential = pl.pallas_call(
        potential_kernel,
        out_shape=jax.ShapeDtypeStruct((2, M, M), F32),
        in_specs=[VMEM] * 3,
        out_specs=VMEM,
        compiler_params=params(48),
        cost_estimate=cost(4e9, 1e6),
        name="potential",
    )(back.reshape(devices * 16, M // 2), y_back, z_back)
    return (density.reshape(-1), acceleration, heating, potential)


def solution(mesh):
    in_specs = (
        P(None, "cells"),
        P(None, "cells"),
        P("cells"),
        P("cells"),
        P("cells"),
        P("cells"),
        P(None, "cells"),
        P("cells", None, None),
        P("cells", None),
        P("cells"),
    )
    out_specs = (P("cells"), P(None, "cells"), P("cells"), P("cells", None, None))
    return jax.shard_map(
        per_device, mesh=mesh, in_specs=in_specs, out_specs=out_specs, check_vma=False
    )
```

time: 311 us -> 239 us (0.77)
  waiting for transfers between devices: 47.5 us -> 16.3 us
  Pallas kernels: 154 us -> 130 us
  other arithmetic: 11.2 us -> 4.72 us
  starting transfers between devices: 61.3 us -> 55.9 us
  local copies, waits for them, and re-layouts: 34.6 us -> 30.1 us
    all_to_all x7 -> x6, waiting for transfers between devices: 47.5 us -> 16.3 us  [swap(): lax.all_to_all(data, 'cells', 0, 0, axis_index_groups=groups, tiled=True)]
    pallas_call x3 -> x2, Pallas kernels: 73.2 us -> 59 us  [the longest x1 48.7 us: per_device(): pl.pallas_call(force_cross_kernel, out_shape=jax.ShapeDtypeStruct((4, CEL...]
    pallas_call x1, Pallas kernels: 15.2 us -> 7 us  [per_device(): pl.pallas_call(sort_kernel, out_shape=[jax.ShapeDtypeStruct((devices, 128...]
    unnamed x53 -> x48, local copies, waits for them, and re-layouts: 22.6 us -> 16 us
    all_to_all x7 -> x6, starting transfers between devices: 61.3 us -> 55.9 us  [swap(): lax.all_to_all(data, 'cells', 0, 0, axis_index_groups=groups, tiled=True)]
    select_n x4 -> x1, other arithmetic: 4.95 us -> 0.02 us  [wanted(): return jnp.maximum(jnp.take(exports, row, axis=0), 0).reshape(-1)]
    all_to_all x2 -> x0, other arithmetic: 3.52 us -> none  [swap(): lax.all_to_all(data, 'cells', 0, 0, axis_index_groups=groups, tiled=True)]
    gather x4 -> x3, local copies, waits for them, and re-layouts: 6.71 us -> 9.42 us  [pick(): return jnp.take(data, cells, axis=0, mode='clip')]
  transfers between devices with their start and end apart: 7 -> 6, of which waited for: 4 -> 2; matrix products, arithmetic and copies ran while one was open for 6% -> 6% of each run, Pallas kernels for 30% -> 52%
where the time goes in v2:
time: 239 us; the launch traced here: 238 us
  Pallas kernels  130 us (54%)
  starting transfers between devices  55.9 us (23%)
  local copies, waits for them, and re-layouts  30.1 us (13%)
  waiting for transfers between devices  16.3 us (7%)
  other arithmetic  4.72 us (2%)
    all_to_all x6, starting transfers between devices, swap(): lax.all_to_all(data, 'cells', 0, 0, axis_index_groups=groups, tiled=True)  55.9 us
    pallas_call x1, Pallas kernels, per_device(): pl.pallas_call(force_cross_kernel, out_shape=jax.ShapeDtypeStruct((4, CEL...  48.7 us
    pallas_call x2, Pallas kernels, density_cross(): pl.pallas_call(functools.partial(density_cross_kernel, which, finish), ou...  28.3 us
    all_to_all x6, waiting for transfers between devices, swap(): lax.all_to_all(data, 'cells', 0, 0, axis_index_groups=groups, tiled=True)  16.3 us
    unnamed x48, local copies, waits for them, and re-layouts  16 us
    pallas_call x1, Pallas kernels, per_device(): pl.pallas_call(deposit_kernel, out_shape=wide, in_specs=[VMEM] * 4, out_s...  15.3 us
    pallas_call x1, Pallas kernels, per_device(): pl.pallas_call(force_self_kernel, out_shape=many, in_specs=[VMEM] * 3, ou...  10.3 us
    gather x3, local copies, waits for them, and re-layouts, pick(): return jnp.take(data, cells, axis=0, mode='clip')  9.42 us
  transfers between devices with their start and end apart: 6, of which 2 were waited for; matrix products, arithmetic and copies ran while one was open for 6% of the time, Pallas kernels for 52%

profile of v2, /device:TPU:1, one launch (start us, length us, event | category | flops | bytes accessed | tf_op | source)
XLA Modules:
  0.0 238.0 jit_solution(15477184550900975537)
XLA Ops:
  3.1 1.1 maximum_bitcast_fusion.own_ref
  4.2 2.4 gather_fusion.1
  6.6 8.7 %all-to-all-start = ((f32[256,8,256]{2,1,0:T(8,128)}), f32[256,8,256]{2,1,0:T(8,128)S(1)}, u32[]{:S(2)}, u32[]{:S(2)}) async-start(f32[256,8,256]{2,1,0:T(8,128)} %gather_fusion.1), calls=%async_computation | async-start | bytes 4194304 | tf_op jit(solution)/shard_map/all_to_all | solution.py:579
  17.3 7.0 %sort_masses.1 = (f32[128,128]{1,0:T(8,128)S(1)}, f32[128,128]{1,0:T(8,128)S(1)}) custom-call(s32[32,256]{1,0:T(8,128)S(1)} %reshape.212.owner_ref, s32[32,256]{1,0:T(8,128)S(1)} %reshape.213.cell_ref, f32[32,256]{1,0:T(8,128)S(1)} %fusion.1.mass_ref), custom_call_target="tpu_custom_call" | custom-call | flops 1000000000 | bytes 100000 | tf_op jit(solution)/shard_map/sort_masses/pallas_call | solution.py:603
  24.4 7.7 %density_self.1 = (bf16[32,256,128]{2,1,0:T(8,128)(2,1)S(1)}, bf16[32,48,256]{2,1,0:T(8,128)(2,1)S(1)}, f32[32,256]{1,0:T(8,128)S(1)}) custom-call(f32[32,8,256]{2,1,0:T(8,128)S(1)} %maximum_bitcast_fusion.own_ref), custom_call_target="tpu_custom_call" | custom-call | flops 1333333376 | bytes 100000 | tf_op jit(solution)/shard_map/density_self/pallas_call | solution.py:618
  32.1 1.3 copy-done.8
  33.4 1.0 copy-done.11
  34.4 8.8 %all-to-all-done.far_ref.far_a_ref = f32[256,8,256]{2,1,0:T(8,128)S(1)} async-done(((f32[256,8,256]{2,1,0:T(8,128)}), f32[256,8,256]{2,1,0:T(8,128)S(1)}, u32[]{:S(2)}, u32[]{:S(2)}) %all-to-all-start) | async-done | bytes 2097184 | tf_op jit(solution)/shard_map/all_to_all | solution.py:579
  43.9 8.1 %all-to-all-start.1 = ((f32[128,2,128]{2,1,0:T(2,128)}), f32[128,2,128]{2,1,0:T(2,128)S(1)}, u32[]{:S(2)}, u32[]{:S(2)}) async-start(f32[128,2,128]{2,1,0:T(2,128)} %copy.23), calls=%async_computation.1 | async-start | bytes 262144 | tf_op jit(solution)/shard_map/all_to_all | solution.py:579
  52.2 2.4 %gather_fusion = f32[256,8,256]{2,1,0:T(8,128)} fusion(f32[32,8,256]{2,1,0:T(8,128)S(1)} %maximum_bitcast_fusion.own_ref, s32[1024]{0:T(1024)S(1)} %pad_clamp_fusion.3), kind=kCustom, calls=%fused_computation.2 | custom fusion | bytes 4195328 | tf_op jit(solution)/shard_map/jit(_take)/gather | solution.py:582
  54.6 7.5 %all-to-all-done.1 = f32[128,2,128]{2,1,0:T(2,128)S(1)} async-done(((f32[128,2,128]{2,1,0:T(2,128)}), f32[128,2,128]{2,1,0:T(2,128)S(1)}, u32[]{:S(2)}, u32[]{:S(2)}) %all-to-all-start.1) | async-done | bytes 131104 | tf_op jit(solution)/shard_map/all_to_all | solution.py:579
  62.1 7.9 %all-to-all-start.2 = ((f32[256,8,256]{2,1,0:T(8,128)}), f32[256,8,256]{2,1,0:T(8,128)}, u32[]{:S(2)}, u32[]{:S(2)}) async-start(f32[256,8,256]{2,1,0:T(8,128)} %gather_fusion), calls=%async_computation.2 | async-start | bytes 4194304 | tf_op jit(solution)/shard_map/all_to_all | solution.py:579
  70.1 1.6 copy-done.9
  71.7 14.2 %density_cross.2.refs_1_ = f32[32,256]{1,0:T(8,128)S(1)} custom-call(s32[32]{0:T(128)S(1)} %copy-done.5, s32[4,128]{1,0:T(4,128)S(1)} %pad_add_fusion.info_ref, f32[3,128]{1,0:T(4,128)S(1)} %add_convert_fusion.shift_ref, bf16[32,256,128]{2,1,0:T(8,128)(2,1)S(1)} %copy-done.9, f32[32,8,256]{2,1,0:T(8,128)S(1)} %maximum_bitcast_fusion.own_ref, ...), custom_call_target="tpu_custom_call" | custom-call | flops 1666666624 | bytes 100000 | tf_op jit(solution)/shard_map/density_cross/pallas_call | solution.py:639
  86.0 15.3 %deposit.1 = f32[2048,128]{1,0:T(8,128)S(1)} custom-call(f32[128,128]{1,0:T(8,128)S(1)} %bitcast.39, f32[128,128]{1,0:T(8,128)S(1)} %bitcast.38, f32[256,512]{1,0:T(8,128)S(1)} %copy-done.7, f32[512,512]{1,0:T(8,128)S(1)} %copy-done.6), custom_call_target="tpu_custom_call" | custom-call | flops 2500000000 | bytes 100000 | tf_op jit(solution)/shard_map/deposit/pallas_call | solution.py:655
  102.3 11.7 %all-to-all-start.3 = ((f32[128,16,128]{2,1,0:T(8,128)}), f32[128,16,128]{2,1,0:T(8,128)S(1)}, u32[]{:S(2)}, u32[]{:S(2)}) async-start(f32[128,16,128]{2,1,0:T(8,128)} %bitcast.35), calls=%async_computation.3 | async-start | bytes 2097152 | tf_op jit(solution)/shard_map/all_to_all | solution.py:579
  114.1 1.2 gather_fusion.2
  117.6 1.6 copy-done.10
  119.2 14.1 %density_cross.3 = (f32[32,256]{1,0:T(8,128)S(1)}, f32[32,256]{1,0:T(8,128)S(1)}) custom-call(s32[32]{0:T(128)S(1)} %copy-done.5, s32[4,128]{1,0:T(4,128)S(1)} %pad_add_fusion.info_ref, f32[3,128]{1,0:T(4,128)S(1)} %add_convert_fusion.shift_ref, bf16[32,256,128]{2,1,0:T(8,128)(2,1)S(1)} %copy-done.10, f32[32,8,256]{2,1,0:T(8,128)S(1)} %maximum_bitcast_fusion.own_ref, ...), custom_call_target="tpu_custom_call" | custom-call | flops 1666666624 | bytes 100000 | tf_op jit(solution)/shard_map/density_cross/pallas_call | solution.py:639
  133.3 4.7 %gather_fusion.3 = f32[1024,256]{1,0:T(8,128)} fusion(f32[32,256]{1,0:T(8,128)S(1)} %get-tuple-element.31.factor_ref, s32[1024]{0:T(1024)S(1)} %broadcast_clamp_fusion), kind=kCustom, calls=%fused_computation.5 | custom fusion | bytes 2101248 | tf_op jit(solution)/shard_map/jit(_take)/gather | solution.py:582
  138.0 9.7 %all-to-all-start.4 = ((f32[128,8,256]{2,1,0:T(8,128)}), f32[128,8,256]{2,1,0:T(8,128)}, u32[]{:S(2)}, u32[]{:S(2)}) async-start(f32[128,8,256]{2,1,0:T(8,128)} %bitcast.44), calls=%async_computation.4 | async-start | bytes 2097152 | tf_op jit(solution)/shard_map/all_to_all | solution.py:579
  148.4 1.1 copy-done.12
  149.5 10.3 %force_self.1.before_ref = f32[33,32,256]{2,1,0:T(8,128)S(1)} custom-call(f32[32,8,256]{2,1,0:T(8,128)S(1)} %maximum_bitcast_fusion.own_ref, f32[32,256]{1,0:T(8,128)S(1)} %get-tuple-element.31.factor_ref, bf16[32,48,256]{2,1,0:T(8,128)(2,1)S(1)} %copy-done.12), custom_call_target="tpu_custom_call" | custom-call | flops 2500000000 | bytes 100000 | tf_op jit(solution)/shard_map/force_self/pallas_call | solution.py:669
  159.8 1.0 copy-done.14
  160.8 6.6 %filter.1 = f32[2048,128]{1,0:T(8,128)} custom-call(s32[1]{0:T(128)} %bitcast.14.first_ref, f32[2048,128]{1,0:T(8,128)S(1)} %bitcast.33, f32[512,512]{1,0:T(8,128)S(1)} %copy-done.1, f32[512,512]{1,0:T(8,128)S(1)} %copy-done.2), custom_call_target="tpu_custom_call" | custom-call | flops 833333312 | bytes 100000 | tf_op jit(solution)/shard_map/filter/pallas_call | solution.py:693
  167.5 9.8 %all-to-all-start.5 = ((f32[128,16,128]{2,1,0:T(8,128)}), f32[128,16,128]{2,1,0:T(8,128)S(1)}, u32[]{:S(2)}, u32[]{:S(2)}) async-start(f32[128,16,128]{2,1,0:T(8,128)} %bitcast.16), calls=%async_computation.5 | async-start | bytes 2097152 | tf_op jit(solution)/shard_map/all_to_all | solution.py:579
  177.3 1.1 copy-done.13
  178.4 1.2 copy-done.15
  179.6 48.7 %force_cross.1 = f32[4,32,256]{2,1,0:T(8,128)S(1)} custom-call(s32[32]{0:T(128)S(1)} %copy-done.5, s32[4,128]{1,0:T(4,128)S(1)} %pad_add_fusion.info_ref, f32[3,128]{1,0:T(4,128)S(1)} %add_convert_fusion.shift_ref, bf16[32,48,256]{2,1,0:T(8,128)(2,1)S(1)} %copy-done.13, f32[32,8,256]{2,1,0:T(8,128)S(1)} %maximum_bitcast_fusion.own_ref, ...), custom_call_target="tpu_custom_call" | custom-call | flops 10000000000 | bytes 100000 | tf_op jit(solution)/shard_map/force_cross/pallas_call | solution.py:680
  229.7 1.2 copy-done
  230.9 1.0 copy-done.4
  232.0 6.0 %potential.1 = f32[2,256,256]{2,1,0:T(8,128)} custom-call(f32[2048,128]{1,0:T(8,128)S(1)} %bitcast.34, f32[512,512]{1,0:T(8,128)S(1)} %copy-done, f32[512,256]{1,0:T(8,128)S(1)} %copy-done.4), custom_call_target="tpu_custom_call" | custom-call | flops 666666688 | bytes 100000 | tf_op jit(solution)/shard_map/potential/pallas_call | solution.py:703
  (75 shorter events, 10.8 us)
Async XLA Ops:
  6.6 8.8 %copy-start.16 = (f32[8192]{0:T(1024)S(1)}, f32[8192]{0:T(1024)}, u32[]{:S(2)}) copy-start(f32[8192]{0:T(1024)} %param.20) | copy-start | bytes 98308
  6.6 9.4 %copy-start.5 = (s32[32]{0:T(128)S(1)}, s32[32]{0:T(128)}, u32[]{:S(2)}) copy-start(s32[32]{0:T(128)} %count_ref.5) | copy-start | bytes 388
  6.6 10.0 %copy-start.17 = (s32[8192,1]{0,1:T(1,128)S(1)}, s32[8192,1]{0,1:T(1,128)}, u32[]{:S(2)}) copy-start(s32[8192,1]{0,1:T(1,128)} %param.26) | copy-start | bytes 98308
  6.6 10.7 %copy-start.18 = (s32[8192]{0:T(1024)S(1)}, s32[8192]{0:T(1024)}, u32[]{:S(2)}) copy-start(s32[8192]{0:T(1024)} %param.27) | copy-start | bytes 98308
  6.6 36.6 %all-to-all-start = ((f32[256,8,256]{2,1,0:T(8,128)}), f32[256,8,256]{2,1,0:T(8,128)S(1)}, u32[]{:S(2)}, u32[]{:S(2)}) async-start(f32[256,8,256]{2,1,0:T(8,128)} %gather_fusion.1), calls=%async_computation | async-start | bytes 4194304 | tf_op jit(solution)/shard_map/all_to_all | solution.py:579
  32.1 1.3 copy-start.8
  33.4 1.0 copy-start.11
  43.9 18.1 %all-to-all-start.1 = ((f32[128,2,128]{2,1,0:T(2,128)}), f32[128,2,128]{2,1,0:T(2,128)S(1)}, u32[]{:S(2)}, u32[]{:S(2)}) async-start(f32[128,2,128]{2,1,0:T(2,128)} %copy.23), calls=%async_computation.1 | async-start | bytes 262144 | tf_op jit(solution)/shard_map/all_to_all | solution.py:579
  54.6 15.4 %copy-start.20 = (s32[4,128]{1,0:T(4,128)S(1)}, s32[4,128]{1,0:T(4,128)}, u32[]{:S(2)}) copy-start(s32[4,128]{1,0:T(4,128)} %param.24) | copy-start | bytes 6148
  62.1 40.2 %all-to-all-start.2 = ((f32[256,8,256]{2,1,0:T(8,128)}), f32[256,8,256]{2,1,0:T(8,128)}, u32[]{:S(2)}, u32[]{:S(2)}) async-start(f32[256,8,256]{2,1,0:T(8,128)} %gather_fusion), calls=%async_computation.2 | async-start | bytes 4194304 | tf_op jit(solution)/shard_map/all_to_all | solution.py:579
  70.1 1.6 copy-start.9
  71.7 14.3 %copy-start.6 = (f32[512,512]{1,0:T(8,128)S(1)}, f32[512,512]{1,0:T(8,128)}, u32[]{:S(2)}) copy-start(f32[512,512]{1,0:T(8,128)} %constant.210.clone.y_ref) | copy-start | bytes 3145732
  71.7 14.3 %copy-start.7 = (f32[256,512]{1,0:T(8,128)S(1)}, f32[256,512]{1,0:T(8,128)}, u32[]{:S(2)}) copy-start(f32[256,512]{1,0:T(8,128)} %constant.209.clone.z_ref) | copy-start | bytes 1572868
  101.3 1.0 copy-start.3
  102.3 11.7 %copy-start.19 = (f32[8192]{0:T(1024)S(1)}, f32[8192]{0:T(1024)}, u32[]{:S(2)}) copy-start(f32[8192]{0:T(1024)} %param.22) | copy-start | bytes 98308
  102.3 35.7 %all-to-all-start.3 = ((f32[128,16,128]{2,1,0:T(8,128)}), f32[128,16,128]{2,1,0:T(8,128)S(1)}, u32[]{:S(2)}, u32[]{:S(2)}) async-start(f32[128,16,128]{2,1,0:T(8,128)} %bitcast.35), calls=%async_computation.3 | async-start | bytes 2097152 | tf_op jit(solution)/shard_map/all_to_all | solution.py:579
  117.6 1.6 copy-start.10
  138.0 29.5 %all-to-all-start.4 = ((f32[128,8,256]{2,1,0:T(8,128)}), f32[128,8,256]{2,1,0:T(8,128)}, u32[]{:S(2)}, u32[]{:S(2)}) async-start(f32[128,8,256]{2,1,0:T(8,128)} %bitcast.44), calls=%async_computation.4 | async-start | bytes 2097152 | tf_op jit(solution)/shard_map/all_to_all | solution.py:579
  148.3 1.1 copy-start.12
  149.5 11.3 %copy-start.1 = (f32[512,512]{1,0:T(8,128)S(1)}, f32[512,512]{1,0:T(8,128)}, u32[]{:S(2)}) copy-start(f32[512,512]{1,0:T(8,128)} %constant.211.clone.forward_ref) | copy-start | bytes 3145732
  149.5 11.3 %copy-start.2 = (f32[512,512]{1,0:T(8,128)S(1)}, f32[512,512]{1,0:T(8,128)}, u32[]{:S(2)}) copy-start(f32[512,512]{1,0:T(8,128)} %constant.212.clone.back_ref) | copy-start | bytes 3145732
  159.8 1.0 copy-start.14
  167.5 62.2 %all-to-all-start.5 = ((f32[128,16,128]{2,1,0:T(8,128)}), f32[128,16,128]{2,1,0:T(8,128)S(1)}, u32[]{:S(2)}, u32[]{:S(2)}) async-start(f32[128,16,128]{2,1,0:T(8,128)} %bitcast.16), calls=%async_computation.5 | async-start | bytes 2097152 | tf_op jit(solution)/shard_map/all_to_all | solution.py:579
  177.3 1.1 copy-start.13
  178.4 1.2 copy-start.15
  229.7 1.2 copy-start
  230.9 1.0 copy-start.4

commit v3 on v2

--- a/solution.py
+++ b/solution.py
@@ -17,6 +17,7 @@
 SLOTS = 256
 STRIP = 32
 TOGETHER = 8
+EARLY = 64
 F32 = jnp.float32
 BF16 = jnp.bfloat16
 NORM = 8.0 / math.pi
@@ -79,8 +80,6 @@
 
 
 def own_tables(own_ref, scaled_ref, table_ref):
-    zeros = jnp.zeros((80, SLOTS), F32)
-
     def some_cells(step, carry):
         for part in range(4):
             cell = step * 4 + part
@@ -90,24 +89,26 @@
                 row < 3, -2.0 * place, jnp.where(row == 3, 1.0, jnp.where(row == 4, square, 0.0))
             )
             table_ref[cell] = own_stack(basis).astype(BF16)
-            scaled = own_stack(basis * own_inverse(own_ref, cell))
-            scaled_ref[cell] = jnp.concatenate([scaled, zeros], axis=0).T.astype(BF16)
+            scaled_ref[cell] = own_stack(basis * own_inverse(own_ref, cell)).astype(BF16)
         return carry
 
     lax.fori_loop(0, CELLS // 4, some_cells, 0)
 
 
-def kernel_half(square):
+def kernel_and_slope(square):
     square = jnp.maximum(square, TINY)
-    dist = square * lax.rsqrt(square)
+    inverse = lax.rsqrt(square)
+    dist = square * inverse
     left = jnp.maximum(1.0 - dist, 0.0)
-    inner = 0.5 - 3.0 * square * left
-    outer = left * left * left
-    return jnp.where(square <= 0.25, inner, outer)
+    left_square = left * left
+    near = square <= 0.25
+    value = jnp.where(near, 0.5 - 3.0 * square * left, left_square * left)
+    slope = jnp.where(near, 2.0 - 3.0 * dist, left_square * inverse)
+    return value, slope
 
 
 def slope_sixth(square):
-    square = jnp.minimum(square, 1.0)
+    square = jnp.minimum(jnp.maximum(square, TINY), 1.0)
     inverse = lax.rsqrt(square)
     dist = square * inverse
     inner = 3.0 * dist - 2.0
@@ -115,7 +116,7 @@
     return jnp.where(square <= 0.25, inner, outer)
 
 
-def together(amount, first_half, second_half):
+def together(begin, amount, first_half, second_half):
     def some_pairs(step, carry):
         for part in range(TOGETHER):
             first_half(step * TOGETHER + part, part)
@@ -123,29 +124,7 @@
             second_half(step * TOGETHER + part, part)
         return carry
 
-    lax.fori_loop(0, amount // TOGETHER, some_pairs, 0)
-
-
-def density_pairs(amount, scaled_ref, total_ref, square_refs, pair):
-    def first_half(place, part):
-        owner, _, block, shift = pair(place)
-        _, _, basis = far_basis(block, shift)
-        square_refs[part][...] = lax.dot_general(
-            scaled_ref[owner, :, 0:48],
-            far_stack(basis).astype(BF16),
-            NN,
-            preferred_element_type=F32,
-        )
-
-    def second_half(place, part):
-        _, target, block, _ = pair(place)
-        weight = block[3:4]
-        for start in range(0, SLOTS, STRIP):
-            rows = slice(start, start + STRIP)
-            terms = kernel_half(square_refs[part][rows, :]) * weight
-            total_ref[target, rows, :] += terms[:, 0:128] + terms[:, 128:256]
-
-    together(amount, first_half, second_half)
+    lax.fori_loop(begin // TOGETHER, amount // TOGETHER, some_pairs, 0)
 
 
 def own_inverse(own_ref, owner):
@@ -175,60 +154,157 @@
     return owner, jnp.where(real, owner, CELLS), info_ref[1, pair], shift
 
 
-def density_scratch():
-    return [pltpu.VMEM((SLOTS, SLOTS), F32)] * TOGETHER
-
-
-def summed(total_ref, cell):
-    return jnp.sum(total_ref[cell].T, axis=0, keepdims=True)
-
-
-def density_self_kernel(own_ref, scaled_ref, table_ref, sum_ref, total_ref, *square_refs):
+def halves(value):
+    first = rounded(value)
+    return first, value - first
+
+
+def split(value):
+    high = value.astype(BF16)
+    return high, (value - high.astype(F32)).astype(BF16)
+
+
+def pair_scratch(pieces):
+    return (
+        [pltpu.VMEM((SLOTS, SLOTS), F32)] * TOGETHER
+        + [pltpu.VMEM((8 * pieces, pieces * SLOTS), BF16)] * TOGETHER
+        + [pltpu.VMEM((pieces * SLOTS, SLOTS), BF16)] * TOGETHER
+    )
+
+
+def add_sums(total_ref, line_ref, value_ref, target):
+    total_ref[target] += lax.dot_general(
+        line_ref[...], value_ref[...], NN, preferred_element_type=F32
+    )
+
+
+def near_pairs(begin, amount, scaled_ref, total_ref, refs, pair):
+    squares, lines, values = (refs[i : i + TOGETHER] for i in range(0, 3 * TOGETHER, TOGETHER))
+
+    def first_half(place, part):
+        owner, _, block, shift = pair(place)
+        row, seat, basis = far_basis(block, shift)
+        squares[part][...] = lax.dot_general(
+            far_stack(basis).astype(BF16), scaled_ref[owner], TN, preferred_element_type=F32
+        )
+        swirl = jnp.sum(seat[0:3] * block[4:7], axis=0, keepdims=True)
+        side = jnp.where(
+            row < 3, seat, jnp.where(row == 3, 1.0, jnp.where(row == 7, swirl, block))
+        )
+        first, second = halves(side * block[3:4])
+        none = jnp.zeros((8, SLOTS), F32)
+        lines[part][...] = jnp.concatenate(
+            [
+                jnp.concatenate([first, second, none, none], axis=0),
+                jnp.concatenate([first, none, none, none], axis=0),
+                jnp.concatenate([none, none, first, second], axis=0),
+                jnp.concatenate([none, none, first, none], axis=0),
+            ],
+            axis=1,
+        ).astype(BF16)
+
+    def second_half(place, part):
+        target = pair(place)[1]
+        for start in range(0, SLOTS, STRIP):
+            value, slope = kernel_and_slope(squares[part][start : start + STRIP, :])
+            for piece, item in enumerate(split(slope) + split(value)):
+                values[part][piece * SLOTS + start : piece * SLOTS + start + STRIP, :] = item
+        add_sums(total_ref, lines[part], values[part], target)
+
+    together(begin, amount, first_half, second_half)
+
+
+def far_pairs(begin, amount, table_ref, total_ref, refs, pair):
+    squares, lines, values = (refs[i : i + TOGETHER] for i in range(0, 3 * TOGETHER, TOGETHER))
+
+    def first_half(place, part):
+        owner, _, block, shift, factor = pair(place)
+        row, seat, basis = far_basis(block, shift)
+        reach = block[7:8]
+        inverse = 1.0 / (reach * reach)
+        squares[part][...] = lax.dot_general(
+            far_stack(basis * inverse).astype(BF16),
+            table_ref[owner],
+            TN,
+            preferred_element_type=F32,
+        )
+        side = jnp.where(row < 3, seat, jnp.where(row == 3, 1.0, 0.0))
+        first, second = halves(
+            side * (block[3:4] * factor * (6.0 * NORM) * inverse * inverse / reach)
+        )
+        none = jnp.zeros((8, SLOTS), F32)
+        lines[part][...] = jnp.concatenate(
+            [
+                jnp.concatenate([first, second], axis=0),
+                jnp.concatenate([first, none], axis=0),
+            ],
+            axis=1,
+        ).astype(BF16)
+
+    def second_half(place, part):
+        target = pair(place)[1]
+        for start in range(0, SLOTS, STRIP):
+            slope = slope_sixth(squares[part][start : start + STRIP, :])
+            for piece, item in enumerate(split(slope)):
+                values[part][piece * SLOTS + start : piece * SLOTS + start + STRIP, :] = item
+        add_sums(total_ref, lines[part], values[part], target)
+
+    together(begin, amount, first_half, second_half)
+
+
+def near_self_kernel(own_ref, scaled_ref, table_ref, total_ref, *refs):
     own_tables(own_ref, scaled_ref, table_ref)
     total_ref[...] = jnp.zeros_like(total_ref)
-    density_pairs(
-        CELLS,
-        scaled_ref,
-        total_ref,
-        square_refs,
-        lambda cell: (cell, cell, own_ref[cell], NO_SHIFT),
+    near_pairs(
+        0, CELLS, scaled_ref, total_ref, refs, lambda cell: (cell, cell, own_ref[cell], NO_SHIFT)
     )
 
-    def some_cells(step, carry):
-        for part in range(4):
-            cell = step * 4 + part
-            sum_ref[pl.ds(cell, 1), :] = summed(total_ref, cell)
-        return carry
-
-    lax.fori_loop(0, CELLS // 4, some_cells, 0)
-
-
-def density_cross_kernel(
-    which, finish, count_ref, info_ref, shift_ref, scaled_ref, own_ref, far_ref, *refs
+
+def near_early_kernel(
+    info_ref, shift_ref, scaled_ref, far_ref, before_ref, total_ref, list_ref, *refs
 ):
-    if finish:
-        heat_ref, before_ref, density_ref, factor_ref = refs[:4]
-    else:
-        before_ref, sum_ref = refs[:2]
-    total_ref, list_ref, *square_refs = refs[-2 - TOGETHER :]
-    amount = listed(which, info_ref, list_ref)
-    total_ref[...] = jnp.zeros_like(total_ref)
+    amount = jnp.minimum(listed(0, info_ref, list_ref), EARLY)
+    total_ref[...] = before_ref[...]
 
     def pair(place):
         owner, target, source, shift = pair_at(list_ref, info_ref, shift_ref, place)
         return owner, target, far_ref[source], shift
 
-    density_pairs(amount, scaled_ref, total_ref, square_refs, pair)
+    near_pairs(0, amount, scaled_ref, total_ref, refs, pair)
+
+
+def near_late_kernel(
+    count_ref,
+    info_ref,
+    shift_ref,
+    scaled_ref,
+    far_a_ref,
+    far_b_ref,
+    before_ref,
+    own_ref,
+    heat_ref,
+    total_ref,
+    density_ref,
+    factor_ref,
+    list_ref,
+    *refs,
+):
+    total_ref[...] = before_ref[...]
+    for which, far_ref in enumerate((far_a_ref, far_b_ref)):
+        amount = listed(which, info_ref, list_ref)
+
+        def pair(place, far_ref=far_ref):
+            owner, target, source, shift = pair_at(list_ref, info_ref, shift_ref, place)
+            return owner, target, far_ref[source], shift
+
+        near_pairs((EARLY, 0)[which], amount, scaled_ref, total_ref, refs, pair)
     lane = lax.broadcasted_iota(jnp.int32, (1, SLOTS), 1)
 
     def some_cells(step, carry):
         for part in range(4):
             cell = step * 4 + part
             line = pl.ds(cell, 1)
-            raw = summed(total_ref, cell) + before_ref[line, :]
-            if not finish:
-                sum_ref[line, :] = raw
-                continue
+            raw = total_ref[cell, 19:20, :] + total_ref[cell, 27:28, :]
             reach = own_ref[cell, 7:8, :]
             raw = raw * (2.0 * NORM) / (reach * reach * reach)
             density = jnp.where(lane < count_ref[cell], raw, 1.0)
@@ -239,91 +315,16 @@
     lax.fori_loop(0, CELLS // 4, some_cells, 0)
 
 
-def force_first(table_ref, square_ref, column_ref, line_ref, owner, block, factor, shift):
-    row, place, basis = far_basis(block, shift)
-    square_ref[...] = lax.dot_general(
-        far_stack(basis).astype(BF16), table_ref[owner], TN, preferred_element_type=F32
-    )
-    reach = block[7:8]
-    weight = block[3:4]
-    inverse = 1.0 / (reach * reach)
-    column_ref[...] = jnp.broadcast_to(jnp.broadcast_to(inverse, (8, SLOTS)).T[:, 0:1], (SLOTS, 128))
-    swirl = jnp.sum(place[0:3] * block[4:7], axis=0, keepdims=True)
-    own_side = jnp.where(
-        row < 3, place, jnp.where(row == 3, 1.0, jnp.where(row == 7, swirl, block))
-    )
-    own_side = own_side * weight
-    far_side = jnp.where(row < 3, place, jnp.where(row == 3, 1.0, 0.0))
-    far_side = far_side * (weight * factor * (6.0 * NORM) * inverse * inverse / reach)
-    own_first = rounded(own_side)
-    own_second = own_side - own_first
-    far_first = rounded(far_side)
-    far_second = far_side - far_first
-    none = jnp.zeros((8, SLOTS), F32)
-    line_ref[...] = jnp.concatenate(
-        [
-            jnp.concatenate([own_first, own_second, none, none], axis=0),
-            jnp.concatenate([own_first, none, none, none], axis=0),
-            jnp.concatenate([none, none, far_first, far_second], axis=0),
-            jnp.concatenate([none, none, far_first, none], axis=0),
-        ],
-        axis=1,
-    ).astype(BF16)
-
-
-def split(slope):
-    high = slope.astype(BF16)
-    return high, (slope - high.astype(F32)).astype(BF16)
-
-
-def force_second(total_ref, square_ref, column_ref, line_ref, slope_ref, target, inverse):
-    for start in range(0, SLOTS, STRIP):
-        rows = slice(start, start + STRIP)
-        square = jnp.maximum(square_ref[rows, :], TINY)
-        far_inverse = column_ref[rows, :]
-        far_inverse = jnp.concatenate([far_inverse, far_inverse], axis=1)
-        own_high, own_low = split(slope_sixth(square * inverse))
-        far_high, far_low = split(slope_sixth(square * far_inverse))
-        for part, piece in enumerate((own_high, own_low, far_high, far_low)):
-            slope_ref[part * SLOTS + start : part * SLOTS + start + STRIP, :] = piece
-    total_ref[target] += lax.dot_general(
-        line_ref[...], slope_ref[...], NN, preferred_element_type=F32
-    )
-
-
-def force_scratch():
-    return (
-        [pltpu.VMEM((SLOTS, SLOTS), F32)] * TOGETHER
-        + [pltpu.VMEM((SLOTS, 128), F32)] * TOGETHER
-        + [pltpu.VMEM((32, 4 * SLOTS), BF16)] * TOGETHER
-        + [pltpu.VMEM((4 * SLOTS, SLOTS), BF16)] * TOGETHER
-    )
-
-
-def force_pairs(amount, table_ref, own_ref, total_ref, refs, pair):
-    def first_half(place, part):
-        owner, _, block, factor, shift = pair(place)
-        force_first(
-            table_ref, *refs[part : 3 * TOGETHER : TOGETHER], owner, block, factor, shift
-        )
-
-    def second_half(place, part):
-        owner, target, _, _, _ = pair(place)
-        force_second(total_ref, *refs[part::TOGETHER], target, own_inverse(own_ref, owner))
-
-    together(amount, first_half, second_half)
-
-
-def force_self_kernel(own_ref, factor_ref, table_ref, total_ref, *refs):
+def far_self_kernel(own_ref, factor_ref, table_ref, total_ref, *refs):
     total_ref[...] = jnp.zeros_like(total_ref)
 
     def pair(cell):
-        return cell, cell, own_ref[cell], factor_ref[pl.ds(cell, 1), :], NO_SHIFT
-
-    force_pairs(CELLS, table_ref, own_ref, total_ref, refs, pair)
-
-
-def force_cross_kernel(
+        return cell, cell, own_ref[cell], NO_SHIFT, factor_ref[pl.ds(cell, 1), :]
+
+    far_pairs(0, CELLS, table_ref, total_ref, refs, pair)
+
+
+def far_cross_kernel(
     count_ref,
     info_ref,
     shift_ref,
@@ -333,6 +334,7 @@
     far_b_ref,
     far_factor_ref,
     factor_ref,
+    near_ref,
     before_ref,
     push_ref,
     total_ref,
@@ -346,18 +348,17 @@
         def pair(place, far_ref=far_ref):
             owner, target, source, shift = pair_at(list_ref, info_ref, shift_ref, place)
             line = info_ref[3, jnp.minimum(list_ref[place], info_ref.shape[1] - 1)]
-            return owner, target, far_ref[source], far_factor_ref[pl.ds(line, 1), :], shift
-
-        force_pairs(amount, table_ref, own_ref, total_ref, refs, pair)
+            return owner, target, far_ref[source], shift, far_factor_ref[pl.ds(line, 1), :]
+
+        far_pairs(0, amount, table_ref, total_ref, refs, pair)
 
     lane = lax.broadcasted_iota(jnp.int32, (1, SLOTS), 1)
 
     def some_cells(step, carry):
         for part in range(4):
             cell = step * 4 + part
-            sums = total_ref[cell]
-            own = sums[0:8] + sums[8:16]
-            far = sums[16:24] + sums[24:32]
+            own = -(near_ref[cell, 0:8, :] + near_ref[cell, 8:16, :])
+            far = total_ref[cell, 0:8, :] + total_ref[cell, 8:16, :]
             block = own_ref[cell]
             _, place = place_rows(block, NO_SHIFT)
             reach = block[7:8]
@@ -611,45 +612,35 @@
         name="sort_masses",
     )(mesh_owner.reshape(lines, 256), mesh_cell.reshape(lines, 256), mass.reshape(lines, 256))
 
-    many = jax.ShapeDtypeStruct((CELLS + 1, 32, SLOTS), F32)
+    near_sums = jax.ShapeDtypeStruct((CELLS + 1, 32, SLOTS), F32)
+    far_sums = jax.ShapeDtypeStruct((CELLS + 1, 16, SLOTS), F32)
+    features = jax.ShapeDtypeStruct((CELLS, 48, SLOTS), BF16)
     each = jax.ShapeDtypeStruct((CELLS, SLOTS), F32)
-    wide_total = [pltpu.VMEM((CELLS + 1, SLOTS, 128), F32)]
     places = [pltpu.SMEM((256,), jnp.int32)]
-    scaled, table, partial = pl.pallas_call(
-        density_self_kernel,
-        out_shape=[
-            jax.ShapeDtypeStruct((CELLS, SLOTS, 128), BF16),
-            jax.ShapeDtypeStruct((CELLS, 48, SLOTS), BF16),
-            each,
-        ],
+    scaled, table, near = pl.pallas_call(
+        near_self_kernel,
+        out_shape=[features, features, near_sums],
         in_specs=[VMEM],
         out_specs=[VMEM] * 3,
-        scratch_shapes=wide_total + density_scratch(),
-        compiler_params=params(40),
+        scratch_shapes=pair_scratch(4),
+        compiler_params=params(48),
         cost_estimate=cost(8e9, 1e6),
-        name="density_self",
+        name="near_self",
     )(own)
 
-    swapped = swap(after(jnp.stack([mass_sent, cell_sent], axis=1), far_a, partial), None)
+    swapped = swap(after(jnp.stack([mass_sent, cell_sent], axis=1), far_a, near), None)
     far_b = swap(after(sent_b, swapped), groups_b)
 
-    def density_cross(which, far, partial, finish):
-        extra = (heat, partial) if finish else (partial,)
-        out_shape = [each, each] if finish else [each]
-        return pl.pallas_call(
-            functools.partial(density_cross_kernel, which, finish),
-            out_shape=out_shape,
-            in_specs=[SMEM] * 3 + [VMEM] * (3 + len(extra)),
-            out_specs=[VMEM] * len(out_shape),
-            scratch_shapes=wide_total + places + density_scratch(),
-            compiler_params=params(40),
-            cost_estimate=cost(1e10, 1e6),
-            name="density_cross",
-        )(cell_counts, info, shift, scaled, own, far, *extra)
-
-    (partial_a,) = density_cross(0, far_a, partial, False)
-    density, factor = density_cross(1, far_b, partial_a, True)
-
+    near = pl.pallas_call(
+        near_early_kernel,
+        out_shape=near_sums,
+        in_specs=[SMEM] * 2 + [VMEM] * 3,
+        out_specs=VMEM,
+        scratch_shapes=places + pair_scratch(4),
+        compiler_params=params(48),
+        cost_estimate=cost(1.5e10, 1e6),
+        name="near_early",
+    )(info, shift, scaled, far_a, near)
     z_forward, y_forward, x_forward, x_back, y_back, z_back = wave_tables()
     wide = jax.ShapeDtypeStruct((devices * 16, M // 2), F32)
     half_way = pl.pallas_call(
@@ -662,31 +653,40 @@
         cost_estimate=cost(1.5e10, 1e6),
         name="deposit",
     )(swapped[:, 0], swapped[:, 1], z_forward, y_forward)
-    half_way = swap(after(half_way.reshape(devices, 16, M // 2), far_b, partial_a), None)
+    half_way = swap(after(half_way.reshape(devices, 16, M // 2), far_b, near), None)
+    near, density, factor = pl.pallas_call(
+        near_late_kernel,
+        out_shape=[near_sums, each, each],
+        in_specs=[SMEM] * 3 + [VMEM] * 6,
+        out_specs=[VMEM] * 3,
+        scratch_shapes=places + pair_scratch(4),
+        compiler_params=params(48),
+        cost_estimate=cost(1.5e10, 1e6),
+        name="near_late",
+    )(cell_counts, info, shift, scaled, far_a, far_b, near, own, heat)
     to_all = wanted(jnp.arange(devices, dtype=jnp.int32))
     far_factor = swap(after(pick(factor, to_all), half_way), None)
 
-    total = pl.pallas_call(
-        force_self_kernel,
-        out_shape=many,
+    far_total = pl.pallas_call(
+        far_self_kernel,
+        out_shape=far_sums,
         in_specs=[VMEM] * 3,
         out_specs=VMEM,
-        scratch_shapes=force_scratch(),
-        compiler_params=params(40),
-        cost_estimate=cost(1.5e10, 1e6),
-        name="force_self",
+        scratch_shapes=pair_scratch(2),
+        compiler_params=params(48),
+        cost_estimate=cost(8e9, 1e6),
+        name="far_self",
     )(own, factor, table)
-
     push = pl.pallas_call(
-        force_cross_kernel,
+        far_cross_kernel,
         out_shape=jax.ShapeDtypeStruct((4, CELLS, SLOTS), F32),
-        in_specs=[SMEM] * 3 + [VMEM] * 7,
+        in_specs=[SMEM] * 3 + [VMEM] * 8,
         out_specs=VMEM,
-        scratch_shapes=[pltpu.VMEM(many.shape, F32)] + places + force_scratch(),
+        scratch_shapes=[pltpu.VMEM(far_sums.shape, F32)] + places + pair_scratch(2),
         compiler_params=params(48),
-        cost_estimate=cost(6e10, 1e6),
-        name="force_cross",
-    )(cell_counts, info, shift, table, own, far_a, far_b, far_factor, factor, total)
+        cost_estimate=cost(3e10, 1e6),
+        name="far_cross",
+    )(cell_counts, info, shift, table, own, far_a, far_b, far_factor, factor, near, far_total)
     acceleration = push[0:3].reshape(3, -1)
     heating = push[3].reshape(-1)
 
@@ -699,7 +699,7 @@
         cost_estimate=cost(5e9, 1e6),
         name="filter",
     )((2 * me).reshape(1), half_way.reshape(devices * 16, M // 2), x_forward, x_back)
-    back = swap(after(back.reshape(devices, 16, M // 2), far_factor), None)
+    back = swap(after(back.reshape(devices, 16, M // 2), far_factor, far_total), None)
     potential = pl.pallas_call(
         potential_kernel,
         out_shape=jax.ShapeDtypeStruct((2, M, M), F32),

time: 239 us -> 228 us (0.954)
  starting transfers between devices: 55.9 us -> 44.1 us
  Pallas kernels: 130 us -> 123 us
  local copies, waits for them, and re-layouts: 30.1 us -> 34.3 us
  waiting for transfers between devices: 16.3 us -> 19.8 us
    all_to_all x6, starting transfers between devices: 55.9 us -> 44.1 us  [swap(): lax.all_to_all(data, 'cells', 0, 0, axis_index_groups=groups, tiled=True)]
    pallas_call x5, Pallas kernels: 95 us -> 88.1 us  [the longest x1 28.4 us: per_device(): pl.pallas_call(far_cross_kernel, out_shape=jax.ShapeDtypeStruct((4, CELLS...]
    unnamed x48 -> x60, local copies, waits for them, and re-layouts: 16 us -> 20.1 us
    all_to_all x6, waiting for transfers between devices: 16.3 us -> 19.8 us  [swap(): lax.all_to_all(data, 'cells', 0, 0, axis_index_groups=groups, tiled=True)]
  transfers between devices with their start and end apart: 6 -> 6, of which waited for: 2 -> 3; matrix products, arithmetic and copies ran while one was open for 6% -> 7% of each run, Pallas kernels for 52% -> 52%
where the time goes in v3:
time: 228 us; the launch traced here: 227 us
  Pallas kernels  123 us (54%)
  starting transfers between devices  44.1 us (19%)
  local copies, waits for them, and re-layouts  34.3 us (15%)
  waiting for transfers between devices  19.8 us (9%)
  other arithmetic  4.67 us (2%)
    all_to_all x6, starting transfers between devices, swap(): lax.all_to_all(data, 'cells', 0, 0, axis_index_groups=groups, tiled=True)  44.1 us
    pallas_call x1, Pallas kernels, per_device(): pl.pallas_call(far_cross_kernel, out_shape=jax.ShapeDtypeStruct((4, CELLS...  28.4 us
    pallas_call x1, Pallas kernels, per_device(): pl.pallas_call(near_late_kernel, out_shape=[near_sums, each, each], in_sp...  24.8 us
    pallas_call x1, Pallas kernels, per_device(): pl.pallas_call(near_early_kernel, out_shape=near_sums, in_specs=[SMEM] *...  20.1 us
    unnamed x60, local copies, waits for them, and re-layouts  20.1 us
    all_to_all x6, waiting for transfers between devices, swap(): lax.all_to_all(data, 'cells', 0, 0, axis_index_groups=groups, tiled=True)  19.8 us
    pallas_call x1, Pallas kernels, per_device(): pl.pallas_call(deposit_kernel, out_shape=wide, in_specs=[VMEM] * 4, out_s...  15.3 us
    pallas_call x1, Pallas kernels, per_device(): pl.pallas_call(near_self_kernel, out_shape=[features, features, near_sums...  9.46 us
  transfers between devices with their start and end apart: 6, of which 3 were waited for; matrix products, arithmetic and copies ran while one was open for 7% of the time, Pallas kernels for 52%

profile of v3, /device:TPU:1, one launch (start us, length us, event | category | flops | bytes accessed | tf_op | source)
XLA Modules:
  0.0 227.1 jit_solution(3119022241680992861)
XLA Ops:
  3.1 1.1 maximum_bitcast_fusion.own_ref
  4.2 2.4 %gather_fusion = f32[256,8,256]{2,1,0:T(8,128)} fusion(f32[32,8,256]{2,1,0:T(8,128)S(1)} %maximum_bitcast_fusion.own_ref, s32[1024]{0:T(1024)S(1)} %pad_clamp_fusion.3), kind=kCustom, calls=%fused_computation.2 | custom fusion | bytes 4195328 | tf_op jit(solution)/shard_map/jit(_take)/gather | solution.py:583
  6.6 8.7 %all-to-all-start = ((f32[256,8,256]{2,1,0:T(8,128)}), f32[256,8,256]{2,1,0:T(8,128)S(1)}, u32[]{:S(2)}, u32[]{:S(2)}) async-start(f32[256,8,256]{2,1,0:T(8,128)} %gather_fusion), calls=%async_computation | async-start | bytes 4194304 | tf_op jit(solution)/shard_map/all_to_all | solution.py:580
  17.3 7.0 %sort_masses.1 = (f32[128,128]{1,0:T(8,128)S(1)}, f32[128,128]{1,0:T(8,128)S(1)}) custom-call(s32[32,256]{1,0:T(8,128)S(1)} %reshape.212.owner_ref, s32[32,256]{1,0:T(8,128)S(1)} %reshape.213.cell_ref, f32[32,256]{1,0:T(8,128)S(1)} %fusion.1.mass_ref), custom_call_target="tpu_custom_call" | custom-call | flops 1000000000 | bytes 100000 | tf_op jit(solution)/shard_map/sort_masses/pallas_call | solution.py:604
  24.4 9.5 %near_self.1 = (bf16[32,48,256]{2,1,0:T(8,128)(2,1)S(1)}, bf16[32,48,256]{2,1,0:T(8,128)(2,1)S(1)}, f32[33,32,256]{2,1,0:T(8,128)S(1)}) custom-call(f32[32,8,256]{2,1,0:T(8,128)S(1)} %maximum_bitcast_fusion.own_ref), custom_call_target="tpu_custom_call" | custom-call | flops 1333333376 | bytes 100000 | tf_op jit(solution)/shard_map/near_self/pallas_call | solution.py:620
  35.7 7.5 %all-to-all-done.far_ref.far_a_ref = f32[256,8,256]{2,1,0:T(8,128)S(1)} async-done(((f32[256,8,256]{2,1,0:T(8,128)}), f32[256,8,256]{2,1,0:T(8,128)S(1)}, u32[]{:S(2)}, u32[]{:S(2)}) %all-to-all-start) | async-done | bytes 2097184 | tf_op jit(solution)/shard_map/all_to_all | solution.py:580
  44.0 8.1 %all-to-all-start.1 = ((f32[128,2,128]{2,1,0:T(2,128)}), f32[128,2,128]{2,1,0:T(2,128)S(1)}, u32[]{:S(2)}, u32[]{:S(2)}) async-start(f32[128,2,128]{2,1,0:T(2,128)} %copy.23), calls=%async_computation.1 | async-start | bytes 262144 | tf_op jit(solution)/shard_map/all_to_all | solution.py:580
  52.2 2.3 %gather_fusion.1 = f32[256,8,256]{2,1,0:T(8,128)} fusion(f32[32,8,256]{2,1,0:T(8,128)S(1)} %maximum_bitcast_fusion.own_ref, s32[1024]{0:T(1024)S(1)} %pad_clamp_fusion.1), kind=kCustom, calls=%fused_computation.3 | custom fusion | bytes 4195328 | tf_op jit(solution)/shard_map/jit(_take)/gather | solution.py:583
  54.6 7.5 %all-to-all-done.1 = f32[128,2,128]{2,1,0:T(2,128)S(1)} async-done(((f32[128,2,128]{2,1,0:T(2,128)}), f32[128,2,128]{2,1,0:T(2,128)S(1)}, u32[]{:S(2)}, u32[]{:S(2)}) %all-to-all-start.1) | async-done | bytes 131104 | tf_op jit(solution)/shard_map/all_to_all | solution.py:580
  62.1 7.9 %all-to-all-start.2 = ((f32[256,8,256]{2,1,0:T(8,128)}), f32[256,8,256]{2,1,0:T(8,128)}, u32[]{:S(2)}, u32[]{:S(2)}) async-start(f32[256,8,256]{2,1,0:T(8,128)} %gather_fusion.1), calls=%async_computation.2 | async-start | bytes 4194304 | tf_op jit(solution)/shard_map/all_to_all | solution.py:580
  70.1 1.1 copy-done.13
  71.2 1.2 copy-done.19
  72.5 20.1 %near_early.1.before_ref = f32[33,32,256]{2,1,0:T(8,128)S(1)} custom-call(s32[4,128]{1,0:T(4,128)S(1)} %pad_add_fusion.info_ref, f32[3,128]{1,0:T(4,128)S(1)} %add_convert_fusion.shift_ref, bf16[32,48,256]{2,1,0:T(8,128)(2,1)S(1)} %copy-done.13, f32[256,8,256]{2,1,0:T(8,128)S(1)} %all-to-all-done.far_ref.far_a_ref, f32[33,32,256]{2,1,0:T(8,128)S(1)} %copy-done.19), custom_call_target="tpu_custom_call" | custom-call | flops 2500000000 | bytes 100000 | tf_op jit(solution)/shard_map/near_early/pallas_call | solution.py:634
  93.7 15.3 %deposit.1 = f32[2048,128]{1,0:T(8,128)S(1)} custom-call(f32[128,128]{1,0:T(8,128)S(1)} %bitcast.39, f32[128,128]{1,0:T(8,128)S(1)} %bitcast.38, f32[256,512]{1,0:T(8,128)S(1)} %copy-done.7, f32[512,512]{1,0:T(8,128)S(1)} %copy-done.6), custom_call_target="tpu_custom_call" | custom-call | flops 2500000000 | bytes 100000 | tf_op jit(solution)/shard_map/deposit/pallas_call | solution.py:646
  110.0 4.2 %all-to-all-start.3 = ((f32[128,16,128]{2,1,0:T(8,128)}), f32[128,16,128]{2,1,0:T(8,128)S(1)}, u32[]{:S(2)}, u32[]{:S(2)}) async-start(f32[128,16,128]{2,1,0:T(8,128)} %bitcast.35), calls=%async_computation.3 | async-start | bytes 2097152 | tf_op jit(solution)/shard_map/all_to_all | solution.py:580
  114.3 1.2 gather_fusion.2
  115.5 1.6 select_maximum_fusion
  118.0 1.2 copy-done.11
  119.3 1.1 copy-done.14
  120.4 24.8 %near_late.1 = (f32[33,32,256]{2,1,0:T(8,128)S(1)}, f32[32,256]{1,0:T(8,128)S(1)}, f32[32,256]{1,0:T(8,128)S(1)}) custom-call(s32[32]{0:T(128)S(1)} %copy-done.5, s32[4,128]{1,0:T(4,128)S(1)} %pad_add_fusion.info_ref, f32[3,128]{1,0:T(4,128)S(1)} %add_convert_fusion.shift_ref, bf16[32,48,256]{2,1,0:T(8,128)(2,1)S(1)} %copy-done.14, ...), custom_call_target="tpu_custom_call" | custom-call | flops 2500000000 | bytes 100000 | tf_op jit(solution)/shard_map/near_late/pallas_call | solution.py:657
  146.2 4.6 %gather_fusion.3 = f32[1024,256]{1,0:T(8,128)} fusion(f32[32,256]{1,0:T(8,128)S(1)} %get-tuple-element.32.factor_ref, s32[1024]{0:T(1024)S(1)} %broadcast_clamp_fusion), kind=kCustom, calls=%fused_computation.5 | custom fusion | bytes 2101248 | tf_op jit(solution)/shard_map/jit(_take)/gather | solution.py:583
  150.8 10.2 %all-to-all-start.4 = ((f32[128,8,256]{2,1,0:T(8,128)}), f32[128,8,256]{2,1,0:T(8,128)}, u32[]{:S(2)}, u32[]{:S(2)}) async-start(f32[128,8,256]{2,1,0:T(8,128)} %bitcast.44), calls=%async_computation.4 | async-start | bytes 2097152 | tf_op jit(solution)/shard_map/all_to_all | solution.py:580
  161.1 1.1 copy-done.16
  162.2 5.4 %far_self.1.before_ref = f32[33,16,256]{2,1,0:T(8,128)S(1)} custom-call(f32[32,8,256]{2,1,0:T(8,128)S(1)} %maximum_bitcast_fusion.own_ref, f32[32,256]{1,0:T(8,128)S(1)} %get-tuple-element.32.factor_ref, bf16[32,48,256]{2,1,0:T(8,128)(2,1)S(1)} %copy-done.16), custom_call_target="tpu_custom_call" | custom-call | flops 1333333376 | bytes 100000 | tf_op jit(solution)/shard_map/far_self/pallas_call | solution.py:670
  168.5 6.7 %filter.1 = f32[2048,128]{1,0:T(8,128)} custom-call(s32[1]{0:T(128)} %bitcast.14.first_ref, f32[2048,128]{1,0:T(8,128)S(1)} %bitcast.33, f32[512,512]{1,0:T(8,128)S(1)} %copy-done.1, f32[512,512]{1,0:T(8,128)S(1)} %copy-done.2), custom_call_target="tpu_custom_call" | custom-call | flops 833333312 | bytes 100000 | tf_op jit(solution)/shard_map/filter/pallas_call | solution.py:693
  175.2 4.8 %all-to-all-done.4 = f32[128,8,256]{2,1,0:T(8,128)} async-done(((f32[128,8,256]{2,1,0:T(8,128)}), f32[128,8,256]{2,1,0:T(8,128)}, u32[]{:S(2)}, u32[]{:S(2)}) %all-to-all-start.4) | async-done | bytes 1048608 | tf_op jit(solution)/shard_map/all_to_all | solution.py:580
  180.1 4.9 %all-to-all-start.5 = ((f32[128,16,128]{2,1,0:T(8,128)}), f32[128,16,128]{2,1,0:T(8,128)S(1)}, u32[]{:S(2)}, u32[]{:S(2)}) async-start(f32[128,16,128]{2,1,0:T(8,128)} %bitcast.16), calls=%async_computation.5 | async-start | bytes 2097152 | tf_op jit(solution)/shard_map/all_to_all | solution.py:580
  185.6 1.2 copy-done.9
  186.9 1.1 copy-done.17
  189.1 28.4 %far_cross.1 = f32[4,32,256]{2,1,0:T(8,128)S(1)} custom-call(s32[32]{0:T(128)S(1)} %copy-done.5, s32[4,128]{1,0:T(4,128)S(1)} %pad_add_fusion.info_ref, f32[3,128]{1,0:T(4,128)S(1)} %add_convert_fusion.shift_ref, bf16[32,48,256]{2,1,0:T(8,128)(2,1)S(1)} %copy-done.17, f32[32,8,256]{2,1,0:T(8,128)S(1)} %maximum_bitcast_fusion.own_ref, ...), custom_call_target="tpu_custom_call" | custom-call | flops 5000000000 | bytes 100000 | tf_op jit(solution)/shard_map/far_cross/pallas_call | solution.py:680
  218.8 1.2 copy-done
  221.1 6.1 %potential.1 = f32[2,256,256]{2,1,0:T(8,128)} custom-call(f32[2048,128]{1,0:T(8,128)S(1)} %bitcast.34, f32[512,512]{1,0:T(8,128)S(1)} %copy-done, f32[512,256]{1,0:T(8,128)S(1)} %copy-done.4), custom_call_target="tpu_custom_call" | custom-call | flops 666666688 | bytes 100000 | tf_op jit(solution)/shard_map/potential/pallas_call | solution.py:703
  (87 shorter events, 16.3 us)
Async XLA Ops:
  6.6 8.8 %copy-start.22 = (f32[8192]{0:T(1024)S(1)}, f32[8192]{0:T(1024)}, u32[]{:S(2)}) copy-start(f32[8192]{0:T(1024)} %param.20) | copy-start | bytes 98308
  6.6 9.4 %copy-start.5 = (s32[32]{0:T(128)S(1)}, s32[32]{0:T(128)}, u32[]{:S(2)}) copy-start(s32[32]{0:T(128)} %count_ref.3) | copy-start | bytes 388
  6.6 10.0 %copy-start.23 = (s32[8192,1]{0,1:T(1,128)S(1)}, s32[8192,1]{0,1:T(1,128)}, u32[]{:S(2)}) copy-start(s32[8192,1]{0,1:T(1,128)} %param.26) | copy-start | bytes 98308
  6.6 10.7 %copy-start.24 = (s32[8192]{0:T(1024)S(1)}, s32[8192]{0:T(1024)}, u32[]{:S(2)}) copy-start(s32[8192]{0:T(1024)} %param.27) | copy-start | bytes 98308
  6.6 36.6 %all-to-all-start = ((f32[256,8,256]{2,1,0:T(8,128)}), f32[256,8,256]{2,1,0:T(8,128)S(1)}, u32[]{:S(2)}, u32[]{:S(2)}) async-start(f32[256,8,256]{2,1,0:T(8,128)} %gather_fusion), calls=%async_computation | async-start | bytes 4194304 | tf_op jit(solution)/shard_map/all_to_all | solution.py:580
  33.8 0.9 copy-start.12
  34.7 1.0 copy-start.18
  35.7 18.9 %copy-start.15 = (bf16[32,48,256]{2,1,0:T(8,128)(2,1)}, bf16[32,48,256]{2,1,0:T(8,128)(2,1)S(1)}, u32[]{:S(2)}) copy-start(bf16[32,48,256]{2,1,0:T(8,128)(2,1)S(1)} %get-tuple-element.31.table_ref) | copy-start | bytes 2359300
  44.0 18.1 %all-to-all-start.1 = ((f32[128,2,128]{2,1,0:T(2,128)}), f32[128,2,128]{2,1,0:T(2,128)S(1)}, u32[]{:S(2)}, u32[]{:S(2)}) async-start(f32[128,2,128]{2,1,0:T(2,128)} %copy.23), calls=%async_computation.1 | async-start | bytes 262144 | tf_op jit(solution)/shard_map/all_to_all | solution.py:580
  54.6 15.4 %copy-start.26 = (s32[4,128]{1,0:T(4,128)S(1)}, s32[4,128]{1,0:T(4,128)}, u32[]{:S(2)}) copy-start(s32[4,128]{1,0:T(4,128)} %param.24) | copy-start | bytes 6148
  62.1 47.9 %all-to-all-start.2 = ((f32[256,8,256]{2,1,0:T(8,128)}), f32[256,8,256]{2,1,0:T(8,128)}, u32[]{:S(2)}, u32[]{:S(2)}) async-start(f32[256,8,256]{2,1,0:T(8,128)} %gather_fusion.1), calls=%async_computation.2 | async-start | bytes 4194304 | tf_op jit(solution)/shard_map/all_to_all | solution.py:580
  70.1 1.1 copy-start.13
  71.2 1.2 copy-start.19
  72.5 21.2 %copy-start.6 = (f32[512,512]{1,0:T(8,128)S(1)}, f32[512,512]{1,0:T(8,128)}, u32[]{:S(2)}) copy-start(f32[512,512]{1,0:T(8,128)} %constant.210.clone.y_ref) | copy-start | bytes 3145732
  72.5 21.2 %copy-start.7 = (f32[256,512]{1,0:T(8,128)S(1)}, f32[256,512]{1,0:T(8,128)}, u32[]{:S(2)}) copy-start(f32[256,512]{1,0:T(8,128)} %constant.209.clone.z_ref) | copy-start | bytes 1572868
  92.5 1.0 copy-start.10
  109.0 1.0 copy-start.3
  110.0 4.2 %copy-start.25 = (f32[8192]{0:T(1024)S(1)}, f32[8192]{0:T(1024)}, u32[]{:S(2)}) copy-start(f32[8192]{0:T(1024)} %param.22) | copy-start | bytes 98308
  110.0 40.8 %all-to-all-start.3 = ((f32[128,16,128]{2,1,0:T(8,128)}), f32[128,16,128]{2,1,0:T(8,128)S(1)}, u32[]{:S(2)}, u32[]{:S(2)}) async-start(f32[128,16,128]{2,1,0:T(8,128)} %bitcast.35), calls=%async_computation.3 | async-start | bytes 2097152 | tf_op jit(solution)/shard_map/all_to_all | solution.py:580
  118.0 1.2 copy-start.11
  119.3 1.1 copy-start.14
  145.2 1.0 copy-start.8
  150.8 29.2 %all-to-all-start.4 = ((f32[128,8,256]{2,1,0:T(8,128)}), f32[128,8,256]{2,1,0:T(8,128)}, u32[]{:S(2)}, u32[]{:S(2)}) async-start(f32[128,8,256]{2,1,0:T(8,128)} %bitcast.44), calls=%async_computation.4 | async-start | bytes 2097152 | tf_op jit(solution)/shard_map/all_to_all | solution.py:580
  161.1 1.1 copy-start.16
  162.2 6.3 %copy-start.1 = (f32[512,512]{1,0:T(8,128)S(1)}, f32[512,512]{1,0:T(8,128)}, u32[]{:S(2)}) copy-start(f32[512,512]{1,0:T(8,128)} %constant.211.clone.forward_ref) | copy-start | bytes 3145732
  162.2 6.3 %copy-start.2 = (f32[512,512]{1,0:T(8,128)S(1)}, f32[512,512]{1,0:T(8,128)}, u32[]{:S(2)}) copy-start(f32[512,512]{1,0:T(8,128)} %constant.212.clone.back_ref) | copy-start | bytes 3145732
  180.1 38.7 %all-to-all-start.5 = ((f32[128,16,128]{2,1,0:T(8,128)}), f32[128,16,128]{2,1,0:T(8,128)S(1)}, u32[]{:S(2)}, u32[]{:S(2)}) async-start(f32[128,16,128]{2,1,0:T(8,128)} %bitcast.16), calls=%async_computation.5 | async-start | bytes 2097152 | tf_op jit(solution)/shard_map/all_to_all | solution.py:580
  185.6 1.2 copy-start.9
  186.9 1.1 copy-start.17
  188.0 1.0 copy-start.21
  218.8 1.2 copy-start
  220.0 1.0 copy-start.4
  (1 other events, 0.8 us)

commit v4 on v3

--- a/solution.py
+++ b/solution.py
@@ -274,6 +274,8 @@
 
 
 def near_late_kernel(
+    me_ref,
+    export_ref,
     count_ref,
     info_ref,
     shift_ref,
@@ -286,9 +288,11 @@
     total_ref,
     density_ref,
     factor_ref,
+    sent_ref,
     list_ref,
     *refs,
 ):
+    sent_ref[...] = jnp.zeros_like(sent_ref)
     total_ref[...] = before_ref[...]
     for which, far_ref in enumerate((far_a_ref, far_b_ref)):
         amount = listed(which, info_ref, list_ref)
@@ -313,6 +317,15 @@
         return carry
 
     lax.fori_loop(0, CELLS // 4, some_cells, 0)
+
+    def one_peer(peer, carry):
+        cells = [jnp.maximum(export_ref[peer, slot], 0) for slot in range(CAP)]
+        sent_ref[receiver(peer, me_ref[0], sent_ref.shape[0])] = jnp.concatenate(
+            [factor_ref[pl.ds(cell, 1), :] for cell in cells], axis=0
+        )
+        return carry
+
+    lax.fori_loop(0, 2 * HALF, one_peer, 0)
 
 
 def far_self_kernel(own_ref, factor_ref, table_ref, total_ref, *refs):
@@ -381,6 +394,63 @@
         return carry
 
     lax.fori_loop(0, CELLS // 4, some_cells, 0)
+
+
+def receiver(peer, me, devices):
+    step = jnp.where(peer < HALF, peer - HALF, peer - HALF + 1)
+    return lax.rem(me - step + devices, devices)
+
+
+def export_kernel(
+    devices,
+    me_ref,
+    export_ref,
+    count_ref,
+    place_ref,
+    speed_ref,
+    mass_ref,
+    reach_ref,
+    own_ref,
+    live_ref,
+    sent_a_ref,
+    sent_b_ref,
+):
+    lane = lax.broadcasted_iota(jnp.int32, (1, SLOTS), 1)
+
+    def some_cells(step, carry):
+        for part in range(4):
+            cell = step * 4 + part
+            line = pl.ds(cell, 1)
+            lanes = pl.ds(pl.multiple_of(cell * SLOTS, SLOTS), SLOTS)
+            mass = jnp.where(lane < count_ref[cell], mass_ref[line, :], 0.0)
+            live_ref[line, :] = mass
+            own_ref[cell] = jnp.concatenate(
+                [place_ref[:, lanes], mass / SLOTS, speed_ref[:, lanes], reach_ref[line, :]], axis=0
+            )
+        return carry
+
+    lax.fori_loop(0, CELLS // 4, some_cells, 0)
+    me = me_ref[0]
+
+    def one_peer(peer, carry):
+        target = receiver(peer, me, devices)
+        same = target // GROUP == me // GROUP
+        seat_a = lax.rem(target, GROUP) * CAP
+        seat_b = lax.rem(target + devices - GROUP // 2, GROUP) * CAP
+
+        @pl.when(same)
+        def _():
+            for slot in range(CAP):
+                sent_a_ref[seat_a + slot] = own_ref[jnp.maximum(export_ref[peer, slot], 0)]
+
+        @pl.when(jnp.logical_not(same))
+        def _():
+            for slot in range(CAP):
+                sent_b_ref[seat_b + slot] = own_ref[jnp.maximum(export_ref[peer, slot], 0)]
+
+        return carry
+
+    lax.fori_loop(0, 2 * HALF, one_peer, 0)
 
 
 def sort_kernel(owner_ref, cell_ref, mass_ref, mass_out, cell_out, parts_ref):
@@ -547,46 +617,41 @@
 ):
     devices = lax.axis_size("cells")
     me = lax.axis_index("cells").astype(jnp.int32)
-    slots_iota = jnp.arange(SLOTS, dtype=jnp.int32)
-    live = (slots_iota[None, :] < cell_counts[:, None]).astype(F32)
     heat = energies.reshape(CELLS, SLOTS)
-    mass = masses.reshape(CELLS, SLOTS) * live
-    own = jnp.concatenate(
-        [
-            positions.reshape(3, CELLS, SLOTS),
-            (mass / SLOTS)[None],
-            velocities.reshape(3, CELLS, SLOTS),
-            smoothing.reshape(1, CELLS, SLOTS),
-        ],
-        axis=0,
-    ).transpose(1, 0, 2)
 
     groups_a = [list(range(g, g + GROUP)) for g in range(0, devices, GROUP)]
     groups_b = [[(i + GROUP // 2) % devices for i in g] for g in groups_a]
-    exports = export_list[0]
-    lane32 = jnp.arange(GROUP, dtype=jnp.int32)
-
-    def wanted(others):
-        step = (me - others + devices // 2) % devices - devices // 2
-        row = jnp.where(step < 0, step + HALF, step + HALF - 1)
-        row = jnp.clip(row, 0, 2 * HALF - 1)
-        return jnp.maximum(jnp.take(exports, row, axis=0), 0).reshape(-1)
-
-    to_a = wanted(me // GROUP * GROUP + lane32)
-    start_b = (me - GROUP // 2) % devices // GROUP * GROUP + GROUP // 2
-    to_b = wanted((start_b + lane32) % devices)
-
     def swap(data, groups):
         return lax.all_to_all(data, "cells", 0, 0, axis_index_groups=groups, tiled=True)
 
-    def pick(data, cells):
-        return jnp.take(data, cells, axis=0, mode="clip")
-
     def after(data, *others):
         return lax.optimization_barrier((data, *others))[0]
 
-    sent_a = pick(own, to_a)
-    sent_b = pick(own, to_b)
+    exports = export_list[0]
+    here = me.reshape(1)
+    sent = jax.ShapeDtypeStruct((GROUP * CAP, 8, SLOTS), F32)
+    own, mass, sent_a, sent_b = pl.pallas_call(
+        functools.partial(export_kernel, devices),
+        out_shape=[
+            jax.ShapeDtypeStruct((CELLS, 8, SLOTS), F32),
+            jax.ShapeDtypeStruct((CELLS, SLOTS), F32),
+            sent,
+            sent,
+        ],
+        in_specs=[SMEM] * 3 + [VMEM] * 4,
+        out_specs=[VMEM] * 4,
+        compiler_params=params(32),
+        cost_estimate=cost(2e9, 5e6),
+        name="exports",
+    )(
+        here,
+        exports,
+        cell_counts,
+        positions,
+        velocities,
+        masses.reshape(CELLS, SLOTS),
+        smoothing.reshape(CELLS, SLOTS),
+    )
     far_a = swap(sent_a, groups_a)
     mesh_owner, mesh_cell, mass = lax.optimization_barrier((mesh_owner, mesh_cell, mass, sent_a))[:3]
 
@@ -654,18 +719,17 @@
         name="deposit",
     )(swapped[:, 0], swapped[:, 1], z_forward, y_forward)
     half_way = swap(after(half_way.reshape(devices, 16, M // 2), far_b, near), None)
-    near, density, factor = pl.pallas_call(
+    near, density, factor, sent_factor = pl.pallas_call(
         near_late_kernel,
-        out_shape=[near_sums, each, each],
-        in_specs=[SMEM] * 3 + [VMEM] * 6,
-        out_specs=[VMEM] * 3,
+        out_shape=[near_sums, each, each, jax.ShapeDtypeStruct((devices, CAP, SLOTS), F32)],
+        in_specs=[SMEM] * 5 + [VMEM] * 6,
+        out_specs=[VMEM] * 4,
         scratch_shapes=places + pair_scratch(4),
         compiler_params=params(48),
         cost_estimate=cost(1.5e10, 1e6),
         name="near_late",
-    )(cell_counts, info, shift, scaled, far_a, far_b, near, own, heat)
-    to_all = wanted(jnp.arange(devices, dtype=jnp.int32))
-    far_factor = swap(after(pick(factor, to_all), half_way), None)
+    )(here, exports, cell_counts, info, shift, scaled, far_a, far_b, near, own, heat)
+    far_factor = swap(after(sent_factor, half_way), None).reshape(devices * CAP, SLOTS)
 
     far_total = pl.pallas_call(
         far_self_kernel,

time: 228 us -> 222 us (0.974)
  blocking collectives: 0 us -> 18 us
  local copies, waits for them, and re-layouts: 34.3 us -> 23.1 us
  starting transfers between devices: 44.1 us -> 35.6 us
  waiting for transfers between devices: 19.8 us -> 14.1 us
  Pallas kernels: 123 us -> 128 us
  other arithmetic: 4.67 us -> 0.81 us
    all_to_all x0 -> x1, blocking collectives: none -> 18 us  [swap(): lax.all_to_all(data, 'cells', 0, 0, axis_index_groups=groups, tiled=True)]
    gather x6 -> x0, local copies, waits for them, and re-layouts: 11.7 us -> none  [the longest x3 9.35 us: pick(): return jnp.take(data, cells, axis=0, mode='clip')]
    all_to_all x6 -> x5, starting transfers between devices: 44.1 us -> 35.6 us  [swap(): lax.all_to_all(data, 'cells', 0, 0, axis_index_groups=groups, tiled=True)]
    all_to_all x6 -> x5, waiting for transfers between devices: 19.8 us -> 14.1 us  [swap(): lax.all_to_all(data, 'cells', 0, 0, axis_index_groups=groups, tiled=True)]
    pallas_call x1 -> x2, Pallas kernels: 24.8 us -> 29.2 us  [the longest x1 27.2 us: per_device(): pl.pallas_call(near_late_kernel, out_shape=[near_sums, each, each, jax.Sh...]
    unnamed x60 -> x70, local copies, waits for them, and re-layouts: 20.1 us -> 20.8 us
  transfers between devices with their start and end apart: 6 -> 5, of which waited for: 3 -> 2; matrix products, arithmetic and copies ran while one was open for 7% -> 2% of each run, Pallas kernels for 52% -> 54%
where the time goes in v4:
time: 222 us; the launch traced here: 221 us
  Pallas kernels  128 us (58%)
  starting transfers between devices  35.6 us (16%)
  local copies, waits for them, and re-layouts  23.1 us (10%)
  blocking collectives  18 us (8%)
  waiting for transfers between devices  14.1 us (6%)
    all_to_all x5, starting transfers between devices, swap(): lax.all_to_all(data, 'cells', 0, 0, axis_index_groups=groups, tiled=True)  35.6 us
    pallas_call x1, Pallas kernels, per_device(): pl.pallas_call(far_cross_kernel, out_shape=jax.ShapeDtypeStruct((4, CELLS...  28.3 us
    pallas_call x1, Pallas kernels, per_device(): pl.pallas_call(near_late_kernel, out_shape=[near_sums, each, each, jax.Sh...  27.2 us
    unnamed x70, local copies, waits for them, and re-layouts  20.8 us
    pallas_call x1, Pallas kernels, per_device(): pl.pallas_call(near_early_kernel, out_shape=near_sums, in_specs=[SMEM] *...  19.9 us
    all_to_all x1, blocking collectives, swap(): lax.all_to_all(data, 'cells', 0, 0, axis_index_groups=groups, tiled=True)  18 us
    pallas_call x1, Pallas kernels, per_device(): pl.pallas_call(deposit_kernel, out_shape=wide, in_specs=[VMEM] * 4, out_s...  16.3 us
    all_to_all x5, waiting for transfers between devices, swap(): lax.all_to_all(data, 'cells', 0, 0, axis_index_groups=groups, tiled=True)  14.1 us
  transfers between devices with their start and end apart: 5, of which 2 were waited for; matrix products, arithmetic and copies ran while one was open for 2% of the time, Pallas kernels for 54%

profile of v4, /device:TPU:1, one launch (start us, length us, event | category | flops | bytes accessed | tf_op | source)
XLA Modules:
  0.0 220.9 jit_solution(12234280113843807702)
XLA Ops:
  3.9 0.9 copy-done.9
  5.4 2.0 exports.1
  7.5 1.4 copy-done.2
  8.8 1.3 copy-done.3
  10.2 8.7 %all-to-all-start = ((f32[256,8,256]{2,1,0:T(8,128)}), f32[256,8,256]{2,1,0:T(8,128)S(1)}, u32[]{:S(2)}, u32[]{:S(2)}) async-start(f32[256,8,256]{2,1,0:T(8,128)} %copy-done.3), calls=%async_computation | async-start | bytes 4194304 | tf_op jit(solution)/shard_map/all_to_all | solution.py:625
  20.2 7.0 %sort_masses.1 = (f32[128,128]{1,0:T(8,128)S(1)}, f32[128,128]{1,0:T(8,128)S(1)}) custom-call(s32[32,256]{1,0:T(8,128)S(1)} %reshape.53.owner_ref, s32[32,256]{1,0:T(8,128)S(1)} %reshape.54.cell_ref, f32[32,256]{1,0:T(8,128)S(1)} %get-tuple-element.32.mass_ref), custom_call_target="tpu_custom_call" | custom-call | flops 1000000000 | bytes 100000 | tf_op jit(solution)/shard_map/sort_masses/pallas_call | solution.py:669
  27.2 9.5 %near_self.1 = (bf16[32,48,256]{2,1,0:T(8,128)(2,1)S(1)}, bf16[32,48,256]{2,1,0:T(8,128)(2,1)S(1)}, f32[33,32,256]{2,1,0:T(8,128)S(1)}) custom-call(f32[32,8,256]{2,1,0:T(8,128)S(1)} %get-tuple-element.25.own_ref), custom_call_target="tpu_custom_call" | custom-call | flops 1333333376 | bytes 100000 | tf_op jit(solution)/shard_map/near_self/pallas_call | solution.py:685
  36.7 0.9 copy-done.18
  37.7 1.0 copy-done.24
  38.7 8.1 %all-to-all-done.far_ref.far_a_ref = f32[256,8,256]{2,1,0:T(8,128)S(1)} async-done(((f32[256,8,256]{2,1,0:T(8,128)}), f32[256,8,256]{2,1,0:T(8,128)S(1)}, u32[]{:S(2)}, u32[]{:S(2)}) %all-to-all-start) | async-done | bytes 2097184 | tf_op jit(solution)/shard_map/all_to_all | solution.py:625
  46.9 18.0 %all_to_all.30 = f32[128,2,128]{2,1,0:T(2,128)S(1)} all-to-all(f32[128,2,128]{2,1,0:T(2,128)S(1)} %copy.22), channel_id=1, replica_groups=mesh['cells'=128] {'cells'}, dimensions={0} | all-to-all | bytes 262144 | tf_op jit(solution)/shard_map/all_to_all | solution.py:625
  64.9 8.1 %all-to-all-start.2 = ((f32[256,8,256]{2,1,0:T(8,128)}), f32[256,8,256]{2,1,0:T(8,128)}, u32[]{:S(2)}, u32[]{:S(2)}) async-start(f32[256,8,256]{2,1,0:T(8,128)} %copy-done.2), calls=%async_computation.2 | async-start | bytes 4194304 | tf_op jit(solution)/shard_map/all_to_all | solution.py:625
  73.1 1.1 copy-done.19
  74.3 1.2 copy-done.25
  75.5 19.9 %near_early.1.before_ref = f32[33,32,256]{2,1,0:T(8,128)S(1)} custom-call(s32[4,128]{1,0:T(4,128)S(1)} %pad_add_fusion.info_ref, f32[3,128]{1,0:T(4,128)S(1)} %add_convert_fusion.shift_ref, bf16[32,48,256]{2,1,0:T(8,128)(2,1)S(1)} %copy-done.19, f32[256,8,256]{2,1,0:T(8,128)S(1)} %all-to-all-done.far_ref.far_a_ref, f32[33,32,256]{2,1,0:T(8,128)S(1)} %copy-done.25), custom_call_target="tpu_custom_call" | custom-call | flops 2500000000 | bytes 100000 | tf_op jit(solution)/shard_map/near_early/pallas_call | solution.py:699
  95.4 1.0 copy-done.16
  96.5 16.3 %deposit.1 = f32[2048,128]{1,0:T(8,128)} custom-call(f32[128,128]{1,0:T(8,128)S(1)} %bitcast.30, f32[128,128]{1,0:T(8,128)S(1)} %bitcast.29, f32[256,512]{1,0:T(8,128)S(1)} %copy-done.13, f32[512,512]{1,0:T(8,128)S(1)} %copy-done.12), custom_call_target="tpu_custom_call" | custom-call | flops 2500000000 | bytes 100000 | tf_op jit(solution)/shard_map/deposit/pallas_call | solution.py:711
  112.8 4.2 %all-to-all-start.3 = ((f32[128,16,128]{2,1,0:T(8,128)}), f32[128,16,128]{2,1,0:T(8,128)S(1)}, u32[]{:S(2)}, u32[]{:S(2)}) async-start(f32[128,16,128]{2,1,0:T(8,128)} %bitcast.6), calls=%async_computation.3 | async-start | bytes 2097152 | tf_op jit(solution)/shard_map/all_to_all | solution.py:625
  117.1 27.2 %near_late.1 = (f32[33,32,256]{2,1,0:T(8,128)S(1)}, f32[32,256]{1,0:T(8,128)S(1)}, f32[32,256]{1,0:T(8,128)S(1)}, f32[128,8,256]{2,1,0:T(8,128)}) custom-call(s32[1]{0:T(128)} %bitcast.me_ref, s32[26,8]{1,0:T(8,128)S(1)} %bitcast.33, s32[32]{0:T(128)S(1)} %copy-done.11, s32[4,128]{1,0:T(4,128)S(1)} %pad_add_fusion.info_ref, ...), custom_call_target="tpu_custom_call" | custom-call | flops 2500000000 | bytes 100000 | tf_op jit(solution)/shard_map/near_late/pallas_call | solution.py:722
  144.3 1.0 copy-done.14
  145.3 10.3 %all-to-all-start.4 = ((f32[128,8,256]{2,1,0:T(8,128)}), f32[128,8,256]{2,1,0:T(8,128)}, u32[]{:S(2)}, u32[]{:S(2)}) async-start(f32[128,8,256]{2,1,0:T(8,128)} %get-tuple-element.42), calls=%async_computation.4 | async-start | bytes 2097152 | tf_op jit(solution)/shard_map/all_to_all | solution.py:625
  155.6 5.5 %far_self.1.before_ref = f32[33,16,256]{2,1,0:T(8,128)S(1)} custom-call(f32[32,8,256]{2,1,0:T(8,128)S(1)} %get-tuple-element.25.own_ref, f32[32,256]{1,0:T(8,128)S(1)} %get-tuple-element.43.factor_ref, bf16[32,48,256]{2,1,0:T(8,128)(2,1)S(1)} %copy-done.22), custom_call_target="tpu_custom_call" | custom-call | flops 1333333376 | bytes 100000 | tf_op jit(solution)/shard_map/far_self/pallas_call | solution.py:734
  161.9 6.6 %filter.1 = f32[2048,128]{1,0:T(8,128)} custom-call(s32[1]{0:T(128)} %bitcast.8.first_ref, f32[2048,128]{1,0:T(8,128)S(1)} %bitcast.26, f32[512,512]{1,0:T(8,128)S(1)} %copy-done.5, f32[512,512]{1,0:T(8,128)S(1)} %copy-done.6), custom_call_target="tpu_custom_call" | custom-call | flops 833333312 | bytes 100000 | tf_op jit(solution)/shard_map/filter/pallas_call | solution.py:757
  168.5 6.0 %all-to-all-done.4 = f32[128,8,256]{2,1,0:T(8,128)} async-done(((f32[128,8,256]{2,1,0:T(8,128)}), f32[128,8,256]{2,1,0:T(8,128)}, u32[]{:S(2)}, u32[]{:S(2)}) %all-to-all-start.4) | async-done | bytes 1048608 | tf_op jit(solution)/shard_map/all_to_all | solution.py:625
  174.6 4.3 %all-to-all-start.5 = ((f32[128,16,128]{2,1,0:T(8,128)}), f32[128,16,128]{2,1,0:T(8,128)S(1)}, u32[]{:S(2)}, u32[]{:S(2)}) async-start(f32[128,16,128]{2,1,0:T(8,128)} %bitcast.10), calls=%async_computation.5 | async-start | bytes 2097152 | tf_op jit(solution)/shard_map/all_to_all | solution.py:625
  179.5 1.2 copy-done.15
  180.8 1.1 copy-done.23
  181.9 1.0 copy-done.27
  182.9 28.3 %far_cross.1 = f32[4,32,256]{2,1,0:T(8,128)S(1)} custom-call(s32[32]{0:T(128)S(1)} %copy-done.11, s32[4,128]{1,0:T(4,128)S(1)} %pad_add_fusion.info_ref, f32[3,128]{1,0:T(4,128)S(1)} %add_convert_fusion.shift_ref, bf16[32,48,256]{2,1,0:T(8,128)(2,1)S(1)} %copy-done.23, f32[32,8,256]{2,1,0:T(8,128)S(1)} %get-tuple-element.25.own_ref, ...), custom_call_target="tpu_custom_call" | custom-call | flops 5000000000 | bytes 100000 | tf_op jit(solution)/shard_map/far_cross/pallas_call | solution.py:744
  212.6 1.2 copy-done.4
  213.8 1.0 copy-done.7
  214.9 6.0 %potential.1 = f32[2,256,256]{2,1,0:T(8,128)} custom-call(f32[2048,128]{1,0:T(8,128)S(1)} %bitcast.25, f32[512,512]{1,0:T(8,128)S(1)} %copy-done.4, f32[512,256]{1,0:T(8,128)S(1)} %copy-done.7), custom_call_target="tpu_custom_call" | custom-call | flops 666666688 | bytes 100000 | tf_op jit(solution)/shard_map/potential/pallas_call | solution.py:767
  (74 shorter events, 8.4 us)
Async XLA Ops:
  7.5 1.4 copy-start.2
  8.8 1.3 copy-start.3
  10.2 9.2 %copy-start.28 = (s32[8192,1]{0,1:T(1,128)S(1)}, s32[8192,1]{0,1:T(1,128)}, u32[]{:S(2)}) copy-start(s32[8192,1]{0,1:T(1,128)} %param.24) | copy-start | bytes 98308
  10.2 10.0 %copy-start.29 = (s32[8192]{0:T(1024)S(1)}, s32[8192]{0:T(1024)}, u32[]{:S(2)}) copy-start(s32[8192]{0:T(1024)} %param.25) | copy-start | bytes 98308
  10.2 36.6 %all-to-all-start = ((f32[256,8,256]{2,1,0:T(8,128)}), f32[256,8,256]{2,1,0:T(8,128)S(1)}, u32[]{:S(2)}, u32[]{:S(2)}) async-start(f32[256,8,256]{2,1,0:T(8,128)} %copy-done.3), calls=%async_computation | async-start | bytes 4194304 | tf_op jit(solution)/shard_map/all_to_all | solution.py:625
  37.7 1.0 copy-start.24
  38.7 26.3 %copy-start.21 = (bf16[32,48,256]{2,1,0:T(8,128)(2,1)}, bf16[32,48,256]{2,1,0:T(8,128)(2,1)S(1)}, u32[]{:S(2)}) copy-start(bf16[32,48,256]{2,1,0:T(8,128)(2,1)S(1)} %get-tuple-element.39.table_ref) | copy-start | bytes 2359300
  46.8 26.3 %copy-start = (f32[256,8,256]{2,1,0:T(8,128)}, f32[256,8,256]{2,1,0:T(8,128)S(1)}, u32[]{:S(2)}) copy-start(f32[256,8,256]{2,1,0:T(8,128)S(1)} %all-to-all-done.far_ref.far_a_ref) | copy-start | bytes 6291460
  64.9 8.1 %copy-start.31 = (s32[4,128]{1,0:T(4,128)S(1)}, s32[4,128]{1,0:T(4,128)}, u32[]{:S(2)}) copy-start(s32[4,128]{1,0:T(4,128)} %param.22) | copy-start | bytes 6148
  64.9 47.9 %all-to-all-start.2 = ((f32[256,8,256]{2,1,0:T(8,128)}), f32[256,8,256]{2,1,0:T(8,128)}, u32[]{:S(2)}, u32[]{:S(2)}) async-start(f32[256,8,256]{2,1,0:T(8,128)} %copy-done.2), calls=%async_computation.2 | async-start | bytes 4194304 | tf_op jit(solution)/shard_map/all_to_all | solution.py:625
  73.1 1.1 copy-start.19
  74.2 1.2 copy-start.25
  75.5 21.0 %copy-start.12 = (f32[512,512]{1,0:T(8,128)S(1)}, f32[512,512]{1,0:T(8,128)}, u32[]{:S(2)}) copy-start(f32[512,512]{1,0:T(8,128)} %constant.110.clone.y_ref) | copy-start | bytes 3145732
  75.5 21.0 %copy-start.13 = (f32[256,512]{1,0:T(8,128)S(1)}, f32[256,512]{1,0:T(8,128)}, u32[]{:S(2)}) copy-start(f32[256,512]{1,0:T(8,128)} %constant.109.clone.z_ref) | copy-start | bytes 1572868
  95.4 1.0 copy-start.16
  112.8 4.2 %copy-start.30 = (f32[8192]{0:T(1024)S(1)}, f32[8192]{0:T(1024)}, u32[]{:S(2)}) copy-start(f32[8192]{0:T(1024)} %param.20) | copy-start | bytes 98308
  112.8 4.3 %copy-start.11 = (s32[32]{0:T(128)S(1)}, s32[32]{0:T(128)}, u32[]{:S(2)}) copy-start(s32[32]{0:T(128)} %count_ref.5) | copy-start | bytes 388
  112.8 4.3 %copy-start.17 = (f32[33,32,256]{2,1,0:T(8,128)S(1)}, f32[33,32,256]{2,1,0:T(8,128)}, u32[]{:S(2)}) copy-start(f32[33,32,256]{2,1,0:T(8,128)} %copy-done.16) | copy-start | bytes 3244036
  112.8 4.3 %copy-start.20 = (bf16[32,48,256]{2,1,0:T(8,128)(2,1)S(1)}, bf16[32,48,256]{2,1,0:T(8,128)(2,1)}, u32[]{:S(2)}) copy-start(bf16[32,48,256]{2,1,0:T(8,128)(2,1)} %copy-done.18) | copy-start | bytes 2359300
  112.8 32.5 %all-to-all-start.3 = ((f32[128,16,128]{2,1,0:T(8,128)}), f32[128,16,128]{2,1,0:T(8,128)S(1)}, u32[]{:S(2)}, u32[]{:S(2)}) async-start(f32[128,16,128]{2,1,0:T(8,128)} %bitcast.6), calls=%async_computation.3 | async-start | bytes 2097152 | tf_op jit(solution)/shard_map/all_to_all | solution.py:625
  144.3 1.0 copy-start.14
  145.3 10.3 %copy-start.22 = (bf16[32,48,256]{2,1,0:T(8,128)(2,1)S(1)}, bf16[32,48,256]{2,1,0:T(8,128)(2,1)}, u32[]{:S(2)}) copy-start(bf16[32,48,256]{2,1,0:T(8,128)(2,1)} %copy-done.21) | copy-start | bytes 2359300
  145.3 29.3 %all-to-all-start.4 = ((f32[128,8,256]{2,1,0:T(8,128)}), f32[128,8,256]{2,1,0:T(8,128)}, u32[]{:S(2)}, u32[]{:S(2)}) async-start(f32[128,8,256]{2,1,0:T(8,128)} %get-tuple-element.42), calls=%async_computation.4 | async-start | bytes 2097152 | tf_op jit(solution)/shard_map/all_to_all | solution.py:625
  155.6 6.3 %copy-start.5 = (f32[512,512]{1,0:T(8,128)S(1)}, f32[512,512]{1,0:T(8,128)}, u32[]{:S(2)}) copy-start(f32[512,512]{1,0:T(8,128)} %constant.111.clone.forward_ref) | copy-start | bytes 3145732
  155.6 6.3 %copy-start.6 = (f32[512,512]{1,0:T(8,128)S(1)}, f32[512,512]{1,0:T(8,128)}, u32[]{:S(2)}) copy-start(f32[512,512]{1,0:T(8,128)} %constant.112.clone.back_ref) | copy-start | bytes 3145732
  168.5 11.0 %copy-start.1 = (f32[256,8,256]{2,1,0:T(8,128)S(1)}, f32[256,8,256]{2,1,0:T(8,128)}, u32[]{:S(2)}) copy-start(f32[256,8,256]{2,1,0:T(8,128)} %copy-done) | copy-start | bytes 6291460
  174.6 38.1 %all-to-all-start.5 = ((f32[128,16,128]{2,1,0:T(8,128)}), f32[128,16,128]{2,1,0:T(8,128)S(1)}, u32[]{:S(2)}, u32[]{:S(2)}) async-start(f32[128,16,128]{2,1,0:T(8,128)} %bitcast.10), calls=%async_computation.5 | async-start | bytes 2097152 | tf_op jit(solution)/shard_map/all_to_all | solution.py:625
  179.5 1.2 copy-start.15
  180.8 1.1 copy-start.23
  181.9 1.0 copy-start.27
  212.6 1.2 copy-start.4
  213.8 1.0 copy-start.7
  (5 other events, 4.3 us)

commit v5 on v4

--- a/solution.py
+++ b/solution.py
@@ -516,6 +516,17 @@
     return lax.dot_general(left, right, NN, precision=highest, preferred_element_type=F32)
 
 
+def dot_halves(left, right):
+    left_high, left_low = split(left)
+    right_high, right_low = split(right)
+    return lax.dot_general(
+        jnp.concatenate([left_high, left_high, left_low], axis=1),
+        jnp.concatenate([right_high, right_low, right_high], axis=0),
+        NN,
+        preferred_element_type=F32,
+    )
+
+
 def deposit_kernel(mass_ref, cell_ref, z_ref, y_ref, out_ref, grid_ref):
     lanes = 128
     planes = grid_ref.shape[0]
@@ -580,9 +591,9 @@
 def potential_kernel(in_ref, y_ref, z_ref, out_ref):
     for plane in range(2):
         pieces = [get_line(in_ref, plane * 4 + part) for part in range(4)]
-        turned = dot32(y_ref[...], jnp.concatenate(pieces, axis=0))
-        out_ref[plane] = dot32(turned[0:M], z_ref[0:M, :]) + dot32(
-            turned[M : 2 * M], z_ref[M : 2 * M, :]
+        turned = dot_halves(y_ref[...], jnp.concatenate(pieces, axis=0))
+        out_ref[plane] = dot_halves(
+            jnp.concatenate([turned[0:M], turned[M : 2 * M]], axis=1), z_ref[...]
         )
 
 

time: 222 us -> 219 us (0.986)
    pallas_call x1, Pallas kernels: 5.99 us -> 3.44 us  [per_device(): pl.pallas_call(potential_kernel, out_shape=jax.ShapeDtypeStruct((2, M, M)...]
  transfers between devices with their start and end apart: 5 -> 5, of which waited for: 2 -> 2; matrix products, arithmetic and copies ran while one was open for 2% -> 2% of each run, Pallas kernels for 54% -> 55%
where the time goes in v5:
time: 219 us; the launch traced here: 218 us
  Pallas kernels  126 us (58%)
  starting transfers between devices  35.6 us (16%)
  local copies, waits for them, and re-layouts  23.1 us (11%)
  blocking collectives  18 us (8%)
  waiting for transfers between devices  14.1 us (6%)
    all_to_all x5, starting transfers between devices, swap(): lax.all_to_all(data, 'cells', 0, 0, axis_index_groups=groups, tiled=True)  35.6 us
    pallas_call x1, Pallas kernels, per_device(): pl.pallas_call(far_cross_kernel, out_shape=jax.ShapeDtypeStruct((4, CELLS...  28.2 us
    pallas_call x1, Pallas kernels, per_device(): pl.pallas_call(near_late_kernel, out_shape=[near_sums, each, each, jax.Sh...  27.2 us
    unnamed x70, local copies, waits for them, and re-layouts  20.8 us
    pallas_call x1, Pallas kernels, per_device(): pl.pallas_call(near_early_kernel, out_shape=near_sums, in_specs=[SMEM] *...  19.9 us
    all_to_all x1, blocking collectives, swap(): lax.all_to_all(data, 'cells', 0, 0, axis_index_groups=groups, tiled=True)  18 us
    pallas_call x1, Pallas kernels, per_device(): pl.pallas_call(deposit_kernel, out_shape=wide, in_specs=[VMEM] * 4, out_s...  16.3 us
    all_to_all x5, waiting for transfers between devices, swap(): lax.all_to_all(data, 'cells', 0, 0, axis_index_groups=groups, tiled=True)  14.1 us
  transfers between devices with their start and end apart: 5, of which 2 were waited for; matrix products, arithmetic and copies ran while one was open for 2% of the time, Pallas kernels for 55%

profile of v5, /device:TPU:1, one launch (start us, length us, event | category | flops | bytes accessed | tf_op | source)
XLA Modules:
  0.0 218.2 jit_solution(10340719158492409609)
XLA Ops:
  3.9 0.9 copy-done.9
  5.4 2.0 exports.1
  7.5 1.4 copy-done.2
  8.8 1.3 copy-done.3
  10.2 8.7 %all-to-all-start = ((f32[256,8,256]{2,1,0:T(8,128)}), f32[256,8,256]{2,1,0:T(8,128)S(1)}, u32[]{:S(2)}, u32[]{:S(2)}) async-start(f32[256,8,256]{2,1,0:T(8,128)} %copy-done.3), calls=%async_computation | async-start | bytes 4194304 | tf_op jit(solution)/shard_map/all_to_all | solution.py:636
  20.2 7.0 %sort_masses.1 = (f32[128,128]{1,0:T(8,128)S(1)}, f32[128,128]{1,0:T(8,128)S(1)}) custom-call(s32[32,256]{1,0:T(8,128)S(1)} %reshape.53.owner_ref, s32[32,256]{1,0:T(8,128)S(1)} %reshape.54.cell_ref, f32[32,256]{1,0:T(8,128)S(1)} %get-tuple-element.32.mass_ref), custom_call_target="tpu_custom_call" | custom-call | flops 1000000000 | bytes 100000 | tf_op jit(solution)/shard_map/sort_masses/pallas_call | solution.py:680
  27.2 9.5 %near_self.1 = (bf16[32,48,256]{2,1,0:T(8,128)(2,1)S(1)}, bf16[32,48,256]{2,1,0:T(8,128)(2,1)S(1)}, f32[33,32,256]{2,1,0:T(8,128)S(1)}) custom-call(f32[32,8,256]{2,1,0:T(8,128)S(1)} %get-tuple-element.25.own_ref), custom_call_target="tpu_custom_call" | custom-call | flops 1333333376 | bytes 100000 | tf_op jit(solution)/shard_map/near_self/pallas_call | solution.py:696
  36.7 0.9 copy-done.18
  37.7 1.0 copy-done.24
  38.7 8.1 %all-to-all-done.far_ref.far_a_ref = f32[256,8,256]{2,1,0:T(8,128)S(1)} async-done(((f32[256,8,256]{2,1,0:T(8,128)}), f32[256,8,256]{2,1,0:T(8,128)S(1)}, u32[]{:S(2)}, u32[]{:S(2)}) %all-to-all-start) | async-done | bytes 2097184 | tf_op jit(solution)/shard_map/all_to_all | solution.py:636
  46.9 18.0 %all_to_all.30 = f32[128,2,128]{2,1,0:T(2,128)S(1)} all-to-all(f32[128,2,128]{2,1,0:T(2,128)S(1)} %copy.22), channel_id=1, replica_groups=mesh['cells'=128] {'cells'}, dimensions={0} | all-to-all | bytes 262144 | tf_op jit(solution)/shard_map/all_to_all | solution.py:636
  64.9 8.1 %all-to-all-start.2 = ((f32[256,8,256]{2,1,0:T(8,128)}), f32[256,8,256]{2,1,0:T(8,128)}, u32[]{:S(2)}, u32[]{:S(2)}) async-start(f32[256,8,256]{2,1,0:T(8,128)} %copy-done.2), calls=%async_computation.2 | async-start | bytes 4194304 | tf_op jit(solution)/shard_map/all_to_all | solution.py:636
  73.1 1.1 copy-done.19
  74.3 1.2 copy-done.25
  75.5 19.9 %near_early.1.before_ref = f32[33,32,256]{2,1,0:T(8,128)S(1)} custom-call(s32[4,128]{1,0:T(4,128)S(1)} %pad_add_fusion.info_ref, f32[3,128]{1,0:T(4,128)S(1)} %add_convert_fusion.shift_ref, bf16[32,48,256]{2,1,0:T(8,128)(2,1)S(1)} %copy-done.19, f32[256,8,256]{2,1,0:T(8,128)S(1)} %all-to-all-done.far_ref.far_a_ref, f32[33,32,256]{2,1,0:T(8,128)S(1)} %copy-done.25), custom_call_target="tpu_custom_call" | custom-call | flops 2500000000 | bytes 100000 | tf_op jit(solution)/shard_map/near_early/pallas_call | solution.py:710
  95.4 1.0 copy-done.16
  96.5 16.3 %deposit.1 = f32[2048,128]{1,0:T(8,128)} custom-call(f32[128,128]{1,0:T(8,128)S(1)} %bitcast.30, f32[128,128]{1,0:T(8,128)S(1)} %bitcast.29, f32[256,512]{1,0:T(8,128)S(1)} %copy-done.13, f32[512,512]{1,0:T(8,128)S(1)} %copy-done.12), custom_call_target="tpu_custom_call" | custom-call | flops 2500000000 | bytes 100000 | tf_op jit(solution)/shard_map/deposit/pallas_call | solution.py:722
  112.8 4.2 %all-to-all-start.3 = ((f32[128,16,128]{2,1,0:T(8,128)}), f32[128,16,128]{2,1,0:T(8,128)S(1)}, u32[]{:S(2)}, u32[]{:S(2)}) async-start(f32[128,16,128]{2,1,0:T(8,128)} %bitcast.6), calls=%async_computation.3 | async-start | bytes 2097152 | tf_op jit(solution)/shard_map/all_to_all | solution.py:636
  117.1 27.2 %near_late.1 = (f32[33,32,256]{2,1,0:T(8,128)S(1)}, f32[32,256]{1,0:T(8,128)S(1)}, f32[32,256]{1,0:T(8,128)S(1)}, f32[128,8,256]{2,1,0:T(8,128)}) custom-call(s32[1]{0:T(128)} %bitcast.me_ref, s32[26,8]{1,0:T(8,128)S(1)} %bitcast.33, s32[32]{0:T(128)S(1)} %copy-done.11, s32[4,128]{1,0:T(4,128)S(1)} %pad_add_fusion.info_ref, ...), custom_call_target="tpu_custom_call" | custom-call | flops 2500000000 | bytes 100000 | tf_op jit(solution)/shard_map/near_late/pallas_call | solution.py:733
  144.3 1.0 copy-done.14
  145.3 10.3 %all-to-all-start.4 = ((f32[128,8,256]{2,1,0:T(8,128)}), f32[128,8,256]{2,1,0:T(8,128)}, u32[]{:S(2)}, u32[]{:S(2)}) async-start(f32[128,8,256]{2,1,0:T(8,128)} %get-tuple-element.42), calls=%async_computation.4 | async-start | bytes 2097152 | tf_op jit(solution)/shard_map/all_to_all | solution.py:636
  155.6 5.5 %far_self.1.before_ref = f32[33,16,256]{2,1,0:T(8,128)S(1)} custom-call(f32[32,8,256]{2,1,0:T(8,128)S(1)} %get-tuple-element.25.own_ref, f32[32,256]{1,0:T(8,128)S(1)} %get-tuple-element.43.factor_ref, bf16[32,48,256]{2,1,0:T(8,128)(2,1)S(1)} %copy-done.22), custom_call_target="tpu_custom_call" | custom-call | flops 1333333376 | bytes 100000 | tf_op jit(solution)/shard_map/far_self/pallas_call | solution.py:745
  161.9 6.6 %filter.1 = f32[2048,128]{1,0:T(8,128)} custom-call(s32[1]{0:T(128)} %bitcast.8.first_ref, f32[2048,128]{1,0:T(8,128)S(1)} %bitcast.26, f32[512,512]{1,0:T(8,128)S(1)} %copy-done.5, f32[512,512]{1,0:T(8,128)S(1)} %copy-done.6), custom_call_target="tpu_custom_call" | custom-call | flops 833333312 | bytes 100000 | tf_op jit(solution)/shard_map/filter/pallas_call | solution.py:768
  168.5 6.0 %all-to-all-done.4 = f32[128,8,256]{2,1,0:T(8,128)} async-done(((f32[128,8,256]{2,1,0:T(8,128)}), f32[128,8,256]{2,1,0:T(8,128)}, u32[]{:S(2)}, u32[]{:S(2)}) %all-to-all-start.4) | async-done | bytes 1048608 | tf_op jit(solution)/shard_map/all_to_all | solution.py:636
  174.6 4.3 %all-to-all-start.5 = ((f32[128,16,128]{2,1,0:T(8,128)}), f32[128,16,128]{2,1,0:T(8,128)S(1)}, u32[]{:S(2)}, u32[]{:S(2)}) async-start(f32[128,16,128]{2,1,0:T(8,128)} %bitcast.10), calls=%async_computation.5 | async-start | bytes 2097152 | tf_op jit(solution)/shard_map/all_to_all | solution.py:636
  179.5 1.2 copy-done.15
  180.8 1.1 copy-done.23
  181.9 1.0 copy-done.27
  182.9 28.2 %far_cross.1 = f32[4,32,256]{2,1,0:T(8,128)S(1)} custom-call(s32[32]{0:T(128)S(1)} %copy-done.11, s32[4,128]{1,0:T(4,128)S(1)} %pad_add_fusion.info_ref, f32[3,128]{1,0:T(4,128)S(1)} %add_convert_fusion.shift_ref, bf16[32,48,256]{2,1,0:T(8,128)(2,1)S(1)} %copy-done.23, f32[32,8,256]{2,1,0:T(8,128)S(1)} %get-tuple-element.25.own_ref, ...), custom_call_target="tpu_custom_call" | custom-call | flops 5000000000 | bytes 100000 | tf_op jit(solution)/shard_map/far_cross/pallas_call | solution.py:755
  212.5 1.2 copy-done.4
  213.8 1.0 copy-done.7
  214.8 3.4 %potential.1 = f32[2,256,256]{2,1,0:T(8,128)} custom-call(f32[2048,128]{1,0:T(8,128)S(1)} %bitcast.25, f32[512,512]{1,0:T(8,128)S(1)} %copy-done.4, f32[512,256]{1,0:T(8,128)S(1)} %copy-done.7), custom_call_target="tpu_custom_call" | custom-call | flops 666666688 | bytes 100000 | tf_op jit(solution)/shard_map/potential/pallas_call | solution.py:778
  (74 shorter events, 8.4 us)
Async XLA Ops:
  7.5 1.4 copy-start.2
  8.8 1.3 copy-start.3
  10.2 9.2 %copy-start.28 = (s32[8192,1]{0,1:T(1,128)S(1)}, s32[8192,1]{0,1:T(1,128)}, u32[]{:S(2)}) copy-start(s32[8192,1]{0,1:T(1,128)} %param.24) | copy-start | bytes 98308
  10.2 10.0 %copy-start.29 = (s32[8192]{0:T(1024)S(1)}, s32[8192]{0:T(1024)}, u32[]{:S(2)}) copy-start(s32[8192]{0:T(1024)} %param.25) | copy-start | bytes 98308
  10.2 36.6 %all-to-all-start = ((f32[256,8,256]{2,1,0:T(8,128)}), f32[256,8,256]{2,1,0:T(8,128)S(1)}, u32[]{:S(2)}, u32[]{:S(2)}) async-start(f32[256,8,256]{2,1,0:T(8,128)} %copy-done.3), calls=%async_computation | async-start | bytes 4194304 | tf_op jit(solution)/shard_map/all_to_all | solution.py:636
  37.7 1.0 copy-start.24
  38.7 26.3 %copy-start.21 = (bf16[32,48,256]{2,1,0:T(8,128)(2,1)}, bf16[32,48,256]{2,1,0:T(8,128)(2,1)S(1)}, u32[]{:S(2)}) copy-start(bf16[32,48,256]{2,1,0:T(8,128)(2,1)S(1)} %get-tuple-element.39.table_ref) | copy-start | bytes 2359300
  46.8 26.3 %copy-start = (f32[256,8,256]{2,1,0:T(8,128)}, f32[256,8,256]{2,1,0:T(8,128)S(1)}, u32[]{:S(2)}) copy-start(f32[256,8,256]{2,1,0:T(8,128)S(1)} %all-to-all-done.far_ref.far_a_ref) | copy-start | bytes 6291460
  64.9 8.1 %copy-start.31 = (s32[4,128]{1,0:T(4,128)S(1)}, s32[4,128]{1,0:T(4,128)}, u32[]{:S(2)}) copy-start(s32[4,128]{1,0:T(4,128)} %param.22) | copy-start | bytes 6148
  64.9 47.9 %all-to-all-start.2 = ((f32[256,8,256]{2,1,0:T(8,128)}), f32[256,8,256]{2,1,0:T(8,128)}, u32[]{:S(2)}, u32[]{:S(2)}) async-start(f32[256,8,256]{2,1,0:T(8,128)} %copy-done.2), calls=%async_computation.2 | async-start | bytes 4194304 | tf_op jit(solution)/shard_map/all_to_all | solution.py:636
  73.1 1.1 copy-start.19
  74.2 1.2 copy-start.25
  75.5 21.0 %copy-start.12 = (f32[512,512]{1,0:T(8,128)S(1)}, f32[512,512]{1,0:T(8,128)}, u32[]{:S(2)}) copy-start(f32[512,512]{1,0:T(8,128)} %constant.110.clone.y_ref) | copy-start | bytes 3145732
  75.5 21.0 %copy-start.13 = (f32[256,512]{1,0:T(8,128)S(1)}, f32[256,512]{1,0:T(8,128)}, u32[]{:S(2)}) copy-start(f32[256,512]{1,0:T(8,128)} %constant.109.clone.z_ref) | copy-start | bytes 1572868
  95.4 1.0 copy-start.16
  112.8 4.2 %copy-start.30 = (f32[8192]{0:T(1024)S(1)}, f32[8192]{0:T(1024)}, u32[]{:S(2)}) copy-start(f32[8192]{0:T(1024)} %param.20) | copy-start | bytes 98308
  112.8 4.3 %copy-start.11 = (s32[32]{0:T(128)S(1)}, s32[32]{0:T(128)}, u32[]{:S(2)}) copy-start(s32[32]{0:T(128)} %count_ref.5) | copy-start | bytes 388
  112.8 4.3 %copy-start.17 = (f32[33,32,256]{2,1,0:T(8,128)S(1)}, f32[33,32,256]{2,1,0:T(8,128)}, u32[]{:S(2)}) copy-start(f32[33,32,256]{2,1,0:T(8,128)} %copy-done.16) | copy-start | bytes 3244036
  112.8 4.3 %copy-start.20 = (bf16[32,48,256]{2,1,0:T(8,128)(2,1)S(1)}, bf16[32,48,256]{2,1,0:T(8,128)(2,1)}, u32[]{:S(2)}) copy-start(bf16[32,48,256]{2,1,0:T(8,128)(2,1)} %copy-done.18) | copy-start | bytes 2359300
  112.8 32.5 %all-to-all-start.3 = ((f32[128,16,128]{2,1,0:T(8,128)}), f32[128,16,128]{2,1,0:T(8,128)S(1)}, u32[]{:S(2)}, u32[]{:S(2)}) async-start(f32[128,16,128]{2,1,0:T(8,128)} %bitcast.6), calls=%async_computation.3 | async-start | bytes 2097152 | tf_op jit(solution)/shard_map/all_to_all | solution.py:636
  144.3 1.0 copy-start.14
  145.3 10.3 %copy-start.22 = (bf16[32,48,256]{2,1,0:T(8,128)(2,1)S(1)}, bf16[32,48,256]{2,1,0:T(8,128)(2,1)}, u32[]{:S(2)}) copy-start(bf16[32,48,256]{2,1,0:T(8,128)(2,1)} %copy-done.21) | copy-start | bytes 2359300
  145.3 29.3 %all-to-all-start.4 = ((f32[128,8,256]{2,1,0:T(8,128)}), f32[128,8,256]{2,1,0:T(8,128)}, u32[]{:S(2)}, u32[]{:S(2)}) async-start(f32[128,8,256]{2,1,0:T(8,128)} %get-tuple-element.42), calls=%async_computation.4 | async-start | bytes 2097152 | tf_op jit(solution)/shard_map/all_to_all | solution.py:636
  155.6 6.3 %copy-start.5 = (f32[512,512]{1,0:T(8,128)S(1)}, f32[512,512]{1,0:T(8,128)}, u32[]{:S(2)}) copy-start(f32[512,512]{1,0:T(8,128)} %constant.111.clone.forward_ref) | copy-start | bytes 3145732
  155.6 6.3 %copy-start.6 = (f32[512,512]{1,0:T(8,128)S(1)}, f32[512,512]{1,0:T(8,128)}, u32[]{:S(2)}) copy-start(f32[512,512]{1,0:T(8,128)} %constant.112.clone.back_ref) | copy-start | bytes 3145732
  168.5 11.0 %copy-start.1 = (f32[256,8,256]{2,1,0:T(8,128)S(1)}, f32[256,8,256]{2,1,0:T(8,128)}, u32[]{:S(2)}) copy-start(f32[256,8,256]{2,1,0:T(8,128)} %copy-done) | copy-start | bytes 6291460
  174.6 38.0 %all-to-all-start.5 = ((f32[128,16,128]{2,1,0:T(8,128)}), f32[128,16,128]{2,1,0:T(8,128)S(1)}, u32[]{:S(2)}, u32[]{:S(2)}) async-start(f32[128,16,128]{2,1,0:T(8,128)} %bitcast.10), calls=%async_computation.5 | async-start | bytes 2097152 | tf_op jit(solution)/shard_map/all_to_all | solution.py:636
  179.5 1.2 copy-start.15
  180.8 1.1 copy-start.23
  181.9 1.0 copy-start.27
  212.5 1.2 copy-start.4
  213.8 1.0 copy-start.7
  (5 other events, 4.3 us)
